TPU v7x, 32 devices: a whole 2x2x4 slice. The times are simulated.
32 devices in a mesh: lat: 2 (over x), dp: 8 (over z, core), exp: 2 (over y).
Axes of the slice: x: 2, y: 2, z: 4, core: 2. Of those that a mesh axis runs over, the one named last changes fastest.
Arguments:
- images: bfloat16 [16, 32, 256, 192], P(('dp', 'exp'), 'lat'), may hold values from -6 to 6
- cotangent: bfloat16 [16, 32, 256, 192], P(('dp', 'exp'), 'lat'), may hold values from -0.15625 to 0.15625
- labels: int32 [16, 32, 2, 1], P(('dp', 'exp'), 'lat'), may hold values from 0 to 15; in each aligned block of 32 rows (0 to 31, 32 to 63, ..., all dimensions but the last counted through in order) at most 3 rows name the same one
- dw_kernel: float32 [7, 7, 192], replicated, may hold values from -0.875 to 0.875
- ln_gain: float32 [192], replicated, may hold values from 0.5 to 2
- w_expand: bfloat16 [192, 768], replicated, may hold values from -0.4375 to 0.4375
- w_reduce: bfloat16 [768, 192], replicated, may hold values from -0.21875 to 0.21875
- exp_in: bfloat16 [16, 192, 768], P('exp'), may hold values from -0.4375 to 0.4375
- exp_out: bfloat16 [16, 768, 192], P('exp'), may hold values from -0.21875 to 0.21875
Outputs:
- output: bfloat16 [16, 32, 256, 192], P(('dp', 'exp'), 'lat')
- grad_in: float32 [16, 192, 768], P('exp')
- grad_out: float32 [16, 768, 192], P('exp')
Inputs may be any that keep to these rules, and one draw needn't show every extreme that they name: `labels`: among the 32 row blocks of one device (aligned runs of 32 blocks in the order clip, row, block), no class is named more than 3 times, a bound that some block reaches.
All inputs are finite; a program needn't handle non-finite values.
Results may differ from a plain program's by a relative error of at most 0.0072.
Values may be sent and summed in bfloat16 or wider, within the bound.
No kernel may reach another device: no remote copies, remote signals or barrier semaphores. Data moves between devices by JAX's collectives and lax.ppermute only.
A program may use at most 128 MiB of HBM per device.

v0:
```python
import functools
import jax
import jax.numpy as jnp
import numpy as np
from jax import lax
from jax.experimental import pallas as pl
from jax.experimental.pallas import tpu as pltpu
from jax.sharding import PartitionSpec as P

EXPERTS = 16
BLOCK = 128
CAP = 3
SEG = 8
TILE = 4
SIZES = (4, 4)
BF = jnp.bfloat16
F32 = jnp.float32
VMEM_LIMIT = 56 << 20
ANY = pl.BlockSpec(memory_space=pl.ANY)
VM = pl.BlockSpec(memory_space=pltpu.VMEM)
SM = pl.BlockSpec(memory_space=pltpu.SMEM)


def params(**more):
    return pltpu.CompilerParams(vmem_limit_bytes=VMEM_LIMIT, **more)


def cost(flops):
    return pl.CostEstimate(flops=flops, transcendentals=0, bytes_accessed=1 << 20)


def dot(a, b, dims=((1,), (0,))):
    return lax.dot_general(a, b, (dims, ((), ())), preferred_element_type=F32)


def dense_kernel(place, table, counts, images, halo, dw, gain, w1, w2, spread, gather, sums, *refs):
    dense, slots, (wide, smooth, taps, gains, w1s) = refs[0], refs[1:-5], refs[-5:]
    rows, channels, width = images.shape
    steps = width // SEG
    rest = channels - 128
    step = pl.program_id(0)
    first = step * TILE

    @pl.when(step == 0)
    def _():
        for i in range(7):
            row = dw[i]
            low, high = row[:, :128], row[:, 128:]
            for n, pair in ((0, [low, high, high]), (49, [low, low])):
                joined = jnp.concatenate(pair, axis=1)
                for j in range(7):
                    one = jnp.broadcast_to(joined[j : j + 1], (SEG, 256))
                    taps[n + 7 * i + j] = one.astype(BF)
        zero = jnp.zeros((1, rest), F32)
        low, high = gain[:, :128], gain[:, 128:]
        gains[0] = jnp.concatenate([low, high, zero], axis=1)
        gains[1] = jnp.concatenate([low, zero, high], axis=1)
        zero = jnp.zeros((rest, w1.shape[1]), BF)
        w1s[0, :128] = w1[:128]
        w1s[0, 128 : 128 + rest] = w1[128:]
        w1s[0, 128 + rest :] = zero
        w1s[1, :128] = w1[:128]
        w1s[1, 128 : 256 - rest] = zero
        w1s[1, 256 - rest :] = w1[128:]

    def picture_row(q):
        g = first - 3 + q
        inside = jnp.logical_and(g >= 0, g < rows)
        row = images[jnp.clip(g, 0, rows - 1)]
        wanted = jnp.where(place[3] == 0, g >= rows, g < 0)
        other = halo[jnp.clip(jnp.where(g < 0, g + 3, g - rows), 0, 2)]
        other = jnp.where(wanted, other, jnp.zeros_like(other))
        return jnp.where(inside, row, other)

    picture = [picture_row(q) for q in range(TILE + 6)]
    tall = []
    for q in range(TILE + 6):
        partner = picture[min(q + 2, TILE + 5)]
        joined = jnp.concatenate([picture[q], partner[128:]], axis=0)
        tall.append(dot(spread[...], joined, ((1,), (1,))))
    for q in range(TILE + 4):
        wide[q] = tall[q].astype(BF).reshape(steps + 6, SEG, 256)
    for q in range(7):
        joined = jnp.concatenate([tall[q + 2][:, :128], tall[q + 3][:, :128]], axis=1)
        wide[TILE + 4 + q] = joined.astype(BF).reshape(steps + 6, SEG, 256)

    part = 8
    parts = steps // part

    def conv(n, carry):
        unit, start = n // parts, n % parts * part
        row = jnp.where(unit == 2, TILE + 4, unit)
        kind = jnp.where(unit == 2, 49, 0)
        total = jnp.zeros((part, SEG, 256), F32)
        for i in range(7):
            source = wide[row + i, pl.ds(start, part + 6)]
            terms = [source[j : j + part] * taps[kind + 7 * i + j][None] for j in range(7)]
            low = (terms[0] + terms[1]) + (terms[2] + terms[3])
            high = (terms[4] + terms[5]) + terms[6]
            total = total + (low + high).astype(F32)
        smooth[unit, pl.ds(start, part)] = total.astype(BF)
        return carry

    lax.fori_loop(0, 3 * parts, conv, 0)

    units = [smooth[u].reshape(width, 256) for u in range(3)]
    both = [
        units[0],
        units[1],
        jnp.concatenate([units[2][:, :128], units[0][:, 128:]], axis=1),
        jnp.concatenate([units[2][:, 128:], units[1][:, 128:]], axis=1),
    ]
    every = range(TILE)
    values = [dot(gather[...], both[h]) for h in every]
    mean = [dot(values[h].astype(BF), sums[h // 2]) * (1.0 / channels) for h in every]
    c0 = [values[h][:, :128] - mean[h] for h in every]
    c1 = [values[h][:, 128:] - mean[h] for h in every]
    squares = [
        jnp.concatenate([(c0[h] * c0[h]).astype(BF), (c1[h] * c1[h]).astype(BF)], axis=1)
        for h in every
    ]
    scale = [
        lax.rsqrt(dot(squares[h], sums[h // 2]) * (1.0 / channels) + 1e-6) for h in every
    ]
    normed = [
        jnp.concatenate(
            [
                (c0[h] * scale[h] * gains[h // 2][:, :128]).astype(BF),
                (c1[h] * scale[h] * gains[h // 2][:, 128:]).astype(BF),
            ],
            axis=1,
        )
        for h in every
    ]
    active = []
    for h in every:
        expanded = dot(normed[h], w1s[h // 2])
        halved = 0.5 * expanded
        active.append((halved + halved * lax.erf(expanded * 0.7071067811865476)).astype(BF))
    for h in every:
        result = images[first + h].astype(F32) + dot(w2[...], active[h], ((1,), (1,)))
        dense[first + h] = result.astype(BF)

    @pl.when(step == pl.num_programs(0) - 1)
    def _():
        copy_slots(place, table, dense, slots)


def dense_constants(width, channels):
    steps = width // SEG
    spread = np.zeros((steps + 6, SEG, width), np.float32)
    gather = np.zeros((width, steps, SEG), np.float32)
    for s in range(SEG):
        for t in range(steps + 6):
            if 0 <= s * steps + t - 3 < width:
                spread[t, s, s * steps + t - 3] = 1
        for t in range(steps):
            gather[s * steps + t, t, s] = 1
    rest = channels - 128
    sums = np.zeros((2, 256, 128), np.float32)
    sums[:, :128] = 1
    sums[0, 128 : 128 + rest] = 1
    sums[1, 256 - rest :] = 1
    return (
        jnp.asarray(spread.reshape(-1, width), BF),
        jnp.asarray(gather.reshape(width, width), BF),
        jnp.asarray(sums, BF),
    )


def slot_shapes(channels):
    return [jax.ShapeDtypeStruct((CAP * size, channels, BLOCK), BF) for size in SIZES]


def dense_part(images, halo, dw_kernel, ln_gain, w_expand, w_reduce, place, table, counts):
    rows, channels, width = images.shape
    steps = width // SEG
    hidden = w_expand.shape[1]
    args = [images, halo, dw_kernel, ln_gain[None], w_expand, w_reduce]
    args += dense_constants(width, channels)
    slots = slot_shapes(channels)
    return pl.pallas_call(
        dense_kernel,
        grid=(rows // TILE,),
        in_specs=[SM] * 3 + [VM] * len(args),
        out_specs=[VM] * (1 + len(slots)),
        out_shape=[jax.ShapeDtypeStruct(images.shape, BF)] + slots,
        scratch_shapes=[
            pltpu.VMEM((TILE + 11, steps + 6, SEG, 256), BF),
            pltpu.VMEM((3, steps, SEG, 256), BF),
            pltpu.VMEM((98, SEG, 256), BF),
            pltpu.VMEM((2, 1, 256), F32),
            pltpu.VMEM((2, 256, hidden), BF),
        ],
        compiler_params=params(),
        cost_estimate=cost(64 << 30),
        name="dense_block",
    )(place, table, counts, *args)


def at_block(ref, b):
    return ref.at[b // 2, :, pl.ds(pl.multiple_of(b % 2 * BLOCK, BLOCK), BLOCK)]


def block_of(ref, b):
    return ref[b // 2, :, pl.ds(pl.multiple_of(b % 2 * BLOCK, BLOCK), BLOCK)]


def copy_slots(place, table, blocks, slots):
    n = CAP * place[1]
    for slot in slots:
        for k in range(slot.shape[0]):
            slot[k] = block_of(blocks, table[n + k])
        n = n + slot.shape[0]


def route_kernel(labels, place, blocks, *refs):
    table, counts, slots = refs[0], refs[1], refs[2:]
    for e in range(EXPERTS):
        counts[e] = 0
        for k in range(CAP):
            table[CAP * e + k] = 0

    def step(b, carry):
        e = labels[b]
        k = counts[e]
        table[CAP * e + k] = b
        counts[e] = k + 1
        return carry

    lax.fori_loop(0, labels.shape[0], step, 0)
    copy_slots(place, table, blocks, slots)


def route(blocks, labels, place):
    slots = slot_shapes(blocks.shape[1])
    return pl.pallas_call(
        route_kernel,
        in_specs=[SM, SM, VM],
        out_specs=[SM, SM] + [VM] * len(slots),
        out_shape=[
            jax.ShapeDtypeStruct((CAP * EXPERTS,), jnp.int32),
            jax.ShapeDtypeStruct((EXPERTS,), jnp.int32),
        ]
        + slots,
        compiler_params=params(),
        name="route_blocks",
    )(labels, place, blocks)


def expert_kernel(
    offset, tables, tallies, theirs, place, dense_in, cots, xs, gs, w_in, w_out,
    dense, back, keep, send, xbuf, gbuf, obuf, acc, w_in_t, w_out_t, sems,
):
    base = place[0] + offset
    group = w_in.shape[0]
    core, lat = place[2], place[3]
    counts = [tallies[base + k] for k in range(group)]
    counts2 = [theirs[base + k] for k in range(group)]
    table = [tables[CAP * base + n] for n in range(CAP * group)]

    def spot_of(k, j):
        return pl.ds(pl.multiple_of((counts[k] + j) * BLOCK, BLOCK), BLOCK)

    def own_copies(k, j):
        b, here = table[CAP * k + j], pl.ds(j * BLOCK, BLOCK)
        return (
            pltpu.make_async_copy(at_block(dense_in, b), xbuf.at[k, :, here], sems.at[0, k, j]),
            pltpu.make_async_copy(at_block(cots, b), gbuf.at[k, :, here], sems.at[1, k, j]),
        )

    def far_copies(k, j):
        here = spot_of(k, j)
        return (
            pltpu.make_async_copy(xs.at[CAP * k + j], xbuf.at[k, :, here], sems.at[2, k, j]),
            pltpu.make_async_copy(gs.at[CAP * k + j], gbuf.at[k, :, here], sems.at[3, k, j]),
        )

    def own_back(k, j):
        here = pl.ds(j * BLOCK, BLOCK)
        there = at_block(dense, table[CAP * k + j])
        return (pltpu.make_async_copy(xbuf.at[k, :, here], there, sems.at[0, k, j]),)

    def far_back(k, j):
        here = spot_of(k, j)
        return (pltpu.make_async_copy(obuf.at[k, :, here], back.at[CAP * k + j], sems.at[2, k, j]),)

    def each(k, tally, copies, action):
        for j in range(CAP):
            @pl.when(j < tally[k])
            def _():
                for copy in copies(k, j):
                    action(copy)

    def start(copy):
        copy.start()

    def wait(copy):
        copy.wait()

    for k in range(group):
        each(k, counts, own_copies, start)
        each(k, counts2, far_copies, start)
        total = counts[k] + counts2[k]
        for j in range(2 * CAP):
            @pl.when(jnp.logical_and(j >= total, jnp.logical_or(j < 4, total > 4)))
            def _():
                here = pl.ds(j * BLOCK, BLOCK)
                zero = jnp.zeros((xbuf.shape[1], BLOCK), BF)
                xbuf[k, :, here] = zero
                gbuf[k, :, here] = zero

    for k in range(group):
        w_in_t[...] = w_in[k].T
        w_out_t[...] = w_out[k].T
        each(k, counts, own_copies, wait)
        each(k, counts2, far_copies, wait)

        def tokens(first, many):
            here = pl.ds(first * BLOCK, many * BLOCK)
            x, g = xbuf[k, :, here], gbuf[k, :, here]
            pre = dot(w_in_t[...], x)
            share = 0.5 + 0.5 * lax.erf(pre * 0.7071067811865476)
            hidden = (pre * share).astype(BF)
            slope = share + pre * (jnp.exp(pre * pre * -0.5) * 0.3989422804014327)
            scaled = (dot(w_out_t[...], g) * slope).astype(BF)
            obuf[k, :, here] = dot(w_out[k], hidden).astype(BF)
            return dot(x, scaled, ((1,), (1,))), dot(g, hidden, ((1,), (1,)))

        acc[0], acc[1] = tokens(0, 4)

        @pl.when(counts[k] + counts2[k] > 4)
        def _():
            more = tokens(4, 2)
            acc[0] += more[0]
            acc[1] += more[1]

        spot = (k + lat * (group // 2)) % group
        grad_in, grad_out = acc[0].astype(BF), acc[1].astype(BF)
        first = core == 0
        keep[spot] = jnp.where(first, grad_in, grad_out)
        send[spot] = jnp.where(first, grad_out, grad_in)
        each(k, counts2, far_back, start)
        for j in range(CAP):
            here = pl.ds(j * BLOCK, BLOCK)

            @pl.when(j < counts[k])
            def _():
                both = xbuf[k, :, here].astype(F32) + obuf[k, :, here].astype(F32)
                xbuf[k, :, here] = both.astype(BF)

        each(k, counts, own_back, start)

    for k in range(group):
        each(k, counts2, far_back, wait)
        each(k, counts, own_back, wait)


def expert_part(offset, size, table, counts, theirs, place, dense, cots, xs, gs, exp_in, exp_out):
    channels, hidden = exp_in.shape[1:]
    tokens = 2 * CAP * BLOCK
    group = size
    weights = pl.BlockSpec((group, channels, hidden), lambda i: (offset // size, 0, 0))
    return pl.pallas_call(
        functools.partial(expert_kernel, offset),
        grid=(1,),
        in_specs=[SM, SM, SM, SM, ANY, ANY, ANY, ANY, weights, weights],
        out_specs=[ANY, ANY, VM, VM],
        out_shape=[
            jax.ShapeDtypeStruct(dense.shape, BF),
            jax.ShapeDtypeStruct(xs.shape, BF),
            jax.ShapeDtypeStruct((group, channels, hidden), BF),
            jax.ShapeDtypeStruct((group, channels, hidden), BF),
        ],
        input_output_aliases={4: 0},
        scratch_shapes=[
            pltpu.VMEM((group, channels, tokens), BF),
            pltpu.VMEM((group, channels, tokens), BF),
            pltpu.VMEM((group, channels, tokens), BF),
            pltpu.VMEM((2, channels, hidden), F32),
            pltpu.VMEM((hidden, channels), BF),
            pltpu.VMEM((hidden, channels), BF),
            pltpu.SemaphoreType.DMA((4, group, CAP)),
        ],
        compiler_params=params(),
        cost_estimate=cost(64 << 30),
        name="expert_group",
    )(table, counts, theirs, place, dense, cots, xs, gs, exp_in, exp_out)


def combine_kernel(experts, tables, tallies, place, dense_in, *refs):
    backs, (dense, xbuf, obuf, sems) = refs[:-4], refs[-4:]
    counts = [tallies[place[1] + e] for e in range(experts)]
    table = [tables[CAP * place[1] + n] for n in range(CAP * experts)]

    def each(body):
        for slot in range(CAP * experts):
            @pl.when(slot % CAP < counts[slot // CAP])
            def _():
                body(slot)

    places = [back.at[k] for back in backs for k in range(back.shape[0])]

    def fetches(slot):
        back = places[slot]
        return (
            pltpu.make_async_copy(at_block(dense_in, table[slot]), xbuf.at[slot], sems.at[0, slot]),
            pltpu.make_async_copy(back, obuf.at[slot], sems.at[1, slot]),
        )

    def store(slot):
        return pltpu.make_async_copy(xbuf.at[slot], at_block(dense, table[slot]), sems.at[0, slot])

    def begin(slot):
        for copy in fetches(slot):
            copy.start()

    def work(slot):
        for copy in fetches(slot):
            copy.wait()
        xbuf[slot] = (xbuf[slot].astype(F32) + obuf[slot].astype(F32)).astype(BF)
        store(slot).start()

    each(begin)
    each(work)
    each(lambda slot: store(slot).wait())


def combine(dense, backs, table, counts, place, experts):
    slots = CAP * experts
    channels = dense.shape[1]
    return pl.pallas_call(
        functools.partial(combine_kernel, experts),
        in_specs=[SM] * 3 + [ANY] * (1 + len(backs)),
        out_specs=ANY,
        out_shape=jax.ShapeDtypeStruct(dense.shape, BF),
        input_output_aliases={3: 0},
        scratch_shapes=[
            pltpu.VMEM((slots, channels, BLOCK), BF),
            pltpu.VMEM((slots, channels, BLOCK), BF),
            pltpu.SemaphoreType.DMA((2, slots)),
        ],
        compiler_params=params(),
        cost_estimate=cost(64 << 30),
        name="combine_blocks",
    )(table, counts, place, dense, *backs)


def exchange(value, axis, flip):
    count = lax.axis_size(axis)
    return lax.ppermute(value, axis, [(i, i ^ flip) for i in range(count)])


def shift(value, by):
    count = lax.axis_size("dp")
    copies = count // 2
    perm = [(i, ((i // 2 + by) % copies) * 2 + i % 2) for i in range(count)]
    return lax.ppermute(value, "dp", perm)


def add(*values):
    total = values[0].astype(F32)
    for value in values[1:]:
        total = total + value.astype(F32)
    return total


def reduce_chain(keep, send):
    copies = lax.axis_size("dp") // 2
    place = lax.axis_index("dp") // 2
    half = keep.shape[0] // 2
    (got,) = yield [exchange(send, "dp", 1)]
    (crossed,) = yield [exchange(add(keep[half:], got[half:]).astype(BF), "lat", 1)]
    total = add(keep[:half], got[:half], crossed).astype(BF)
    total = total.reshape(-1, total.shape[-1])
    pieces = total.reshape(copies, -1, total.shape[-1])

    def piece(index):
        return lax.dynamic_index_in_dim(pieces, index, 0, keepdims=False)

    arrived = yield [shift(piece((place + by) % copies), by) for by in range(1, copies)]
    own = add(piece(place), *arrived).astype(BF)
    arrived = yield [shift(own, by) for by in range(1, copies)]
    whole = jnp.stack([own, *arrived])
    rows = whole.shape[1]
    if rows % 16 or keep.shape[1] % rows:
        whole = jnp.take(whole, (place - jnp.arange(copies)) % copies, axis=0)
    other, whole2 = yield [exchange(whole, "lat", 1), exchange(whole, "dp", 1)]
    (other2,) = yield [exchange(other, "dp", 1)]
    return whole, other, whole2, other2


class Rounds:
    def __init__(self):
        self.live, self.results = [], []

    def arrive(self, *others):
        sent = [values for _, values in self.live]
        sent, others = lax.optimization_barrier((sent, others))
        self.live = [(chain, values) for (chain, _), values in zip(self.live, sent)]
        return others

    def send(self):
        going = []
        for chain, values in self.live:
            try:
                going.append((chain, chain.send(values)))
            except StopIteration as stop:
                self.results.append(stop.value)
        self.live = going


def after(value, *needed):
    return lax.optimization_barrier((value, *needed))[0]


def widen_kernel(pieces, place, mine, other, mine2, other2, *refs):
    grad_in, grad_out = refs[-2:]
    core, lat, spot = place[2], place[3], place[4]
    first = core == 0
    half, channels = grad_in.shape[0] // 2, grad_in.shape[1]
    rows = half * channels // pieces
    for side, (a, b) in ((lat, (mine, mine2)), (1 - lat, (other, other2))):
        for s in range(pieces):
            start = ((spot - s + pieces) % pieces) * rows
            expert = side * half + start // channels
            here = pl.ds(pl.multiple_of(start % channels, 16), rows)
            source = pl.ds(s * rows, rows)
            grad_in[expert, here, :] = jnp.where(first, a[source], b[source]).astype(F32)
            grad_out[expert, here, :] = jnp.where(first, b[source], a[source]).astype(F32)


def widen_group(offset, size, place, whole, previous, experts, channels):
    copies, rows, hidden = whole[0].shape
    pieces = size // 2 if rows % 16 or channels % rows else copies
    args = [w.reshape(copies * rows, hidden) for w in whole]
    alias = {}
    specs = [SM] + [VM] * 4
    if previous is not None:
        alias = {5: 0, 6: 1}
        args += list(previous)
        specs += [ANY, ANY]
    block = pl.BlockSpec((size, channels, hidden), lambda i: (offset // size, 0, 0))
    return pl.pallas_call(
        functools.partial(widen_kernel, pieces),
        grid=(1,),
        in_specs=specs,
        out_specs=[block, block],
        out_shape=[jax.ShapeDtypeStruct((experts, channels, hidden), F32)] * 2,
        input_output_aliases=alias,
        compiler_params=params(),
        cost_estimate=cost(64 << 30),
        name="widen_gradients",
    )(place, *args)


def body(images, cotangent, labels, dw_kernel, ln_gain, w_expand, w_reduce, exp_in, exp_out):
    rows, channels = images.shape[1], images.shape[3]
    experts = exp_in.shape[0]
    parts = len(SIZES)
    lat = lax.axis_index("lat")
    side = lax.axis_index("exp")
    dp = lax.axis_index("dp")
    copies = lax.axis_size("dp") // 2
    place = jnp.stack([side * experts, (1 - side) * experts, dp % 2, lat, dp // 2 % copies])
    place = place.astype(jnp.int32)
    picture = jnp.swapaxes(images[0], 1, 2)
    cots = jnp.swapaxes(cotangent[0], 1, 2)
    exp_out = jnp.swapaxes(exp_out, 1, 2)
    edge = lax.dynamic_slice_in_dim(picture, jnp.where(lat == 0, rows - 3, 0), 3, axis=0)
    halo = exchange(edge, "lat", 1)
    table, counts, *cot_out = route(cots, labels.reshape(-1), place)
    theirs = exchange(counts, "exp", 1)
    cot_in = [exchange(c, "exp", 1) for c in cot_out]

    dense, *act_out = dense_part(
        picture, halo, dw_kernel, ln_gain, w_expand, w_reduce.T, place, table, counts
    )
    act_out[0] = after(act_out[0], *cot_in)
    act_in = [exchange(a, "exp", 1) for a in act_out]

    backs, grads, rounds = [], None, Rounds()
    acts = act_in[0]
    offsets = [sum(SIZES[:part]) for part in range(parts)]
    for part in range(parts):
        dense, back, keep, send = expert_part(
            offsets[part], SIZES[part], table, counts, theirs, place, dense, cots, acts,
            cot_in[part], exp_in, exp_out,
        )
        following = act_in[part + 1 : part + 2]
        if part == parts - 1:
            send, *backs = rounds.arrive(send, *backs)
        else:
            send, *following = rounds.arrive(send, *following)
        backs.append(exchange(back, "exp", 1))
        chain = reduce_chain(keep, send)
        arrived, following = lax.optimization_barrier((next(chain), following))
        rounds.live.append((chain, arrived))
        rounds.send()
        if following:
            acts = following[0]
    backs = rounds.arrive(*backs)
    rounds.send()
    output = combine(dense, backs, table, counts, place, experts)
    done = 0
    while rounds.live:
        if done:
            grads = list(rounds.arrive(*grads))
        else:
            (output,) = rounds.arrive(output)
        rounds.send()
        while done < len(rounds.results):
            grads = widen_group(
                offsets[done], SIZES[done], place, rounds.results[done], grads, experts, channels
            )
            done += 1
    output = jnp.swapaxes(output, 1, 2)[None]
    return (output, grads[0], jnp.swapaxes(grads[1], 1, 2))


def solution(mesh):
    in_specs = (
        P(("dp", "exp"), "lat", None, None),
        P(("dp", "exp"), "lat", None, None),
        P(("dp", "exp"), "lat", None, None),
        P(),
        P(),
        P(),
        P(),
        P("exp", None, None),
        P("exp", None, None),
    )
    out_specs = (P(("dp", "exp"), "lat", None, None), P("exp", None, None), P("exp", None, None))
    return jax.shard_map(body, mesh=mesh, in_specs=in_specs, out_specs=out_specs, check_vma=False)
```

profile of v0, /device:TPU:0, one launch (start us, length us, event | category | flops | bytes accessed | tf_op | source)
XLA Modules:
  0.0 185.5 jit_solution(6325732451821458236)
XLA Ops:
  0.6 1.0 dynamic-slice_bitcast_fusion
  1.6 3.0 %collective-permute-start.1 = (bf16[3,192,256]{2,1,0:T(8,128)(2,1)S(1)}, bf16[3,192,256]{2,1,0:T(8,128)(2,1)S(1)}, u32[]{:S(2)}, u32[]{:S(2)}) collective-permute-start(bf16[3,192,256]{2,1,0:T(8,128)(2,1)S(1)} %dynamic-slice_bitcast_fusion), channel_id=1, source_target_pairs={{0,16},{16,0},{1,17},{17,1},{2,18},{18,2},{3,19},{19,3},{4,20},{20... | collective-permute-start | bytes 884744 | tf_op jit(solution)/shard_map/ppermute | solution.py:451
  4.6 0.8 copy.21
  6.7 3.2 %route_blocks.1 = (s32[48]{0:T(128)}, s32[16]{0:T(128)}, bf16[12,192,128]{2,1,0:T(8,128)(2,1)}, bf16[12,192,128]{2,1,0:T(8,128)(2,1)}) custom-call(s32[32]{0:T(128)} %reshape.40.labels, s32[5]{0:T(128)} %stack.53.place, bf16[16,192,256]{2,1,0:T(8,128)(2,1)} %bitcast.66), custom_call_target="tpu_custom_call" | custom-call | tf_op jit(solution)/shard_map/route_blocks/pallas_call | solution.py:237
  9.9 1.6 collective-permute-start.2
  12.0 0.8 copy-done.17
  12.8 21.0 %dense_block.1 = (bf16[16,192,256]{2,1,0:T(8,128)(2,1)}, bf16[12,192,128]{2,1,0:T(8,128)(2,1)}, bf16[12,192,128]{2,1,0:T(8,128)(2,1)}) custom-call(s32[5]{0:T(128)} %stack.53.place, s32[48]{0:T(128)} %get-tuple-element.56.table.tables, s32[16]{0:T(128)} %get-tuple-element.57.counts.tallies, bf16[16,192,256]{2,1,0:T(8,128)(2,1)} %bitcast.79, ...), custom_call_target="tpu_custom_call" | custom-call | flops 68719476736 | bytes 1048576 | tf_op jit(solution)/shard_map/dense_block/pallas_call | solution.py:182
  33.8 3.9 %collective-permute-done.3.gs = bf16[12,192,128]{2,1,0:T(8,128)(2,1)S(1)} collective-permute-done((bf16[12,192,128]{2,1,0:T(8,128)(2,1)}, bf16[12,192,128]{2,1,0:T(8,128)(2,1)S(1)}, u32[]{:S(2)}, u32[]{:S(2)}) %collective-permute-start.3) | collective-permute-done | bytes 589856 | tf_op jit(solution)/shard_map/ppermute | solution.py:451
  37.6 1.5 collective-permute-start.4
  39.7 1.5 collective-permute-start.5
  41.2 13.0 %collective-permute-done.theirs = s32[16]{0:T(128)S(1)} collective-permute-done((s32[16]{0:T(128)S(1)}, s32[16]{0:T(128)S(1)}, u32[]{:S(2)}, u32[]{:S(2)}) %collective-permute-start) | collective-permute-done | bytes 96 | tf_op jit(solution)/shard_map/ppermute | solution.py:451
  55.0 14.2 %expert_group.2 = (bf16[16,192,256]{2,1,0:T(8,128)(2,1)}, bf16[12,192,128]{2,1,0:T(8,128)(2,1)}, bf16[4,192,768]{2,1,0:T(8,128)(2,1)}, bf16[4,192,768]{2,1,0:T(8,128)(2,1)}) custom-call(s32[48]{0:T(128)} %get-tuple-element.56.table.tables, s32[16]{0:T(128)} %get-tuple-element.57.counts.tallies, s32[16]{0:T(128)} %copy-done.19, ...), custom_call_target="tpu_custom_call", output_to_operand_aliasing={{0}: (4, {})} | custom-call | flops 68719476736 | bytes 1048576 | tf_op jit(solution)/shard_map/expert_group/pallas_call | solution.py:364
  69.3 0.7 collective-permute-start.8
  70.0 2.3 %collective-permute-done.6 = bf16[4,192,768]{2,1,0:T(8,128)(2,1)S(1)} collective-permute-done((bf16[4,192,768]{2,1,0:T(8,128)(2,1)}, bf16[4,192,768]{2,1,0:T(8,128)(2,1)S(1)}, u32[]{:S(2)}, u32[]{:S(2)}) %collective-permute-start.6) | collective-permute-done | bytes 1179680 | tf_op jit(solution)/shard_map/ppermute | solution.py:451
  72.3 1.1 copy-done.2
  73.4 1.2 add_convert_fusion.3
  75.0 13.3 %expert_group.3 = (bf16[16,192,256]{2,1,0:T(8,128)(2,1)}, bf16[12,192,128]{2,1,0:T(8,128)(2,1)}, bf16[4,192,768]{2,1,0:T(8,128)(2,1)}, bf16[4,192,768]{2,1,0:T(8,128)(2,1)}) custom-call(s32[48]{0:T(128)} %get-tuple-element.56.table.tables, s32[16]{0:T(128)} %get-tuple-element.57.counts.tallies, s32[16]{0:T(128)} %copy-done.19, ...), custom_call_target="tpu_custom_call", output_to_operand_aliasing={{0}: (4, {})} | custom-call | flops 68719476736 | bytes 1048576 | tf_op jit(solution)/shard_map/expert_group/pallas_call | solution.py:364
  88.3 1.7 collective-permute-done.7
  90.7 2.4 %collective-permute-done.12 = bf16[4,192,768]{2,1,0:T(8,128)(2,1)S(1)} collective-permute-done((bf16[4,192,768]{2,1,0:T(8,128)(2,1)}, bf16[4,192,768]{2,1,0:T(8,128)(2,1)S(1)}, u32[]{:S(2)}, u32[]{:S(2)}) %collective-permute-start.12) | collective-permute-done | bytes 1179680 | tf_op jit(solution)/shard_map/ppermute | solution.py:451
  93.1 1.2 add_convert_fusion.1
  94.7 1.5 add_convert_fusion.2
  96.2 0.8 dynamic-slice_bitcast_fusion.4
  96.9 3.8 %collective-permute-start.11 = (bf16[96,768]{1,0:T(8,128)(2,1)}, bf16[96,768]{1,0:T(8,128)(2,1)}, u32[]{:S(2)}, u32[]{:S(2)}) collective-permute-start(bf16[96,768]{1,0:T(8,128)(2,1)} %get-tuple-element.112), channel_id=1, source_target_pairs={{0,12},{2,14},{4,0},{6,2},{8,4},{10,6},{12,8},{14,10},{1,13},{3,15... | collective-permute-start | bytes 442376 | tf_op jit(solution)/shard_map/ppermute | solution.py:458
  100.7 1.0 collective-permute-start.9
  101.8 4.3 %collective-permute-done.14.refs_1_ = bf16[12,192,128]{2,1,0:T(8,128)(2,1)} collective-permute-done((bf16[12,192,128]{2,1,0:T(8,128)(2,1)}, bf16[12,192,128]{2,1,0:T(8,128)(2,1)}, u32[]{:S(2)}, u32[]{:S(2)}) %collective-permute-start.14) | collective-permute-done | bytes 589856 | tf_op jit(solution)/shard_map/ppermute | solution.py:451
  106.1 7.5 %collective-permute-done.10 = bf16[96,768]{1,0:T(8,128)(2,1)} collective-permute-done((bf16[96,768]{1,0:T(8,128)(2,1)}, bf16[96,768]{1,0:T(8,128)(2,1)}, u32[]{:S(2)}, u32[]{:S(2)}) %collective-permute-start.10) | collective-permute-done | bytes 147488 | tf_op jit(solution)/shard_map/ppermute | solution.py:458
  113.6 1.1 fusion.5
  114.7 1.5 collective-permute-start.17
  116.2 1.4 collective-permute-start.16
  117.6 1.9 %collective-permute-start.15 = (bf16[96,768]{1,0:T(8,128)(2,1)S(1)}, bf16[96,768]{1,0:T(8,128)(2,1)S(1)}, u32[]{:S(2)}, u32[]{:S(2)}) collective-permute-start(bf16[96,768]{1,0:T(8,128)(2,1)S(1)} %fusion.5), channel_id=1, source_target_pairs={{0,4},{2,6},{4,8},{6,10},{8,12},{10,14},{12,0},{14,2},{1,5},{3,7},... | collective-permute-start | bytes 442376 | tf_op jit(solution)/shard_map/ppermute | solution.py:458
  119.6 1.3 add_convert_fusion
  120.9 1.9 %collective-permute-start.20 = (bf16[96,768]{1,0:T(8,128)(2,1)S(1)}, bf16[96,768]{1,0:T(8,128)(2,1)S(1)}, u32[]{:S(2)}, u32[]{:S(2)}) collective-permute-start(bf16[96,768]{1,0:T(8,128)(2,1)S(1)} %get-tuple-element.109), channel_id=1, source_target_pairs={{0,12},{2,14},{4,0},{6,2},{8,4},{10,6},{12,8},{14,10},{1,13},{3,15... | collective-permute-start | bytes 442376 | tf_op jit(solution)/shard_map/ppermute | solution.py:458
  122.8 4.9 %collective-permute-start.18 = (bf16[96,768]{1,0:T(8,128)(2,1)S(1)}, bf16[96,768]{1,0:T(8,128)(2,1)S(1)}, u32[]{:S(2)}, u32[]{:S(2)}) collective-permute-start(bf16[96,768]{1,0:T(8,128)(2,1)S(1)} %get-tuple-element.111), channel_id=1, source_target_pairs={{0,4},{2,6},{4,8},{6,10},{8,12},{10,14},{12,0},{14,2},{1,5},{3,7},... | collective-permute-start | bytes 442376 | tf_op jit(solution)/shard_map/ppermute | solution.py:458
  127.7 3.2 %combine_blocks.1 = bf16[16,192,256]{2,1,0:T(8,128)(2,1)} custom-call(s32[48]{0:T(128)} %get-tuple-element.56.table.tables, s32[16]{0:T(128)} %get-tuple-element.57.counts.tallies, s32[5]{0:T(128)} %stack.53.place, bf16[16,192,256]{2,1,0:T(8,128)(2,1)} %get-tuple-element.82.dense_in, ...), custom_call_target="tpu_custom_call", output_to_operand_aliasing={{}: (3, {})} | custom-call | flops 68719476736 | bytes 1048576 | tf_op jit(solution)/shard_map/combine_blocks/pallas_call | solution.py:432
  130.9 7.2 %collective-permute-done.16 = bf16[96,768]{1,0:T(8,128)(2,1)S(1)} collective-permute-done((bf16[96,768]{1,0:T(8,128)(2,1)S(1)}, bf16[96,768]{1,0:T(8,128)(2,1)S(1)}, u32[]{:S(2)}, u32[]{:S(2)}) %collective-permute-start.16) | collective-permute-done | bytes 147488 | tf_op jit(solution)/shard_map/ppermute | solution.py:458
  138.1 4.8 %collective-permute-done.19 = bf16[96,768]{1,0:T(8,128)(2,1)S(1)} collective-permute-done((bf16[96,768]{1,0:T(8,128)(2,1)S(1)}, bf16[96,768]{1,0:T(8,128)(2,1)S(1)}, u32[]{:S(2)}, u32[]{:S(2)}) %collective-permute-start.19) | collective-permute-done | bytes 147488 | tf_op jit(solution)/shard_map/ppermute | solution.py:458
  143.1 1.6 collective-permute-start.21
  144.8 1.2 collective-permute-start.24
  146.0 1.9 %collective-permute-start.23 = (bf16[96,768]{1,0:T(8,128)(2,1)S(1)}, bf16[96,768]{1,0:T(8,128)(2,1)S(1)}, u32[]{:S(2)}, u32[]{:S(2)}) collective-permute-start(bf16[96,768]{1,0:T(8,128)(2,1)S(1)} %fusion.2), channel_id=1, source_target_pairs={{0,4},{2,6},{4,8},{6,10},{8,12},{10,14},{12,0},{14,2},{1,5},{3,7},... | collective-permute-start | bytes 442376 | tf_op jit(solution)/shard_map/ppermute | solution.py:458
  147.9 3.8 %collective-permute-done.25 = bf16[96,768]{1,0:T(8,128)(2,1)S(1)} collective-permute-done((bf16[96,768]{1,0:T(8,128)(2,1)S(1)}, bf16[96,768]{1,0:T(8,128)(2,1)S(1)}, u32[]{:S(2)}, u32[]{:S(2)}) %collective-permute-start.25) | collective-permute-done | bytes 147488 | tf_op jit(solution)/shard_map/ppermute | solution.py:458
  151.7 7.9 %collective-permute-done.24 = bf16[96,768]{1,0:T(8,128)(2,1)S(1)} collective-permute-done((bf16[96,768]{1,0:T(8,128)(2,1)S(1)}, bf16[96,768]{1,0:T(8,128)(2,1)S(1)}, u32[]{:S(2)}, u32[]{:S(2)}) %collective-permute-start.24) | collective-permute-done | bytes 147488 | tf_op jit(solution)/shard_map/ppermute | solution.py:458
  159.8 0.8 collective-permute-start.27
  160.7 1.0 collective-permute-done.28
  161.8 13.8 %collective-permute-done.27 = bf16[4,96,768]{2,1,0:T(8,128)(2,1)S(1)} collective-permute-done((bf16[4,96,768]{2,1,0:T(8,128)(2,1)S(1)}, bf16[4,96,768]{2,1,0:T(8,128)(2,1)S(1)}, u32[]{:S(2)}, u32[]{:S(2)}) %collective-permute-start.27) | collective-permute-done | bytes 589856 | tf_op jit(solution)/shard_map/ppermute | solution.py:451
  175.6 0.7 copy-done.15
  176.4 4.1 %widen_gradients.2 = (f32[8,192,768]{2,1,0:T(8,128)}, f32[8,192,768]{2,1,0:T(8,128)}) custom-call(s32[5]{0:T(128)} %stack.53.place, bf16[384,768]{1,0:T(8,128)(2,1)} %bitcast.71, bf16[384,768]{1,0:T(8,128)(2,1)} %bitcast.83, bf16[384,768]{1,0:T(8,128)(2,1)} %bitcast.82, bf16[384,768]{1,0:T(8,128)(2,1)} %bitcast.86), custom_call_target="tpu_custom_call" | custom-call | flops 68719476736 | bytes 1048576 | tf_op jit(solution)/shard_map/widen_gradients/pallas_call | solution.py:544
  180.5 0.8 copy-done.16
  181.4 4.1 %widen_gradients.3 = (f32[8,192,768]{2,1,0:T(8,128)}, f32[8,192,768]{2,1,0:T(8,128)}) custom-call(s32[5]{0:T(128)} %stack.53.place, bf16[384,768]{1,0:T(8,128)(2,1)} %bitcast.72, bf16[384,768]{1,0:T(8,128)(2,1)} %bitcast.85, bf16[384,768]{1,0:T(8,128)(2,1)} %bitcast.84, bf16[384,768]{1,0:T(8,128)(2,1)} %bitcast.87, ...), custom_call_target="tpu_custom_call", output_to_operand_aliasing={{0}: (5, {}), {1}: (6, {})} | custom-call | flops 68719476736 | bytes 1048576 | tf_op jit(solution)/shard_map/widen_gradients/pallas_call | solution.py:544
  (73 shorter events, 5.4 us)
Async XLA Ops:
  1.6 10.4 %collective-permute-start.1 = (bf16[3,192,256]{2,1,0:T(8,128)(2,1)S(1)}, bf16[3,192,256]{2,1,0:T(8,128)(2,1)S(1)}, u32[]{:S(2)}, u32[]{:S(2)}) collective-permute-start(bf16[3,192,256]{2,1,0:T(8,128)(2,1)S(1)} %dynamic-slice_bitcast_fusion), channel_id=1, source_target_pairs={{0,16},{16,0},{1,17},{17,1},{2,18},{18,2},{3,19},{19,3},{4,20},{20... | collective-permute-start | bytes 884744 | tf_op jit(solution)/shard_map/ppermute | solution.py:451
  9.9 23.8 %collective-permute-start.2 = (bf16[12,192,128]{2,1,0:T(8,128)(2,1)}, bf16[12,192,128]{2,1,0:T(8,128)(2,1)S(1)}, u32[]{:S(2)}, u32[]{:S(2)}) collective-permute-start(bf16[12,192,128]{2,1,0:T(8,128)(2,1)} %get-tuple-element.60), channel_id=1, source_target_pairs={{0,1},{1,0},{2,3},{3,2},{4,5},{5,4},{6,7},{7,6},{8,9},{9,8},{10,11... | collective-permute-start | bytes 1769480 | tf_op jit(solution)/shard_map/ppermute | solution.py:451
  11.5 26.1 %collective-permute-start.3 = (bf16[12,192,128]{2,1,0:T(8,128)(2,1)}, bf16[12,192,128]{2,1,0:T(8,128)(2,1)S(1)}, u32[]{:S(2)}, u32[]{:S(2)}) collective-permute-start(bf16[12,192,128]{2,1,0:T(8,128)(2,1)} %get-tuple-element.61), channel_id=1, source_target_pairs={{0,1},{1,0},{2,3},{3,2},{4,5},{5,4},{6,7},{7,6},{8,9},{9,8},{10,11... | collective-permute-start | bytes 1769480 | tf_op jit(solution)/shard_map/ppermute | solution.py:451
  12.8 26.4 %copy-start.18 = (s32[16]{0:T(128)S(1)}, s32[16]{0:T(128)}, u32[]{:S(2)}) copy-start(s32[16]{0:T(128)} %get-tuple-element.57.counts.tallies) | copy-start | bytes 196
  33.8 20.4 %copy-start.10 = (bf16[12,192,128]{2,1,0:T(8,128)(2,1)}, bf16[12,192,128]{2,1,0:T(8,128)(2,1)S(1)}, u32[]{:S(2)}) copy-start(bf16[12,192,128]{2,1,0:T(8,128)(2,1)S(1)} %collective-permute-done.2.gs) | copy-start | bytes 1769476
  37.6 31.5 %copy-start.7 = (bf16[12,192,128]{2,1,0:T(8,128)(2,1)}, bf16[12,192,128]{2,1,0:T(8,128)(2,1)S(1)}, u32[]{:S(2)}) copy-start(bf16[12,192,128]{2,1,0:T(8,128)(2,1)S(1)} %collective-permute-done.3.gs) | copy-start | bytes 1769476
  37.6 16.5 %collective-permute-start.4 = (bf16[12,192,128]{2,1,0:T(8,128)(2,1)}, bf16[12,192,128]{2,1,0:T(8,128)(2,1)S(1)}, u32[]{:S(2)}, u32[]{:S(2)}) collective-permute-start(bf16[12,192,128]{2,1,0:T(8,128)(2,1)} %get-tuple-element.62), channel_id=1, source_target_pairs={{0,1},{1,0},{2,3},{3,2},{4,5},{5,4},{6,7},{7,6},{8,9},{9,8},{10,11... | collective-permute-start | bytes 1769480 | tf_op jit(solution)/shard_map/ppermute | solution.py:451
  39.1 15.0 %collective-permute-start = (s32[16]{0:T(128)S(1)}, s32[16]{0:T(128)S(1)}, u32[]{:S(2)}, u32[]{:S(2)}) collective-permute-start(s32[16]{0:T(128)S(1)} %copy-done.18), channel_id=1, source_target_pairs={{0,1},{1,0},{2,3},{3,2},{4,5},{5,4},{6,7},{7,6},{8,9},{9,8},{10,11... | collective-permute-start | bytes 200 | tf_op jit(solution)/shard_map/ppermute | solution.py:451
  39.7 29.5 %collective-permute-start.5 = (bf16[12,192,128]{2,1,0:T(8,128)(2,1)}, bf16[12,192,128]{2,1,0:T(8,128)(2,1)S(1)}, u32[]{:S(2)}, u32[]{:S(2)}) collective-permute-start(bf16[12,192,128]{2,1,0:T(8,128)(2,1)} %get-tuple-element.65), channel_id=1, source_target_pairs={{0,1},{1,0},{2,3},{3,2},{4,5},{5,4},{6,7},{7,6},{8,9},{9,8},{10,11... | collective-permute-start | bytes 1769480 | tf_op jit(solution)/shard_map/ppermute | solution.py:451
  54.2 0.8 copy-start.14
  69.2 5.8 %copy-start.11 = (bf16[12,192,128]{2,1,0:T(8,128)(2,1)}, bf16[12,192,128]{2,1,0:T(8,128)(2,1)S(1)}, u32[]{:S(2)}) copy-start(bf16[12,192,128]{2,1,0:T(8,128)(2,1)S(1)} %collective-permute-done.5.xs) | copy-start | bytes 1769476
  69.2 3.1 %collective-permute-start.6 = (bf16[4,192,768]{2,1,0:T(8,128)(2,1)}, bf16[4,192,768]{2,1,0:T(8,128)(2,1)S(1)}, u32[]{:S(2)}, u32[]{:S(2)}) collective-permute-start(bf16[4,192,768]{2,1,0:T(8,128)(2,1)} %get-tuple-element.66), channel_id=1, source_target_pairs={{0,2},{2,0},{4,6},{6,4},{8,10},{10,8},{12,14},{14,12},{1,3},{3,1},... | collective-permute-start | bytes 3538952 | tf_op jit(solution)/shard_map/ppermute | solution.py:451
  69.3 19.0 %collective-permute-start.8 = (bf16[12,192,128]{2,1,0:T(8,128)(2,1)}, bf16[12,192,128]{2,1,0:T(8,128)(2,1)S(1)}, u32[]{:S(2)}, u32[]{:S(2)}) collective-permute-start(bf16[12,192,128]{2,1,0:T(8,128)(2,1)} %get-tuple-element.72), channel_id=1, source_target_pairs={{0,1},{1,0},{2,3},{3,2},{4,5},{5,4},{6,7},{7,6},{8,9},{9,8},{10,11... | collective-permute-start | bytes 1769480 | tf_op jit(solution)/shard_map/ppermute | solution.py:451
  72.3 1.1 copy-start.2
  74.6 15.4 %collective-permute-start.7 = (bf16[2,192,768]{2,1,0:T(8,128)(2,1)S(1)}, bf16[2,192,768]{2,1,0:T(8,128)(2,1)S(1)}, u32[]{:S(2)}, u32[]{:S(2)}) collective-permute-start(bf16[2,192,768]{2,1,0:T(8,128)(2,1)S(1)} %add_convert_fusion.3), channel_id=1, source_target_pairs={{0,16},{16,0},{1,17},{17,1},{2,18},{18,2},{3,19},{19,3},{4,20},{20... | collective-permute-start | bytes 1769480 | tf_op jit(solution)/shard_map/ppermute | solution.py:451
  88.3 6.4 %copy-start.1 = (bf16[4,192,768]{2,1,0:T(8,128)(2,1)S(1)}, bf16[4,192,768]{2,1,0:T(8,128)(2,1)}, u32[]{:S(2)}) copy-start(bf16[4,192,768]{2,1,0:T(8,128)(2,1)} %get-tuple-element.63) | copy-start | bytes 3538948
  88.3 6.0 %copy-start.6 = (bf16[12,192,128]{2,1,0:T(8,128)(2,1)}, bf16[12,192,128]{2,1,0:T(8,128)(2,1)S(1)}, u32[]{:S(2)}) copy-start(bf16[12,192,128]{2,1,0:T(8,128)(2,1)S(1)} %collective-permute-done.8.refs_0_) | copy-start | bytes 1769476
  90.0 3.1 %copy-start.5 = (bf16[2,192,768]{2,1,0:T(8,128)(2,1)}, bf16[2,192,768]{2,1,0:T(8,128)(2,1)S(1)}, u32[]{:S(2)}) copy-start(bf16[2,192,768]{2,1,0:T(8,128)(2,1)S(1)} %collective-permute-done.7) | copy-start | bytes 1769476
  90.0 3.1 %collective-permute-start.12 = (bf16[4,192,768]{2,1,0:T(8,128)(2,1)}, bf16[4,192,768]{2,1,0:T(8,128)(2,1)S(1)}, u32[]{:S(2)}, u32[]{:S(2)}) collective-permute-start(bf16[4,192,768]{2,1,0:T(8,128)(2,1)} %get-tuple-element.75), channel_id=1, source_target_pairs={{0,2},{2,0},{4,6},{6,4},{8,10},{10,8},{12,14},{14,12},{1,3},{3,1},... | collective-permute-start | bytes 3538952 | tf_op jit(solution)/shard_map/ppermute | solution.py:451
  90.0 16.1 %collective-permute-start.14 = (bf16[12,192,128]{2,1,0:T(8,128)(2,1)}, bf16[12,192,128]{2,1,0:T(8,128)(2,1)}, u32[]{:S(2)}, u32[]{:S(2)}) collective-permute-start(bf16[12,192,128]{2,1,0:T(8,128)(2,1)} %get-tuple-element.77), channel_id=1, source_target_pairs={{0,1},{1,0},{2,3},{3,2},{4,5},{5,4},{6,7},{7,6},{8,9},{9,8},{10,11... | collective-permute-start | bytes 1769480 | tf_op jit(solution)/shard_map/ppermute | solution.py:451
  94.3 19.3 %collective-permute-start.13 = (bf16[2,192,768]{2,1,0:T(8,128)(2,1)S(1)}, bf16[2,192,768]{2,1,0:T(8,128)(2,1)}, u32[]{:S(2)}, u32[]{:S(2)}) collective-permute-start(bf16[2,192,768]{2,1,0:T(8,128)(2,1)S(1)} %add_convert_fusion.1), channel_id=1, source_target_pairs={{0,16},{16,0},{1,17},{17,1},{2,18},{18,2},{3,19},{19,3},{4,20},{20... | collective-permute-start | bytes 1769480 | tf_op jit(solution)/shard_map/ppermute | solution.py:451
  96.2 23.4 %copy-start = (bf16[4,192,768]{2,1,0:T(8,128)(2,1)S(1)}, bf16[4,192,768]{2,1,0:T(8,128)(2,1)}, u32[]{:S(2)}) copy-start(bf16[4,192,768]{2,1,0:T(8,128)(2,1)} %get-tuple-element.74) | copy-start | bytes 3538948
  96.9 9.1 %collective-permute-start.11 = (bf16[96,768]{1,0:T(8,128)(2,1)}, bf16[96,768]{1,0:T(8,128)(2,1)}, u32[]{:S(2)}, u32[]{:S(2)}) collective-permute-start(bf16[96,768]{1,0:T(8,128)(2,1)} %get-tuple-element.112), channel_id=1, source_target_pairs={{0,12},{2,14},{4,0},{6,2},{8,4},{10,6},{12,8},{14,10},{1,13},{3,15... | collective-permute-start | bytes 442376 | tf_op jit(solution)/shard_map/ppermute | solution.py:458
  100.7 12.8 %collective-permute-start.10 = (bf16[96,768]{1,0:T(8,128)(2,1)}, bf16[96,768]{1,0:T(8,128)(2,1)}, u32[]{:S(2)}, u32[]{:S(2)}) collective-permute-start(bf16[96,768]{1,0:T(8,128)(2,1)} %get-tuple-element.113), channel_id=1, source_target_pairs={{0,8},{2,10},{4,12},{6,14},{8,0},{10,2},{12,4},{14,6},{1,9},{3,11}... | collective-permute-start | bytes 442376 | tf_op jit(solution)/shard_map/ppermute | solution.py:458
  100.7 12.8 %collective-permute-start.9 = (bf16[96,768]{1,0:T(8,128)(2,1)}, bf16[96,768]{1,0:T(8,128)(2,1)}, u32[]{:S(2)}, u32[]{:S(2)}) collective-permute-start(bf16[96,768]{1,0:T(8,128)(2,1)} %get-tuple-element.114), channel_id=1, source_target_pairs={{0,4},{2,6},{4,8},{6,10},{8,12},{10,14},{12,0},{14,2},{1,5},{3,7},... | collective-permute-start | bytes 442376 | tf_op jit(solution)/shard_map/ppermute | solution.py:458
  114.7 8.1 %collective-permute-start.17 = (bf16[96,768]{1,0:T(8,128)(2,1)S(1)}, bf16[96,768]{1,0:T(8,128)(2,1)S(1)}, u32[]{:S(2)}, u32[]{:S(2)}) collective-permute-start(bf16[96,768]{1,0:T(8,128)(2,1)S(1)} %fusion.5), channel_id=1, source_target_pairs={{0,12},{2,14},{4,0},{6,2},{8,4},{10,6},{12,8},{14,10},{1,13},{3,15... | collective-permute-start | bytes 442376 | tf_op jit(solution)/shard_map/ppermute | solution.py:458
  116.2 21.9 %collective-permute-start.16 = (bf16[96,768]{1,0:T(8,128)(2,1)S(1)}, bf16[96,768]{1,0:T(8,128)(2,1)S(1)}, u32[]{:S(2)}, u32[]{:S(2)}) collective-permute-start(bf16[96,768]{1,0:T(8,128)(2,1)S(1)} %fusion.5), channel_id=1, source_target_pairs={{0,8},{2,10},{4,12},{6,14},{8,0},{10,2},{12,4},{14,6},{1,9},{3,11}... | collective-permute-start | bytes 442376 | tf_op jit(solution)/shard_map/ppermute | solution.py:458
  117.6 20.5 %collective-permute-start.15 = (bf16[96,768]{1,0:T(8,128)(2,1)S(1)}, bf16[96,768]{1,0:T(8,128)(2,1)S(1)}, u32[]{:S(2)}, u32[]{:S(2)}) collective-permute-start(bf16[96,768]{1,0:T(8,128)(2,1)S(1)} %fusion.5), channel_id=1, source_target_pairs={{0,4},{2,6},{4,8},{6,10},{8,12},{10,14},{12,0},{14,2},{1,5},{3,7},... | collective-permute-start | bytes 442376 | tf_op jit(solution)/shard_map/ppermute | solution.py:458
  120.9 17.2 %collective-permute-start.20 = (bf16[96,768]{1,0:T(8,128)(2,1)S(1)}, bf16[96,768]{1,0:T(8,128)(2,1)S(1)}, u32[]{:S(2)}, u32[]{:S(2)}) collective-permute-start(bf16[96,768]{1,0:T(8,128)(2,1)S(1)} %get-tuple-element.109), channel_id=1, source_target_pairs={{0,12},{2,14},{4,0},{6,2},{8,4},{10,6},{12,8},{14,10},{1,13},{3,15... | collective-permute-start | bytes 442376 | tf_op jit(solution)/shard_map/ppermute | solution.py:458
  122.8 20.1 %collective-permute-start.19 = (bf16[96,768]{1,0:T(8,128)(2,1)S(1)}, bf16[96,768]{1,0:T(8,128)(2,1)S(1)}, u32[]{:S(2)}, u32[]{:S(2)}) collective-permute-start(bf16[96,768]{1,0:T(8,128)(2,1)S(1)} %get-tuple-element.110), channel_id=1, source_target_pairs={{0,8},{2,10},{4,12},{6,14},{8,0},{10,2},{12,4},{14,6},{1,9},{3,11}... | collective-permute-start | bytes 442376 | tf_op jit(solution)/shard_map/ppermute | solution.py:458
  122.8 20.1 %collective-permute-start.18 = (bf16[96,768]{1,0:T(8,128)(2,1)S(1)}, bf16[96,768]{1,0:T(8,128)(2,1)S(1)}, u32[]{:S(2)}, u32[]{:S(2)}) collective-permute-start(bf16[96,768]{1,0:T(8,128)(2,1)S(1)} %get-tuple-element.111), channel_id=1, source_target_pairs={{0,4},{2,6},{4,8},{6,10},{8,12},{10,14},{12,0},{14,2},{1,5},{3,7},... | collective-permute-start | bytes 442376 | tf_op jit(solution)/shard_map/ppermute | solution.py:458
  143.0 32.6 %copy-start.3 = (bf16[4,96,768]{2,1,0:T(8,128)(2,1)}, bf16[4,96,768]{2,1,0:T(8,128)(2,1)S(1)}, u32[]{:S(2)}) copy-start(bf16[4,96,768]{2,1,0:T(8,128)(2,1)S(1)} %pad_maximum_fusion) | copy-start | bytes 1769476
  143.0 16.6 %collective-permute-start.22 = (bf16[4,96,768]{2,1,0:T(8,128)(2,1)S(1)}, bf16[4,96,768]{2,1,0:T(8,128)(2,1)S(1)}, u32[]{:S(2)}, u32[]{:S(2)}) collective-permute-start(bf16[4,96,768]{2,1,0:T(8,128)(2,1)S(1)} %pad_maximum_fusion), channel_id=1, source_target_pairs={{0,2},{2,0},{4,6},{6,4},{8,10},{10,8},{12,14},{14,12},{1,3},{3,1},... | collective-permute-start | bytes 1769480 | tf_op jit(solution)/shard_map/ppermute | solution.py:451
  143.1 16.5 %collective-permute-start.21 = (bf16[4,96,768]{2,1,0:T(8,128)(2,1)S(1)}, bf16[4,96,768]{2,1,0:T(8,128)(2,1)S(1)}, u32[]{:S(2)}, u32[]{:S(2)}) collective-permute-start(bf16[4,96,768]{2,1,0:T(8,128)(2,1)S(1)} %pad_maximum_fusion), channel_id=1, source_target_pairs={{0,16},{16,0},{1,17},{17,1},{2,18},{18,2},{3,19},{19,3},{4,20},{20... | collective-permute-start | bytes 1769480 | tf_op jit(solution)/shard_map/ppermute | solution.py:451
  144.7 7.0 %collective-permute-start.25 = (bf16[96,768]{1,0:T(8,128)(2,1)S(1)}, bf16[96,768]{1,0:T(8,128)(2,1)S(1)}, u32[]{:S(2)}, u32[]{:S(2)}) collective-permute-start(bf16[96,768]{1,0:T(8,128)(2,1)S(1)} %fusion.2), channel_id=1, source_target_pairs={{0,12},{2,14},{4,0},{6,2},{8,4},{10,6},{12,8},{14,10},{1,13},{3,15... | collective-permute-start | bytes 442376 | tf_op jit(solution)/shard_map/ppermute | solution.py:458
  144.8 14.8 %collective-permute-start.24 = (bf16[96,768]{1,0:T(8,128)(2,1)S(1)}, bf16[96,768]{1,0:T(8,128)(2,1)S(1)}, u32[]{:S(2)}, u32[]{:S(2)}) collective-permute-start(bf16[96,768]{1,0:T(8,128)(2,1)S(1)} %fusion.2), channel_id=1, source_target_pairs={{0,8},{2,10},{4,12},{6,14},{8,0},{10,2},{12,4},{14,6},{1,9},{3,11}... | collective-permute-start | bytes 442376 | tf_op jit(solution)/shard_map/ppermute | solution.py:458
  146.0 13.6 %collective-permute-start.23 = (bf16[96,768]{1,0:T(8,128)(2,1)S(1)}, bf16[96,768]{1,0:T(8,128)(2,1)S(1)}, u32[]{:S(2)}, u32[]{:S(2)}) collective-permute-start(bf16[96,768]{1,0:T(8,128)(2,1)S(1)} %fusion.2), channel_id=1, source_target_pairs={{0,4},{2,6},{4,8},{6,10},{8,12},{10,14},{12,0},{14,2},{1,5},{3,7},... | collective-permute-start | bytes 442376 | tf_op jit(solution)/shard_map/ppermute | solution.py:458
  159.6 16.0 %copy-start.8 = (bf16[4,96,768]{2,1,0:T(8,128)(2,1)}, bf16[4,96,768]{2,1,0:T(8,128)(2,1)S(1)}, u32[]{:S(2)}) copy-start(bf16[4,96,768]{2,1,0:T(8,128)(2,1)S(1)} %collective-permute-done.22) | copy-start | bytes 1769476
  159.6 16.0 %copy-start.9 = (bf16[4,96,768]{2,1,0:T(8,128)(2,1)}, bf16[4,96,768]{2,1,0:T(8,128)(2,1)S(1)}, u32[]{:S(2)}) copy-start(bf16[4,96,768]{2,1,0:T(8,128)(2,1)S(1)} %collective-permute-done.21) | copy-start | bytes 1769476
  159.7 20.8 %copy-start.4 = (bf16[4,96,768]{2,1,0:T(8,128)(2,1)}, bf16[4,96,768]{2,1,0:T(8,128)(2,1)S(1)}, u32[]{:S(2)}) copy-start(bf16[4,96,768]{2,1,0:T(8,128)(2,1)S(1)} %pad_maximum_fusion.1) | copy-start | bytes 1769476
  159.7 2.1 %collective-permute-start.28 = (bf16[4,96,768]{2,1,0:T(8,128)(2,1)S(1)}, bf16[4,96,768]{2,1,0:T(8,128)(2,1)S(1)}, u32[]{:S(2)}, u32[]{:S(2)}) collective-permute-start(bf16[4,96,768]{2,1,0:T(8,128)(2,1)S(1)} %pad_maximum_fusion.1), channel_id=1, source_target_pairs={{0,2},{2,0},{4,6},{6,4},{8,10},{10,8},{12,14},{14,12},{1,3},{3,1},... | collective-permute-start | bytes 1769480 | tf_op jit(solution)/shard_map/ppermute | solution.py:451
  159.8 15.7 %collective-permute-start.27 = (bf16[4,96,768]{2,1,0:T(8,128)(2,1)S(1)}, bf16[4,96,768]{2,1,0:T(8,128)(2,1)S(1)}, u32[]{:S(2)}, u32[]{:S(2)}) collective-permute-start(bf16[4,96,768]{2,1,0:T(8,128)(2,1)S(1)} %pad_maximum_fusion.1), channel_id=1, source_target_pairs={{0,16},{16,0},{1,17},{17,1},{2,18},{18,2},{3,19},{19,3},{4,20},{20... | collective-permute-start | bytes 1769480 | tf_op jit(solution)/shard_map/ppermute | solution.py:451
  160.6 15.0 %collective-permute-start.26 = (bf16[4,96,768]{2,1,0:T(8,128)(2,1)S(1)}, bf16[4,96,768]{2,1,0:T(8,128)(2,1)S(1)}, u32[]{:S(2)}, u32[]{:S(2)}) collective-permute-start(bf16[4,96,768]{2,1,0:T(8,128)(2,1)S(1)} %collective-permute-done.21), channel_id=1, source_target_pairs={{0,2},{2,0},{4,6},{6,4},{8,10},{10,8},{12,14},{14,12},{1,3},{3,1},... | collective-permute-start | bytes 1769480 | tf_op jit(solution)/shard_map/ppermute | solution.py:451
  161.8 18.8 %copy-start.12 = (bf16[4,96,768]{2,1,0:T(8,128)(2,1)}, bf16[4,96,768]{2,1,0:T(8,128)(2,1)S(1)}, u32[]{:S(2)}) copy-start(bf16[4,96,768]{2,1,0:T(8,128)(2,1)S(1)} %collective-permute-done.28) | copy-start | bytes 1769476
  175.5 5.0 %copy-start.13 = (bf16[4,96,768]{2,1,0:T(8,128)(2,1)}, bf16[4,96,768]{2,1,0:T(8,128)(2,1)S(1)}, u32[]{:S(2)}) copy-start(bf16[4,96,768]{2,1,0:T(8,128)(2,1)S(1)} %collective-permute-done.27) | copy-start | bytes 1769476
  175.5 0.9 copy-start.15
  175.5 5.0 %collective-permute-start.29 = (bf16[4,96,768]{2,1,0:T(8,128)(2,1)S(1)}, bf16[4,96,768]{2,1,0:T(8,128)(2,1)S(1)}, u32[]{:S(2)}, u32[]{:S(2)}) collective-permute-start(bf16[4,96,768]{2,1,0:T(8,128)(2,1)S(1)} %collective-permute-done.27), channel_id=1, source_target_pairs={{0,2},{2,0},{4,6},{6,4},{8,10},{10,8},{12,14},{14,12},{1,3},{3,1},... | collective-permute-start | bytes 1769480 | tf_op jit(solution)/shard_map/ppermute | solution.py:451
  180.5 0.8 copy-start.16
  (2 other events, 1.3 us)
where the time goes:
time: 186 us
  waiting for transfers between devices  73.6 us (40%)
  Pallas kernels  63.1 us (34%)
  starting transfers between devices  33.3 us (18%)
  local copies, waits for them, and re-layouts  8.08 us (4%)
  other arithmetic  6.49 us (3%)
    ppermute x18, waiting for transfers between devices, exchange(): return lax.ppermute(value, axis, [(i, i ^ flip) for i in range(count)])  42.5 us
    ppermute x12, waiting for transfers between devices, shift(): return lax.ppermute(value, 'dp', perm)  31.1 us
    pallas_call x2, Pallas kernels, expert_part(): pl.pallas_call(functools.partial(expert_kernel, offset), grid=(1,), in_sp...  27.5 us
    pallas_call x1, Pallas kernels, dense_part(): pl.pallas_call(dense_kernel, grid=(rows // TILE,), in_specs=[SM] * 3 + [V...  21 us
    ppermute x12, starting transfers between devices, shift(): return lax.ppermute(value, 'dp', perm)  19.7 us
    ppermute x18, starting transfers between devices, exchange(): return lax.ppermute(value, axis, [(i, i ^ flip) for i in range(count)])  13.6 us
    pallas_call x2, Pallas kernels, widen_group(): pl.pallas_call(functools.partial(widen_kernel, pieces), grid=(1,), in_spe...  8.29 us
    unnamed x41, local copies, waits for them, and re-layouts  5.01 us
  transfers between devices with their start and end apart: 30, of which 13 were waited for; matrix products, arithmetic and copies ran while one was open for 4% of the time, Pallas kernels for 32%

commit v1 on v0

--- a/solution.py
+++ b/solution.py
@@ -12,7 +12,7 @@
 CAP = 3
 SEG = 8
 TILE = 4
-SIZES = (4, 4)
+SIZES = (2, 2, 2, 2)
 BF = jnp.bfloat16
 F32 = jnp.float32
 VMEM_LIMIT = 56 << 20
@@ -84,7 +84,7 @@
         joined = jnp.concatenate([tall[q + 2][:, :128], tall[q + 3][:, :128]], axis=1)
         wide[TILE + 4 + q] = joined.astype(BF).reshape(steps + 6, SEG, 256)
 
-    part = 8
+    part = 16
     parts = steps // part
 
     def conv(n, carry):
@@ -97,21 +97,27 @@
             terms = [source[j : j + part] * taps[kind + 7 * i + j][None] for j in range(7)]
             low = (terms[0] + terms[1]) + (terms[2] + terms[3])
             high = (terms[4] + terms[5]) + terms[6]
-            total = total + (low + high).astype(F32)
-        smooth[unit, pl.ds(start, part)] = total.astype(BF)
+            total = total + low.astype(F32) + high.astype(F32)
+        rounded = total.astype(BF)
+        smooth[unit, pl.ds(start, part)] = rounded
+        smooth[3 + unit, pl.ds(start, part)] = (total - rounded.astype(F32)).astype(BF)
         return carry
 
     lax.fori_loop(0, 3 * parts, conv, 0)
 
-    units = [smooth[u].reshape(width, 256) for u in range(3)]
-    both = [
-        units[0],
-        units[1],
-        jnp.concatenate([units[2][:, :128], units[0][:, 128:]], axis=1),
-        jnp.concatenate([units[2][:, 128:], units[1][:, 128:]], axis=1),
-    ]
+    units = [smooth[u].reshape(width, 256) for u in range(6)]
+
+    def row_of(units):
+        return [
+            units[0],
+            units[1],
+            jnp.concatenate([units[2][:, :128], units[0][:, 128:]], axis=1),
+            jnp.concatenate([units[2][:, 128:], units[1][:, 128:]], axis=1),
+        ]
+
+    both, fine = row_of(units[:3]), row_of(units[3:])
     every = range(TILE)
-    values = [dot(gather[...], both[h]) for h in every]
+    values = [dot(gather[...], both[h]) + dot(gather[...], fine[h]) for h in every]
     mean = [dot(values[h].astype(BF), sums[h // 2]) * (1.0 / channels) for h in every]
     c0 = [values[h][:, :128] - mean[h] for h in every]
     c1 = [values[h][:, 128:] - mean[h] for h in every]
@@ -187,7 +193,7 @@
         out_shape=[jax.ShapeDtypeStruct(images.shape, BF)] + slots,
         scratch_shapes=[
             pltpu.VMEM((TILE + 11, steps + 6, SEG, 256), BF),
-            pltpu.VMEM((3, steps, SEG, 256), BF),
+            pltpu.VMEM((6, steps, SEG, 256), BF),
             pltpu.VMEM((98, SEG, 256), BF),
             pltpu.VMEM((2, 1, 256), F32),
             pltpu.VMEM((2, 256, hidden), BF),
@@ -248,144 +254,128 @@
     )(labels, place, blocks)
 
 
-def expert_kernel(
-    offset, tables, tallies, theirs, place, dense_in, cots, xs, gs, w_in, w_out,
-    dense, back, keep, send, xbuf, gbuf, obuf, acc, w_in_t, w_out_t, sems,
+def expert_tokens(x, g, w_in_t, w_out_t, w_out):
+    pre = dot(w_in_t, x)
+    share = 0.5 + 0.5 * lax.erf(pre * 0.7071067811865476)
+    hidden = (pre * share).astype(BF)
+    slope = share + pre * (jnp.exp(pre * pre * -0.5) * 0.3989422804014327)
+    scaled = (dot(w_out_t, g) * slope).astype(BF)
+    out = dot(w_out, hidden).astype(BF)
+    return out, dot(x, scaled, ((1,), (1,))), dot(g, hidden, ((1,), (1,)))
+
+
+def expert_blocks(count, block, store, grads, w_in, w_out, w_in_t, w_out_t, carried):
+    w_in_t[...] = w_in[...].T
+    w_out_t[...] = w_out[...].T
+
+    def load(j):
+        return [jnp.where(j < count, part, jnp.zeros_like(part)) for part in block(j)]
+
+    both = [load(0), load(1)]
+    x, g = [jnp.concatenate([a, b], axis=1) for a, b in zip(*both)]
+    out, grad_in, grad_out = expert_tokens(x, g, w_in_t[...], w_out_t[...], w_out[...])
+    if carried is not None:
+        grad_in, grad_out = grad_in + carried[0], grad_out + carried[1]
+    grads[0][...] = grad_in
+    grads[1][...] = grad_out
+    for j in range(2):
+        @pl.when(j < count)
+        def _():
+            store(j, x[:, j * BLOCK : (j + 1) * BLOCK], out[:, j * BLOCK : (j + 1) * BLOCK])
+
+    @pl.when(count > 2)
+    def _():
+        x, g = block(2)
+        out, grad_in, grad_out = expert_tokens(x, g, w_in_t[...], w_out_t[...], w_out[...])
+        grads[0][...] += grad_in
+        grads[1][...] += grad_out
+        store(2, x, out)
+
+
+def own_kernel(place, table, counts, dense_in, cots, w_in, w_out, dense, grad_in, grad_out, *scratch):
+    @pl.when(pl.program_id(0) == 0)
+    def _():
+        dense[...] = dense_in[...]
+
+    e = place[0] + pl.program_id(0)
+
+    def block(j):
+        b = table[CAP * e + j]
+        return block_of(dense_in, b), block_of(cots, b)
+
+    def store(j, x, out):
+        b = table[CAP * e + j]
+        here = pl.ds(pl.multiple_of(b % 2 * BLOCK, BLOCK), BLOCK)
+        dense[b // 2, :, here] = (x.astype(F32) + out.astype(F32)).astype(BF)
+
+    grads = (grad_in.at[0], grad_out.at[0])
+    expert_blocks(counts[e], block, store, grads, w_in.at[0], w_out.at[0], *scratch, None)
+
+
+def own_part(place, table, counts, dense, cots, exp_in, exp_out):
+    experts, channels, hidden = exp_in.shape
+    one = pl.BlockSpec((1, channels, hidden), lambda i: (i, 0, 0))
+    return pl.pallas_call(
+        own_kernel,
+        grid=(experts,),
+        in_specs=[SM, SM, SM, VM, VM, one, one],
+        out_specs=[VM, one, one],
+        out_shape=[jax.ShapeDtypeStruct(dense.shape, BF)]
+        + [jax.ShapeDtypeStruct(exp_in.shape, F32)] * 2,
+        scratch_shapes=[pltpu.VMEM((hidden, channels), BF)] * 2,
+        compiler_params=params(),
+        cost_estimate=cost(64 << 30),
+        name="own_blocks",
+    )(place, table, counts, dense, cots, exp_in, exp_out)
+
+
+def far_kernel(
+    offset, place, theirs, xs, gs, w_in, w_out, own_in, own_out,
+    back, keep, send, w_in_t, w_out_t, grad_in, grad_out,
 ):
-    base = place[0] + offset
-    group = w_in.shape[0]
-    core, lat = place[2], place[3]
-    counts = [tallies[base + k] for k in range(group)]
-    counts2 = [theirs[base + k] for k in range(group)]
-    table = [tables[CAP * base + n] for n in range(CAP * group)]
-
-    def spot_of(k, j):
-        return pl.ds(pl.multiple_of((counts[k] + j) * BLOCK, BLOCK), BLOCK)
-
-    def own_copies(k, j):
-        b, here = table[CAP * k + j], pl.ds(j * BLOCK, BLOCK)
-        return (
-            pltpu.make_async_copy(at_block(dense_in, b), xbuf.at[k, :, here], sems.at[0, k, j]),
-            pltpu.make_async_copy(at_block(cots, b), gbuf.at[k, :, here], sems.at[1, k, j]),
-        )
-
-    def far_copies(k, j):
-        here = spot_of(k, j)
-        return (
-            pltpu.make_async_copy(xs.at[CAP * k + j], xbuf.at[k, :, here], sems.at[2, k, j]),
-            pltpu.make_async_copy(gs.at[CAP * k + j], gbuf.at[k, :, here], sems.at[3, k, j]),
-        )
-
-    def own_back(k, j):
-        here = pl.ds(j * BLOCK, BLOCK)
-        there = at_block(dense, table[CAP * k + j])
-        return (pltpu.make_async_copy(xbuf.at[k, :, here], there, sems.at[0, k, j]),)
-
-    def far_back(k, j):
-        here = spot_of(k, j)
-        return (pltpu.make_async_copy(obuf.at[k, :, here], back.at[CAP * k + j], sems.at[2, k, j]),)
-
-    def each(k, tally, copies, action):
-        for j in range(CAP):
-            @pl.when(j < tally[k])
-            def _():
-                for copy in copies(k, j):
-                    action(copy)
-
-    def start(copy):
-        copy.start()
-
-    def wait(copy):
-        copy.wait()
-
-    for k in range(group):
-        each(k, counts, own_copies, start)
-        each(k, counts2, far_copies, start)
-        total = counts[k] + counts2[k]
-        for j in range(2 * CAP):
-            @pl.when(jnp.logical_and(j >= total, jnp.logical_or(j < 4, total > 4)))
-            def _():
-                here = pl.ds(j * BLOCK, BLOCK)
-                zero = jnp.zeros((xbuf.shape[1], BLOCK), BF)
-                xbuf[k, :, here] = zero
-                gbuf[k, :, here] = zero
-
-    for k in range(group):
-        w_in_t[...] = w_in[k].T
-        w_out_t[...] = w_out[k].T
-        each(k, counts, own_copies, wait)
-        each(k, counts2, far_copies, wait)
-
-        def tokens(first, many):
-            here = pl.ds(first * BLOCK, many * BLOCK)
-            x, g = xbuf[k, :, here], gbuf[k, :, here]
-            pre = dot(w_in_t[...], x)
-            share = 0.5 + 0.5 * lax.erf(pre * 0.7071067811865476)
-            hidden = (pre * share).astype(BF)
-            slope = share + pre * (jnp.exp(pre * pre * -0.5) * 0.3989422804014327)
-            scaled = (dot(w_out_t[...], g) * slope).astype(BF)
-            obuf[k, :, here] = dot(w_out[k], hidden).astype(BF)
-            return dot(x, scaled, ((1,), (1,))), dot(g, hidden, ((1,), (1,)))
-
-        acc[0], acc[1] = tokens(0, 4)
-
-        @pl.when(counts[k] + counts2[k] > 4)
-        def _():
-            more = tokens(4, 2)
-            acc[0] += more[0]
-            acc[1] += more[1]
-
-        spot = (k + lat * (group // 2)) % group
-        grad_in, grad_out = acc[0].astype(BF), acc[1].astype(BF)
-        first = core == 0
-        keep[spot] = jnp.where(first, grad_in, grad_out)
-        send[spot] = jnp.where(first, grad_out, grad_in)
-        each(k, counts2, far_back, start)
-        for j in range(CAP):
-            here = pl.ds(j * BLOCK, BLOCK)
-
-            @pl.when(j < counts[k])
-            def _():
-                both = xbuf[k, :, here].astype(F32) + obuf[k, :, here].astype(F32)
-                xbuf[k, :, here] = both.astype(BF)
-
-        each(k, counts, own_back, start)
-
-    for k in range(group):
-        each(k, counts2, far_back, wait)
-        each(k, counts, own_back, wait)
-
-
-def expert_part(offset, size, table, counts, theirs, place, dense, cots, xs, gs, exp_in, exp_out):
+    k = pl.program_id(0)
+
+    def block(j):
+        return xs[CAP * k + j], gs[CAP * k + j]
+
+    def store(j, x, out):
+        back[CAP * k + j] = out
+
+    count = theirs[place[0] + offset + k]
+    expert_blocks(
+        count, block, store, (grad_in, grad_out), w_in.at[0], w_out.at[0], w_in_t, w_out_t,
+        (own_in[0], own_out[0]),
+    )
+    first = place[2] == 0
+    a, b = grad_in[...].astype(BF), grad_out[...].astype(BF)
+    keep[0] = jnp.where(first, a, b)
+    send[0] = jnp.where(first, b, a)
+
+
+def far_part(offset, size, place, theirs, xs, gs, exp_in, exp_out, own_in, own_out):
     channels, hidden = exp_in.shape[1:]
-    tokens = 2 * CAP * BLOCK
-    group = size
-    weights = pl.BlockSpec((group, channels, hidden), lambda i: (offset // size, 0, 0))
+    one = pl.BlockSpec((1, channels, hidden), lambda i, place: (offset + i, 0, 0))
+    half = size // 2
+    turned = pl.BlockSpec((1, channels, hidden), lambda i, place: ((i + place[3] * half) % size, 0, 0))
     return pl.pallas_call(
-        functools.partial(expert_kernel, offset),
-        grid=(1,),
-        in_specs=[SM, SM, SM, SM, ANY, ANY, ANY, ANY, weights, weights],
-        out_specs=[ANY, ANY, VM, VM],
+        functools.partial(far_kernel, offset),
+        grid_spec=pltpu.PrefetchScalarGridSpec(
+            num_scalar_prefetch=1,
+            grid=(size,),
+            in_specs=[SM, VM, VM, one, one, one, one],
+            out_specs=[VM, turned, turned],
+            scratch_shapes=[pltpu.VMEM((hidden, channels), BF)] * 2
+            + [pltpu.VMEM((channels, hidden), F32)] * 2,
+        ),
         out_shape=[
-            jax.ShapeDtypeStruct(dense.shape, BF),
             jax.ShapeDtypeStruct(xs.shape, BF),
-            jax.ShapeDtypeStruct((group, channels, hidden), BF),
-            jax.ShapeDtypeStruct((group, channels, hidden), BF),
-        ],
-        input_output_aliases={4: 0},
-        scratch_shapes=[
-            pltpu.VMEM((group, channels, tokens), BF),
-            pltpu.VMEM((group, channels, tokens), BF),
-            pltpu.VMEM((group, channels, tokens), BF),
-            pltpu.VMEM((2, channels, hidden), F32),
-            pltpu.VMEM((hidden, channels), BF),
-            pltpu.VMEM((hidden, channels), BF),
-            pltpu.SemaphoreType.DMA((4, group, CAP)),
+            jax.ShapeDtypeStruct((size, channels, hidden), BF),
+            jax.ShapeDtypeStruct((size, channels, hidden), BF),
         ],
         compiler_params=params(),
         cost_estimate=cost(64 << 30),
-        name="expert_group",
-    )(table, counts, theirs, place, dense, cots, xs, gs, exp_in, exp_out)
+        name="far_blocks",
+    )(place, theirs, xs, gs, exp_in, exp_out, own_in, own_out)
 
 
 def combine_kernel(experts, tables, tallies, place, dense_in, *refs):
@@ -465,12 +455,24 @@
     return total
 
 
+CORE, LAT = -1, 0
+
+
+def transfer(kind, value):
+    if kind == CORE:
+        return exchange(value, "dp", 1)
+    if kind == LAT:
+        return exchange(value, "lat", 1)
+    return shift(value, kind)
+
+
 def reduce_chain(keep, send):
     copies = lax.axis_size("dp") // 2
     place = lax.axis_index("dp") // 2
     half = keep.shape[0] // 2
-    (got,) = yield [exchange(send, "dp", 1)]
-    (crossed,) = yield [exchange(add(keep[half:], got[half:]).astype(BF), "lat", 1)]
+    ways = range(1, copies)
+    (got,) = yield [(CORE, send)]
+    (crossed,) = yield [(LAT, add(keep[half:], got[half:]).astype(BF))]
     total = add(keep[:half], got[:half], crossed).astype(BF)
     total = total.reshape(-1, total.shape[-1])
     pieces = total.reshape(copies, -1, total.shape[-1])
@@ -478,36 +480,47 @@
     def piece(index):
         return lax.dynamic_index_in_dim(pieces, index, 0, keepdims=False)
 
-    arrived = yield [shift(piece((place + by) % copies), by) for by in range(1, copies)]
+    arrived = yield [(by, piece((place + by) % copies)) for by in ways]
     own = add(piece(place), *arrived).astype(BF)
-    arrived = yield [shift(own, by) for by in range(1, copies)]
+    arrived = yield [(by, own) for by in ways]
     whole = jnp.stack([own, *arrived])
     rows = whole.shape[1]
     if rows % 16 or keep.shape[1] % rows:
         whole = jnp.take(whole, (place - jnp.arange(copies)) % copies, axis=0)
-    other, whole2 = yield [exchange(whole, "lat", 1), exchange(whole, "dp", 1)]
-    (other2,) = yield [exchange(other, "dp", 1)]
+    other, whole2 = yield [(LAT, whole), (CORE, whole)]
+    (other2,) = yield [(CORE, other)]
     return whole, other, whole2, other2
 
 
 class Rounds:
     def __init__(self):
-        self.live, self.results = [], []
+        self.live, self.results, self.sent = [], [], {}
+
+    def start(self, chain):
+        self.live.append((chain, next(chain)))
+
+    def depart(self):
+        ways = {}
+        for _, values in self.live:
+            for kind, value in values:
+                ways.setdefault(kind, []).append(value.reshape(-1, value.shape[-1]))
+        self.sent = {kind: transfer(kind, jnp.concatenate(flat)) for kind, flat in ways.items()}
 
     def arrive(self, *others):
-        sent = [values for _, values in self.live]
-        sent, others = lax.optimization_barrier((sent, others))
-        self.live = [(chain, values) for (chain, _), values in zip(self.live, sent)]
-        return others
-
-    def send(self):
-        going = []
-        for chain, values in self.live:
+        sent, others = lax.optimization_barrier((self.sent, others))
+        live, self.live, used = self.live, [], {}
+        for chain, values in live:
+            got = []
+            for kind, value in values:
+                first = used.get(kind, 0)
+                used[kind] = first + value.size // value.shape[-1]
+                got.append(sent[kind][first : used[kind]].reshape(value.shape))
             try:
-                going.append((chain, chain.send(values)))
+                self.live.append((chain, chain.send(got)))
             except StopIteration as stop:
                 self.results.append(stop.value)
-        self.live = going
+        self.sent = {}
+        return others
 
 
 def after(value, *needed):
@@ -576,31 +589,28 @@
     dense, *act_out = dense_part(
         picture, halo, dw_kernel, ln_gain, w_expand, w_reduce.T, place, table, counts
     )
-    act_out[0] = after(act_out[0], *cot_in)
-    act_in = [exchange(a, "exp", 1) for a in act_out]
-
+    ahead = min(2, parts)
+    act_out = [after(a, *cot_in) for a in act_out[:ahead]] + act_out[ahead:]
+    act_in = [exchange(a, "exp", 1) for a in act_out[:ahead]]
+
+    dense, *own = own_part(place, table, counts, dense, cots, exp_in, exp_out)
+    act_in += [exchange(after(a, *act_in[:ahead], dense), "exp", 1) for a in act_out[ahead:]]
     backs, grads, rounds = [], None, Rounds()
-    acts = act_in[0]
     offsets = [sum(SIZES[:part]) for part in range(parts)]
     for part in range(parts):
-        dense, back, keep, send = expert_part(
-            offsets[part], SIZES[part], table, counts, theirs, place, dense, cots, acts,
-            cot_in[part], exp_in, exp_out,
+        back, keep, send = far_part(
+            offsets[part], SIZES[part], place, theirs, act_in[part], cot_in[part], exp_in, exp_out, *own
         )
-        following = act_in[part + 1 : part + 2]
-        if part == parts - 1:
-            send, *backs = rounds.arrive(send, *backs)
+        if part + 1 < parts:
+            send, act_in[part + 1] = rounds.arrive(send, act_in[part + 1])
         else:
-            send, *following = rounds.arrive(send, *following)
-        backs.append(exchange(back, "exp", 1))
-        chain = reduce_chain(keep, send)
-        arrived, following = lax.optimization_barrier((next(chain), following))
-        rounds.live.append((chain, arrived))
-        rounds.send()
-        if following:
-            acts = following[0]
-    backs = rounds.arrive(*backs)
-    rounds.send()
+            (send,) = rounds.arrive(send)
+        rounds.start(reduce_chain(keep, send))
+        rounds.depart()
+        backs.append(exchange(after(back, *act_in[ahead:], send), "exp", 1))
+    for part in range(parts):
+        (backs[part],) = rounds.arrive(backs[part])
+        rounds.depart()
     output = combine(dense, backs, table, counts, place, experts)
     done = 0
     while rounds.live:
@@ -608,7 +618,7 @@
             grads = list(rounds.arrive(*grads))
         else:
             (output,) = rounds.arrive(output)
-        rounds.send()
+        rounds.depart()
         while done < len(rounds.results):
             grads = widen_group(
                 offsets[done], SIZES[done], place, rounds.results[done], grads, experts, channels

time: 186 us -> 172 us (0.925)
  waiting for transfers between devices: 73.6 us -> 36.7 us
  starting transfers between devices: 33.3 us -> 49.4 us
  Pallas kernels: 63.1 us -> 75.2 us
  other arithmetic: 6.49 us -> 1.34 us
    ppermute x18 -> x30, waiting for transfers between devices: 42.5 us -> 8.71 us  [exchange(): return lax.ppermute(value, axis, [(i, i ^ flip) for i in range(count)])]
    ppermute x18 -> x30, starting transfers between devices: 13.6 us -> 26 us  [exchange(): return lax.ppermute(value, axis, [(i, i ^ flip) for i in range(count)])]
    pallas_call x2 -> x5, Pallas kernels: 27.5 us -> 35 us  [the longest x4 21.7 us: far_part(): pl.pallas_call(functools.partial(far_kernel, offset), grid_spec=pltpu.Pre...]
    ppermute x12 -> x15, starting transfers between devices: 19.7 us -> 23.4 us  [shift(): return lax.ppermute(value, 'dp', perm)]
    ppermute x12 -> x15, waiting for transfers between devices: 31.1 us -> 28 us  [shift(): return lax.ppermute(value, 'dp', perm)]
    pallas_call x2 -> x4, Pallas kernels: 8.29 us -> 11.3 us  [widen_group(): pl.pallas_call(functools.partial(widen_kernel, pieces), grid=(1,), in_spe...]
    slice x0 -> x4, local copies, waits for them, and re-layouts: none -> 2.58 us  [arrive(): got.append(sent[kind][first:used[kind]].reshape(value.shape))]
    unnamed x41 -> x73, local copies, waits for them, and re-layouts: 5.01 us -> 2.47 us
  transfers between devices with their start and end apart: 30 -> 45, of which waited for: 13 -> 10; matrix products, arithmetic and copies ran while one was open for 4% -> 3% of each run, Pallas kernels for 32% -> 42%
where the time goes in v1:
time: 172 us
  Pallas kernels  75.2 us (44%)
  starting transfers between devices  49.4 us (29%)
  waiting for transfers between devices  36.7 us (21%)
  local copies, waits for them, and re-layouts  7.51 us (4%)
    ppermute x15, waiting for transfers between devices, shift(): return lax.ppermute(value, 'dp', perm)  28 us
    ppermute x30, starting transfers between devices, exchange(): return lax.ppermute(value, axis, [(i, i ^ flip) for i in range(count)])  26 us
    ppermute x15, starting transfers between devices, shift(): return lax.ppermute(value, 'dp', perm)  23.4 us
    pallas_call x1, Pallas kernels, dense_part(): pl.pallas_call(dense_kernel, grid=(rows // TILE,), in_specs=[SM] * 3 + [V...  22.5 us
    pallas_call x4, Pallas kernels, far_part(): pl.pallas_call(functools.partial(far_kernel, offset), grid_spec=pltpu.Pre...  21.7 us
    pallas_call x1, Pallas kernels, own_part(): pl.pallas_call(own_kernel, grid=(experts,), in_specs=[SM, SM, SM, VM, VM,...  13.3 us
    pallas_call x4, Pallas kernels, widen_group(): pl.pallas_call(functools.partial(widen_kernel, pieces), grid=(1,), in_spe...  11.3 us
    ppermute x30, waiting for transfers between devices, exchange(): return lax.ppermute(value, axis, [(i, i ^ flip) for i in range(count)])  8.71 us
  transfers between devices with their start and end apart: 45, of which 10 were waited for; matrix products, arithmetic and copies ran while one was open for 3% of the time, Pallas kernels for 42%

profile of v1, /device:TPU:0, one launch (start us, length us, event | category | flops | bytes accessed | tf_op | source)
XLA Modules:
  0.0 171.6 jit_solution(18024842880578401394)
XLA Ops:
  0.6 1.0 dynamic-slice_bitcast_fusion
  1.6 3.0 %collective-permute-start.1 = (bf16[3,192,256]{2,1,0:T(8,128)(2,1)S(1)}, bf16[3,192,256]{2,1,0:T(8,128)(2,1)S(1)}, u32[]{:S(2)}, u32[]{:S(2)}) collective-permute-start(bf16[3,192,256]{2,1,0:T(8,128)(2,1)S(1)} %dynamic-slice_bitcast_fusion), channel_id=1, source_target_pairs={{0,16},{16,0},{1,17},{17,1},{2,18},{18,2},{3,19},{19,3},{4,20},{20... | collective-permute-start | bytes 884744 | tf_op jit(solution)/shard_map/ppermute | solution.py:441
  6.7 3.2 %route_blocks.1 = (s32[48]{0:T(128)}, s32[16]{0:T(128)}, bf16[6,192,128]{2,1,0:T(8,128)(2,1)}, bf16[6,192,128]{2,1,0:T(8,128)(2,1)}, bf16[6,192,128]{2,1,0:T(8,128)(2,1)}, /*index=5*/bf16[6,192,128]{2,1,0:T(8,128)(2,1)}) custom-call(s32[32]{0:T(128)} %reshape.104.labels, s32[5]{0:T(128)} %stack.83.place, bf16[16,192,256]{2,1,0:T(8,128)(2,1)} %bitcast.143), custom_call_target="tpu_custom_call" | custom-call | tf_op jit(solution)/shard_map/route_blocks/pallas_call | solution.py:243
  9.9 1.6 collective-permute-start
  12.0 1.5 collective-permute-start.3
  14.1 1.5 collective-permute-start.5
  15.6 22.5 %dense_block.1 = (bf16[16,192,256]{2,1,0:T(8,128)(2,1)}, bf16[6,192,128]{2,1,0:T(8,128)(2,1)}, bf16[6,192,128]{2,1,0:T(8,128)(2,1)}, bf16[6,192,128]{2,1,0:T(8,128)(2,1)}, bf16[6,192,128]{2,1,0:T(8,128)(2,1)}) custom-call(s32[5]{0:T(128)} %stack.83.place, s32[48]{0:T(128)} %get-tuple-element.91.table.tables, s32[16]{0:T(128)} %get-tuple-element.90.counts.tallies, ...), custom_call_target="tpu_custom_call" | custom-call | flops 68719476736 | bytes 1048576 | tf_op jit(solution)/shard_map/dense_block/pallas_call | solution.py:188
  38.1 0.8 collective-permute-done.5.gs
  39.4 1.5 collective-permute-start.6
  40.9 13.3 %own_blocks.1 = (bf16[16,192,256]{2,1,0:T(8,128)(2,1)}, f32[8,192,768]{2,1,0:T(8,128)}, f32[8,192,768]{2,1,0:T(8,128)}) custom-call(s32[5]{0:T(128)} %stack.83.place, s32[48]{0:T(128)} %get-tuple-element.91.table.tables, s32[16]{0:T(128)} %get-tuple-element.90.counts.tallies, bf16[16,192,256]{2,1,0:T(8,128)(2,1)} %get-tuple-element.98.dense_in, ...), custom_call_target="tpu_custom_call" | custom-call | flops 68719476736 | bytes 1048576 | tf_op jit(solution)/shard_map/own_blocks/pallas_call | solution.py:318
  54.4 1.8 %collective-permute-start.9 = (bf16[6,192,128]{2,1,0:T(8,128)(2,1)S(1)}, bf16[6,192,128]{2,1,0:T(8,128)(2,1)S(1)}, u32[]{:S(2)}, u32[]{:S(2)}) collective-permute-start(bf16[6,192,128]{2,1,0:T(8,128)(2,1)S(1)} %copy-done.29), channel_id=1, source_target_pairs={{0,1},{1,0},{2,3},{3,2},{4,5},{5,4},{6,7},{7,6},{8,9},{9,8},{10,11... | collective-permute-start | bytes 884744 | tf_op jit(solution)/shard_map/ppermute | solution.py:441
  57.0 5.3 %far_blocks.4 = (bf16[6,192,128]{2,1,0:T(8,128)(2,1)}, bf16[2,192,768]{2,1,0:T(8,128)(2,1)}, bf16[2,192,768]{2,1,0:T(8,128)(2,1)}) custom-call(s32[5]{0:T(128)} %stack.83.place, s32[16]{0:T(128)} %copy-done.35, bf16[6,192,128]{2,1,0:T(8,128)(2,1)} %copy-done.33, bf16[6,192,128]{2,1,0:T(8,128)(2,1)} %copy-done.23, bf16[8,192,768]{2,1,0:T(8,128)(2,1)} %w_in.9, ...), custom_call_target="tpu_custom_call" | custom-call | flops 68719476736 | bytes 1048576 | tf_op jit(solution)/shard_map/far_blocks/pallas_call | solution.py:360
  62.4 5.5 %far_blocks.5 = (bf16[6,192,128]{2,1,0:T(8,128)(2,1)}, bf16[2,192,768]{2,1,0:T(8,128)(2,1)}, bf16[2,192,768]{2,1,0:T(8,128)(2,1)}) custom-call(s32[5]{0:T(128)} %stack.83.place, s32[16]{0:T(128)} %copy-done.35, bf16[6,192,128]{2,1,0:T(8,128)(2,1)} %copy-done.32, bf16[6,192,128]{2,1,0:T(8,128)(2,1)} %copy-done.22, bf16[8,192,768]{2,1,0:T(8,128)(2,1)} %w_in.9, ...), custom_call_target="tpu_custom_call" | custom-call | flops 68719476736 | bytes 1048576 | tf_op jit(solution)/shard_map/far_blocks/pallas_call | solution.py:360
  68.7 5.4 %far_blocks.6 = (bf16[6,192,128]{2,1,0:T(8,128)(2,1)}, bf16[2,192,768]{2,1,0:T(8,128)(2,1)}, bf16[2,192,768]{2,1,0:T(8,128)(2,1)}) custom-call(s32[5]{0:T(128)} %stack.83.place, s32[16]{0:T(128)} %copy-done.35, bf16[6,192,128]{2,1,0:T(8,128)(2,1)} %copy-done.31, bf16[6,192,128]{2,1,0:T(8,128)(2,1)} %copy-done.19, bf16[8,192,768]{2,1,0:T(8,128)(2,1)} %w_in.9, ...), custom_call_target="tpu_custom_call" | custom-call | flops 68719476736 | bytes 1048576 | tf_op jit(solution)/shard_map/far_blocks/pallas_call | solution.py:360
  74.1 3.3 %collective-permute-done.11 = bf16[192,768]{1,0:T(8,128)(2,1)S(1)} collective-permute-done((bf16[192,768]{1,0:T(8,128)(2,1)S(1)}, bf16[192,768]{1,0:T(8,128)(2,1)S(1)}, u32[]{:S(2)}, u32[]{:S(2)}) %collective-permute-start.11) | collective-permute-done | bytes 294944 | tf_op jit(solution)/shard_map/ppermute | solution.py:441
  77.5 3.7 %collective-permute-start.17 = (bf16[48,768]{1,0:T(8,128)(2,1)S(1)}, bf16[48,768]{1,0:T(8,128)(2,1)S(1)}, u32[]{:S(2)}, u32[]{:S(2)}) collective-permute-start(bf16[48,768]{1,0:T(8,128)(2,1)S(1)} %get-tuple-element.192), channel_id=1, source_target_pairs={{0,12},{2,14},{4,0},{6,2},{8,4},{10,6},{12,8},{14,10},{1,13},{3,15... | collective-permute-start | bytes 221192 | tf_op jit(solution)/shard_map/ppermute | solution.py:448
  81.2 1.0 collective-permute-start.15
  82.9 5.5 %far_blocks.7 = (bf16[6,192,128]{2,1,0:T(8,128)(2,1)}, bf16[2,192,768]{2,1,0:T(8,128)(2,1)}, bf16[2,192,768]{2,1,0:T(8,128)(2,1)}) custom-call(s32[5]{0:T(128)} %stack.83.place, s32[16]{0:T(128)} %copy-done.35, bf16[6,192,128]{2,1,0:T(8,128)(2,1)} %copy-done.27, bf16[6,192,128]{2,1,0:T(8,128)(2,1)} %copy-done.25, bf16[8,192,768]{2,1,0:T(8,128)(2,1)} %w_in.9, ...), custom_call_target="tpu_custom_call" | custom-call | flops 68719476736 | bytes 1048576 | tf_op jit(solution)/shard_map/far_blocks/pallas_call | solution.py:360
  88.4 2.5 %collective-permute-start.23 = (bf16[6,192,128]{2,1,0:T(8,128)(2,1)S(1)}, bf16[6,192,128]{2,1,0:T(8,128)(2,1)S(1)}, u32[]{:S(2)}, u32[]{:S(2)}) collective-permute-start(bf16[6,192,128]{2,1,0:T(8,128)(2,1)S(1)} %copy-done.24), channel_id=1, source_target_pairs={{0,1},{1,0},{2,3},{3,2},{4,5},{5,4},{6,7},{7,6},{8,9},{9,8},{10,11... | collective-permute-start | bytes 884744 | tf_op jit(solution)/shard_map/ppermute | solution.py:441
  91.2 1.2 collective-permute-start.19
  92.5 3.2 %collective-permute-start.22 = (bf16[96,768]{1,0:T(8,128)(2,1)S(1)}, bf16[96,768]{1,0:T(8,128)(2,1)S(1)}, u32[]{:S(2)}, u32[]{:S(2)}) collective-permute-start(bf16[96,768]{1,0:T(8,128)(2,1)S(1)} %get-tuple-element.201), channel_id=1, source_target_pairs={{0,12},{2,14},{4,0},{6,2},{8,4},{10,6},{12,8},{14,10},{1,13},{3,15... | collective-permute-start | bytes 442376 | tf_op jit(solution)/shard_map/ppermute | solution.py:448
  95.8 1.1 collective-permute-start.21
  96.9 1.6 collective-permute-done.23.refs_0_
  98.5 2.5 %collective-permute-start.20 = (bf16[96,768]{1,0:T(8,128)(2,1)S(1)}, bf16[96,768]{1,0:T(8,128)(2,1)S(1)}, u32[]{:S(2)}, u32[]{:S(2)}) collective-permute-start(bf16[96,768]{1,0:T(8,128)(2,1)S(1)} %get-tuple-element.203), channel_id=1, source_target_pairs={{0,4},{2,6},{4,8},{6,10},{8,12},{10,14},{12,0},{14,2},{1,5},{3,7},... | collective-permute-start | bytes 442376 | tf_op jit(solution)/shard_map/ppermute | solution.py:448
  101.0 1.7 %collective-permute-start.29 = (bf16[6,192,128]{2,1,0:T(8,128)(2,1)S(1)}, bf16[6,192,128]{2,1,0:T(8,128)(2,1)S(1)}, u32[]{:S(2)}, u32[]{:S(2)}) collective-permute-start(bf16[6,192,128]{2,1,0:T(8,128)(2,1)S(1)} %copy-done.18), channel_id=1, source_target_pairs={{0,1},{1,0},{2,3},{3,2},{4,5},{5,4},{6,7},{7,6},{8,9},{9,8},{10,11... | collective-permute-start | bytes 884744 | tf_op jit(solution)/shard_map/ppermute | solution.py:441
  102.7 7.9 %collective-permute-done.21 = bf16[96,768]{1,0:T(8,128)(2,1)S(1)} collective-permute-done((bf16[96,768]{1,0:T(8,128)(2,1)S(1)}, bf16[96,768]{1,0:T(8,128)(2,1)S(1)}, u32[]{:S(2)}, u32[]{:S(2)}) %collective-permute-start.21) | collective-permute-done | bytes 147488 | tf_op jit(solution)/shard_map/ppermute | solution.py:448
  111.8 1.3 collective-permute-start.27
  113.1 3.5 %collective-permute-start.26 = (bf16[96,768]{1,0:T(8,128)(2,1)S(1)}, bf16[96,768]{1,0:T(8,128)(2,1)S(1)}, u32[]{:S(2)}, u32[]{:S(2)}) collective-permute-start(bf16[96,768]{1,0:T(8,128)(2,1)S(1)} %get-tuple-element.200), channel_id=1, source_target_pairs={{0,4},{2,6},{4,8},{6,10},{8,12},{10,14},{12,0},{14,2},{1,5},{3,7},... | collective-permute-start | bytes 442376 | tf_op jit(solution)/shard_map/ppermute | solution.py:448
  116.6 2.1 %collective-permute-done.28 = bf16[96,768]{1,0:T(8,128)(2,1)S(1)} collective-permute-done((bf16[96,768]{1,0:T(8,128)(2,1)S(1)}, bf16[96,768]{1,0:T(8,128)(2,1)S(1)}, u32[]{:S(2)}, u32[]{:S(2)}) %collective-permute-start.28) | collective-permute-done | bytes 147488 | tf_op jit(solution)/shard_map/ppermute | solution.py:448
  118.8 1.2 collective-permute-start.35
  119.9 6.8 %collective-permute-done.27 = bf16[96,768]{1,0:T(8,128)(2,1)S(1)} collective-permute-done((bf16[96,768]{1,0:T(8,128)(2,1)S(1)}, bf16[96,768]{1,0:T(8,128)(2,1)S(1)}, u32[]{:S(2)}, u32[]{:S(2)}) %collective-permute-start.27) | collective-permute-done | bytes 147488 | tf_op jit(solution)/shard_map/ppermute | solution.py:448
  127.5 1.5 collective-permute-start.31
  129.2 1.8 %collective-permute-start.33 = (bf16[96,768]{1,0:T(8,128)(2,1)S(1)}, bf16[96,768]{1,0:T(8,128)(2,1)S(1)}, u32[]{:S(2)}, u32[]{:S(2)}) collective-permute-start(bf16[96,768]{1,0:T(8,128)(2,1)S(1)} %get-tuple-element.196), channel_id=1, source_target_pairs={{0,8},{2,10},{4,12},{6,14},{8,0},{10,2},{12,4},{14,6},{1,9},{3,11}... | collective-permute-start | bytes 442376 | tf_op jit(solution)/shard_map/ppermute | solution.py:448
  131.0 1.9 %collective-permute-start.32 = (bf16[96,768]{1,0:T(8,128)(2,1)S(1)}, bf16[96,768]{1,0:T(8,128)(2,1)S(1)}, u32[]{:S(2)}, u32[]{:S(2)}) collective-permute-start(bf16[96,768]{1,0:T(8,128)(2,1)S(1)} %get-tuple-element.197), channel_id=1, source_target_pairs={{0,4},{2,6},{4,8},{6,10},{8,12},{10,14},{12,0},{14,2},{1,5},{3,7},... | collective-permute-start | bytes 442376 | tf_op jit(solution)/shard_map/ppermute | solution.py:448
  133.0 2.6 %collective-permute-done.34 = bf16[96,768]{1,0:T(8,128)(2,1)S(1)} collective-permute-done((bf16[96,768]{1,0:T(8,128)(2,1)S(1)}, bf16[96,768]{1,0:T(8,128)(2,1)S(1)}, u32[]{:S(2)}, u32[]{:S(2)}) %collective-permute-start.34) | collective-permute-done | bytes 147488 | tf_op jit(solution)/shard_map/ppermute | solution.py:448
  135.6 1.2 collective-permute-start.41
  136.8 7.9 %collective-permute-done.33 = bf16[96,768]{1,0:T(8,128)(2,1)S(1)} collective-permute-done((bf16[96,768]{1,0:T(8,128)(2,1)S(1)}, bf16[96,768]{1,0:T(8,128)(2,1)S(1)}, u32[]{:S(2)}, u32[]{:S(2)}) %collective-permute-start.33) | collective-permute-done | bytes 147488 | tf_op jit(solution)/shard_map/ppermute | solution.py:448
  144.9 1.2 collective-permute-start.39
  146.1 1.9 %collective-permute-start.38 = (bf16[48,768]{1,0:T(8,128)(2,1)S(1)}, bf16[48,768]{1,0:T(8,128)(2,1)S(1)}, u32[]{:S(2)}, u32[]{:S(2)}) collective-permute-start(bf16[48,768]{1,0:T(8,128)(2,1)S(1)} %fusion.14), channel_id=1, source_target_pairs={{0,4},{2,6},{4,8},{6,10},{8,12},{10,14},{12,0},{14,2},{1,5},{3,7},... | collective-permute-start | bytes 221192 | tf_op jit(solution)/shard_map/ppermute | solution.py:448
  148.8 0.8 fusion.24
  149.7 2.8 %widen_gradients.4 = (f32[8,192,768]{2,1,0:T(8,128)}, f32[8,192,768]{2,1,0:T(8,128)}) custom-call(s32[5]{0:T(128)} %stack.83.place, bf16[192,768]{1,0:T(8,128)(2,1)} %bitcast.147, bf16[192,768]{1,0:T(8,128)(2,1)} %copy-done.2, bf16[192,768]{1,0:T(8,128)(2,1)} %copy-done.20, bf16[192,768]{1,0:T(8,128)(2,1)} %get-tuple-element.177.other2), custom_call_target="tpu_custom_call" | custom-call | flops 68719476736 | bytes 1048576 | tf_op jit(solution)/shard_map/widen_gradients/pallas_call | solution.py:557
  153.3 3.0 %collective-permute-done.37.other = bf16[192,768]{1,0:T(8,128)(2,1)S(1)} collective-permute-done((bf16[192,768]{1,0:T(8,128)(2,1)S(1)}, bf16[192,768]{1,0:T(8,128)(2,1)S(1)}, u32[]{:S(2)}, u32[]{:S(2)}) %collective-permute-start.37) | collective-permute-done | bytes 294944 | tf_op jit(solution)/shard_map/ppermute | solution.py:441
  157.0 0.9 fusion.25
  157.8 3.2 %combine_blocks.1 = bf16[16,192,256]{2,1,0:T(8,128)(2,1)} custom-call(s32[48]{0:T(128)} %get-tuple-element.91.table.tables, s32[16]{0:T(128)} %get-tuple-element.90.counts.tallies, s32[5]{0:T(128)} %stack.83.place, bf16[16,192,256]{2,1,0:T(8,128)(2,1)} %get-tuple-element.109.dense_in, ...), custom_call_target="tpu_custom_call", output_to_operand_aliasing={{}: (3, {})} | custom-call | flops 68719476736 | bytes 1048576 | tf_op jit(solution)/shard_map/combine_blocks/pallas_call | solution.py:422
  161.1 2.8 %widen_gradients.5 = (f32[8,192,768]{2,1,0:T(8,128)}, f32[8,192,768]{2,1,0:T(8,128)}) custom-call(s32[5]{0:T(128)} %stack.83.place, bf16[192,768]{1,0:T(8,128)(2,1)} %bitcast.150, bf16[192,768]{1,0:T(8,128)(2,1)} %copy-done.9, bf16[192,768]{1,0:T(8,128)(2,1)} %get-tuple-element.178.mine2, ...), custom_call_target="tpu_custom_call", output_to_operand_aliasing={{0}: (5, {}), {1}: (6, {})} | custom-call | flops 68719476736 | bytes 1048576 | tf_op jit(solution)/shard_map/widen_gradients/pallas_call | solution.py:557
  164.4 0.9 fusion.26
  165.3 2.8 %widen_gradients.6 = (f32[8,192,768]{2,1,0:T(8,128)}, f32[8,192,768]{2,1,0:T(8,128)}) custom-call(s32[5]{0:T(128)} %stack.83.place, bf16[192,768]{1,0:T(8,128)(2,1)} %bitcast.153, bf16[192,768]{1,0:T(8,128)(2,1)} %copy-done.10, bf16[192,768]{1,0:T(8,128)(2,1)} %get-tuple-element.180.mine2, ...), custom_call_target="tpu_custom_call", output_to_operand_aliasing={{0}: (5, {}), {1}: (6, {})} | custom-call | flops 68719476736 | bytes 1048576 | tf_op jit(solution)/shard_map/widen_gradients/pallas_call | solution.py:557
  168.8 2.8 %widen_gradients.7 = (f32[8,192,768]{2,1,0:T(8,128)}, f32[8,192,768]{2,1,0:T(8,128)}) custom-call(s32[5]{0:T(128)} %stack.83.place, bf16[192,768]{1,0:T(8,128)(2,1)} %bitcast.156, bf16[192,768]{1,0:T(8,128)(2,1)} %copy-done.30, bf16[192,768]{1,0:T(8,128)(2,1)} %get-tuple-element.182.mine2, ...), custom_call_target="tpu_custom_call", output_to_operand_aliasing={{0}: (5, {}), {1}: (6, {})} | custom-call | flops 68719476736 | bytes 1048576 | tf_op jit(solution)/shard_map/widen_gradients/pallas_call | solution.py:557
  (169 shorter events, 11.9 us)
Async XLA Ops:
  1.6 12.4 %collective-permute-start.1 = (bf16[3,192,256]{2,1,0:T(8,128)(2,1)S(1)}, bf16[3,192,256]{2,1,0:T(8,128)(2,1)S(1)}, u32[]{:S(2)}, u32[]{:S(2)}) collective-permute-start(bf16[3,192,256]{2,1,0:T(8,128)(2,1)S(1)} %dynamic-slice_bitcast_fusion), channel_id=1, source_target_pairs={{0,16},{16,0},{1,17},{17,1},{2,18},{18,2},{3,19},{19,3},{4,20},{20... | collective-permute-start | bytes 884744 | tf_op jit(solution)/shard_map/ppermute | solution.py:441
  9.9 46.5 %collective-permute-start = (s32[16]{0:T(128)}, s32[16]{0:T(128)S(1)}, u32[]{:S(2)}, u32[]{:S(2)}) collective-permute-start(s32[16]{0:T(128)} %get-tuple-element.90.counts.tallies), channel_id=1, source_target_pairs={{0,1},{1,0},{2,3},{3,2},{4,5},{5,4},{6,7},{7,6},{8,9},{9,8},{10,11... | collective-permute-start | bytes 200 | tf_op jit(solution)/shard_map/ppermute | solution.py:441
  11.5 26.5 %collective-permute-start.2 = (bf16[6,192,128]{2,1,0:T(8,128)(2,1)}, bf16[6,192,128]{2,1,0:T(8,128)(2,1)S(1)}, u32[]{:S(2)}, u32[]{:S(2)}) collective-permute-start(bf16[6,192,128]{2,1,0:T(8,128)(2,1)} %get-tuple-element.93), channel_id=1, source_target_pairs={{0,1},{1,0},{2,3},{3,2},{4,5},{5,4},{6,7},{7,6},{8,9},{9,8},{10,11... | collective-permute-start | bytes 884744 | tf_op jit(solution)/shard_map/ppermute | solution.py:441
  12.0 26.0 %collective-permute-start.3 = (bf16[6,192,128]{2,1,0:T(8,128)(2,1)}, bf16[6,192,128]{2,1,0:T(8,128)(2,1)S(1)}, u32[]{:S(2)}, u32[]{:S(2)}) collective-permute-start(bf16[6,192,128]{2,1,0:T(8,128)(2,1)} %get-tuple-element.94), channel_id=1, source_target_pairs={{0,1},{1,0},{2,3},{3,2},{4,5},{5,4},{6,7},{7,6},{8,9},{9,8},{10,11... | collective-permute-start | bytes 884744 | tf_op jit(solution)/shard_map/ppermute | solution.py:441
  13.6 24.5 %collective-permute-start.4 = (bf16[6,192,128]{2,1,0:T(8,128)(2,1)}, bf16[6,192,128]{2,1,0:T(8,128)(2,1)S(1)}, u32[]{:S(2)}, u32[]{:S(2)}) collective-permute-start(bf16[6,192,128]{2,1,0:T(8,128)(2,1)} %get-tuple-element.95), channel_id=1, source_target_pairs={{0,1},{1,0},{2,3},{3,2},{4,5},{5,4},{6,7},{7,6},{8,9},{9,8},{10,11... | collective-permute-start | bytes 884744 | tf_op jit(solution)/shard_map/ppermute | solution.py:441
  14.1 24.8 %collective-permute-start.5 = (bf16[6,192,128]{2,1,0:T(8,128)(2,1)}, bf16[6,192,128]{2,1,0:T(8,128)(2,1)S(1)}, u32[]{:S(2)}, u32[]{:S(2)}) collective-permute-start(bf16[6,192,128]{2,1,0:T(8,128)(2,1)} %get-tuple-element.96), channel_id=1, source_target_pairs={{0,1},{1,0},{2,3},{3,2},{4,5},{5,4},{6,7},{7,6},{8,9},{9,8},{10,11... | collective-permute-start | bytes 884744 | tf_op jit(solution)/shard_map/ppermute | solution.py:441
  38.9 15.4 %collective-permute-start.7 = (bf16[6,192,128]{2,1,0:T(8,128)(2,1)}, bf16[6,192,128]{2,1,0:T(8,128)(2,1)S(1)}, u32[]{:S(2)}, u32[]{:S(2)}) collective-permute-start(bf16[6,192,128]{2,1,0:T(8,128)(2,1)} %get-tuple-element.104), channel_id=1, source_target_pairs={{0,1},{1,0},{2,3},{3,2},{4,5},{5,4},{6,7},{7,6},{8,9},{9,8},{10,11... | collective-permute-start | bytes 884744 | tf_op jit(solution)/shard_map/ppermute | solution.py:441
  39.4 14.9 %collective-permute-start.6 = (bf16[6,192,128]{2,1,0:T(8,128)(2,1)}, bf16[6,192,128]{2,1,0:T(8,128)(2,1)S(1)}, u32[]{:S(2)}, u32[]{:S(2)}) collective-permute-start(bf16[6,192,128]{2,1,0:T(8,128)(2,1)} %get-tuple-element.97), channel_id=1, source_target_pairs={{0,1},{1,0},{2,3},{3,2},{4,5},{5,4},{6,7},{7,6},{8,9},{9,8},{10,11... | collective-permute-start | bytes 884744 | tf_op jit(solution)/shard_map/ppermute | solution.py:441
  54.4 13.6 %collective-permute-start.9 = (bf16[6,192,128]{2,1,0:T(8,128)(2,1)S(1)}, bf16[6,192,128]{2,1,0:T(8,128)(2,1)S(1)}, u32[]{:S(2)}, u32[]{:S(2)}) collective-permute-start(bf16[6,192,128]{2,1,0:T(8,128)(2,1)S(1)} %copy-done.29), channel_id=1, source_target_pairs={{0,1},{1,0},{2,3},{3,2},{4,5},{5,4},{6,7},{7,6},{8,9},{9,8},{10,11... | collective-permute-start | bytes 884744 | tf_op jit(solution)/shard_map/ppermute | solution.py:441
  56.2 11.7 %collective-permute-start.12 = (bf16[6,192,128]{2,1,0:T(8,128)(2,1)S(1)}, bf16[6,192,128]{2,1,0:T(8,128)(2,1)S(1)}, u32[]{:S(2)}, u32[]{:S(2)}) collective-permute-start(bf16[6,192,128]{2,1,0:T(8,128)(2,1)S(1)} %copy-done.28), channel_id=1, source_target_pairs={{0,1},{1,0},{2,3},{3,2},{4,5},{5,4},{6,7},{7,6},{8,9},{9,8},{10,11... | collective-permute-start | bytes 884744 | tf_op jit(solution)/shard_map/ppermute | solution.py:441
  62.3 5.6 %collective-permute-start.8 = (bf16[384,768]{1,0:T(8,128)(2,1)}, bf16[384,768]{1,0:T(8,128)(2,1)S(1)}, u32[]{:S(2)}, u32[]{:S(2)}) collective-permute-start(bf16[384,768]{1,0:T(8,128)(2,1)} %bitcast.181), channel_id=1, source_target_pairs={{0,2},{2,0},{4,6},{6,4},{8,10},{10,8},{12,14},{14,12},{1,3},{3,1},... | collective-permute-start | bytes 1769480 | tf_op jit(solution)/shard_map/ppermute | solution.py:441
  68.0 9.3 %collective-permute-start.11 = (bf16[192,768]{1,0:T(8,128)(2,1)S(1)}, bf16[192,768]{1,0:T(8,128)(2,1)S(1)}, u32[]{:S(2)}, u32[]{:S(2)}) collective-permute-start(bf16[192,768]{1,0:T(8,128)(2,1)S(1)} %fusion.8), channel_id=1, source_target_pairs={{0,16},{16,0},{1,17},{17,1},{2,18},{18,2},{3,19},{19,3},{4,20},{20... | collective-permute-start | bytes 884744 | tf_op jit(solution)/shard_map/ppermute | solution.py:441
  68.6 8.7 %collective-permute-start.10 = (bf16[384,768]{1,0:T(8,128)(2,1)}, bf16[384,768]{1,0:T(8,128)(2,1)S(1)}, u32[]{:S(2)}, u32[]{:S(2)}) collective-permute-start(bf16[384,768]{1,0:T(8,128)(2,1)} %bitcast.180), channel_id=1, source_target_pairs={{0,2},{2,0},{4,6},{6,4},{8,10},{10,8},{12,14},{14,12},{1,3},{3,1},... | collective-permute-start | bytes 1769480 | tf_op jit(solution)/shard_map/ppermute | solution.py:441
  77.5 10.9 %collective-permute-start.17 = (bf16[48,768]{1,0:T(8,128)(2,1)S(1)}, bf16[48,768]{1,0:T(8,128)(2,1)S(1)}, u32[]{:S(2)}, u32[]{:S(2)}) collective-permute-start(bf16[48,768]{1,0:T(8,128)(2,1)S(1)} %get-tuple-element.192), channel_id=1, source_target_pairs={{0,12},{2,14},{4,0},{6,2},{8,4},{10,6},{12,8},{14,10},{1,13},{3,15... | collective-permute-start | bytes 221192 | tf_op jit(solution)/shard_map/ppermute | solution.py:448
  81.2 9.8 %collective-permute-start.16 = (bf16[48,768]{1,0:T(8,128)(2,1)S(1)}, bf16[48,768]{1,0:T(8,128)(2,1)S(1)}, u32[]{:S(2)}, u32[]{:S(2)}) collective-permute-start(bf16[48,768]{1,0:T(8,128)(2,1)S(1)} %get-tuple-element.193), channel_id=1, source_target_pairs={{0,8},{2,10},{4,12},{6,14},{8,0},{10,2},{12,4},{14,6},{1,9},{3,11}... | collective-permute-start | bytes 221192 | tf_op jit(solution)/shard_map/ppermute | solution.py:448
  81.2 9.8 %collective-permute-start.15 = (bf16[48,768]{1,0:T(8,128)(2,1)S(1)}, bf16[48,768]{1,0:T(8,128)(2,1)S(1)}, u32[]{:S(2)}, u32[]{:S(2)}) collective-permute-start(bf16[48,768]{1,0:T(8,128)(2,1)S(1)} %get-tuple-element.194), channel_id=1, source_target_pairs={{0,4},{2,6},{4,8},{6,10},{8,12},{10,14},{12,0},{14,2},{1,5},{3,7},... | collective-permute-start | bytes 221192 | tf_op jit(solution)/shard_map/ppermute | solution.py:448
  82.3 8.7 %collective-permute-start.14 = (bf16[192,768]{1,0:T(8,128)(2,1)S(1)}, bf16[192,768]{1,0:T(8,128)(2,1)S(1)}, u32[]{:S(2)}, u32[]{:S(2)}) collective-permute-start(bf16[192,768]{1,0:T(8,128)(2,1)S(1)} %fusion.9), channel_id=1, source_target_pairs={{0,16},{16,0},{1,17},{17,1},{2,18},{18,2},{3,19},{19,3},{4,20},{20... | collective-permute-start | bytes 884744 | tf_op jit(solution)/shard_map/ppermute | solution.py:441
  82.9 8.1 %collective-permute-start.13 = (bf16[384,768]{1,0:T(8,128)(2,1)S(1)}, bf16[384,768]{1,0:T(8,128)(2,1)S(1)}, u32[]{:S(2)}, u32[]{:S(2)}) collective-permute-start(bf16[384,768]{1,0:T(8,128)(2,1)S(1)} %bitcast.179), channel_id=1, source_target_pairs={{0,2},{2,0},{4,6},{6,4},{8,10},{10,8},{12,14},{14,12},{1,3},{3,1},... | collective-permute-start | bytes 1769480 | tf_op jit(solution)/shard_map/ppermute | solution.py:441
  88.4 10.1 %collective-permute-start.23 = (bf16[6,192,128]{2,1,0:T(8,128)(2,1)S(1)}, bf16[6,192,128]{2,1,0:T(8,128)(2,1)S(1)}, u32[]{:S(2)}, u32[]{:S(2)}) collective-permute-start(bf16[6,192,128]{2,1,0:T(8,128)(2,1)S(1)} %copy-done.24), channel_id=1, source_target_pairs={{0,1},{1,0},{2,3},{3,2},{4,5},{5,4},{6,7},{7,6},{8,9},{9,8},{10,11... | collective-permute-start | bytes 884744 | tf_op jit(solution)/shard_map/ppermute | solution.py:441
  91.2 19.7 %copy-start.5 = (bf16[2,192,768]{2,1,0:T(8,128)(2,1)S(1)}, bf16[2,192,768]{2,1,0:T(8,128)(2,1)}, u32[]{:S(2)}) copy-start(bf16[2,192,768]{2,1,0:T(8,128)(2,1)} %get-tuple-element.135) | copy-start | bytes 1769476
  91.2 19.4 %collective-permute-start.19 = (bf16[192,768]{1,0:T(8,128)(2,1)S(1)}, bf16[192,768]{1,0:T(8,128)(2,1)S(1)}, u32[]{:S(2)}, u32[]{:S(2)}) collective-permute-start(bf16[192,768]{1,0:T(8,128)(2,1)S(1)} %fusion.10), channel_id=1, source_target_pairs={{0,16},{16,0},{1,17},{17,1},{2,18},{18,2},{3,19},{19,3},{4,20},{20... | collective-permute-start | bytes 884744 | tf_op jit(solution)/shard_map/ppermute | solution.py:441
  92.4 18.2 %collective-permute-start.18 = (bf16[384,768]{1,0:T(8,128)(2,1)S(1)}, bf16[384,768]{1,0:T(8,128)(2,1)S(1)}, u32[]{:S(2)}, u32[]{:S(2)}) collective-permute-start(bf16[384,768]{1,0:T(8,128)(2,1)S(1)} %bitcast.178), channel_id=1, source_target_pairs={{0,2},{2,0},{4,6},{6,4},{8,10},{10,8},{12,14},{14,12},{1,3},{3,1},... | collective-permute-start | bytes 1769480 | tf_op jit(solution)/shard_map/ppermute | solution.py:441
  92.5 8.4 %collective-permute-start.22 = (bf16[96,768]{1,0:T(8,128)(2,1)S(1)}, bf16[96,768]{1,0:T(8,128)(2,1)S(1)}, u32[]{:S(2)}, u32[]{:S(2)}) collective-permute-start(bf16[96,768]{1,0:T(8,128)(2,1)S(1)} %get-tuple-element.201), channel_id=1, source_target_pairs={{0,12},{2,14},{4,0},{6,2},{8,4},{10,6},{12,8},{14,10},{1,13},{3,15... | collective-permute-start | bytes 442376 | tf_op jit(solution)/shard_map/ppermute | solution.py:448
  95.8 14.8 %collective-permute-start.21 = (bf16[96,768]{1,0:T(8,128)(2,1)S(1)}, bf16[96,768]{1,0:T(8,128)(2,1)S(1)}, u32[]{:S(2)}, u32[]{:S(2)}) collective-permute-start(bf16[96,768]{1,0:T(8,128)(2,1)S(1)} %get-tuple-element.202), channel_id=1, source_target_pairs={{0,8},{2,10},{4,12},{6,14},{8,0},{10,2},{12,4},{14,6},{1,9},{3,11}... | collective-permute-start | bytes 442376 | tf_op jit(solution)/shard_map/ppermute | solution.py:448
  98.5 12.1 %collective-permute-start.20 = (bf16[96,768]{1,0:T(8,128)(2,1)S(1)}, bf16[96,768]{1,0:T(8,128)(2,1)S(1)}, u32[]{:S(2)}, u32[]{:S(2)}) collective-permute-start(bf16[96,768]{1,0:T(8,128)(2,1)S(1)} %get-tuple-element.203), channel_id=1, source_target_pairs={{0,4},{2,6},{4,8},{6,10},{8,12},{10,14},{12,0},{14,2},{1,5},{3,7},... | collective-permute-start | bytes 442376 | tf_op jit(solution)/shard_map/ppermute | solution.py:448
  101.0 12.2 %collective-permute-start.29 = (bf16[6,192,128]{2,1,0:T(8,128)(2,1)S(1)}, bf16[6,192,128]{2,1,0:T(8,128)(2,1)S(1)}, u32[]{:S(2)}, u32[]{:S(2)}) collective-permute-start(bf16[6,192,128]{2,1,0:T(8,128)(2,1)S(1)} %copy-done.18), channel_id=1, source_target_pairs={{0,1},{1,0},{2,3},{3,2},{4,5},{5,4},{6,7},{7,6},{8,9},{9,8},{10,11... | collective-permute-start | bytes 884744 | tf_op jit(solution)/shard_map/ppermute | solution.py:441
  110.8 16.0 %collective-permute-start.24 = (bf16[192,768]{1,0:T(8,128)(2,1)S(1)}, bf16[192,768]{1,0:T(8,128)(2,1)S(1)}, u32[]{:S(2)}, u32[]{:S(2)}) collective-permute-start(bf16[192,768]{1,0:T(8,128)(2,1)S(1)} %bitcast.145), channel_id=1, source_target_pairs={{0,2},{2,0},{4,6},{6,4},{8,10},{10,8},{12,14},{14,12},{1,3},{3,1},... | collective-permute-start | bytes 884744 | tf_op jit(solution)/shard_map/ppermute | solution.py:441
  111.0 15.8 %collective-permute-start.25 = (bf16[384,768]{1,0:T(8,128)(2,1)S(1)}, bf16[384,768]{1,0:T(8,128)(2,1)S(1)}, u32[]{:S(2)}, u32[]{:S(2)}) collective-permute-start(bf16[384,768]{1,0:T(8,128)(2,1)S(1)} %pad_maximum_fusion), channel_id=1, source_target_pairs={{0,16},{16,0},{1,17},{17,1},{2,18},{18,2},{3,19},{19,3},{4,20},{20... | collective-permute-start | bytes 1769480 | tf_op jit(solution)/shard_map/ppermute | solution.py:441
  111.8 7.0 %collective-permute-start.28 = (bf16[96,768]{1,0:T(8,128)(2,1)S(1)}, bf16[96,768]{1,0:T(8,128)(2,1)S(1)}, u32[]{:S(2)}, u32[]{:S(2)}) collective-permute-start(bf16[96,768]{1,0:T(8,128)(2,1)S(1)} %get-tuple-element.198), channel_id=1, source_target_pairs={{0,12},{2,14},{4,0},{6,2},{8,4},{10,6},{12,8},{14,10},{1,13},{3,15... | collective-permute-start | bytes 442376 | tf_op jit(solution)/shard_map/ppermute | solution.py:448
  111.8 14.9 %collective-permute-start.27 = (bf16[96,768]{1,0:T(8,128)(2,1)S(1)}, bf16[96,768]{1,0:T(8,128)(2,1)S(1)}, u32[]{:S(2)}, u32[]{:S(2)}) collective-permute-start(bf16[96,768]{1,0:T(8,128)(2,1)S(1)} %get-tuple-element.199), channel_id=1, source_target_pairs={{0,8},{2,10},{4,12},{6,14},{8,0},{10,2},{12,4},{14,6},{1,9},{3,11}... | collective-permute-start | bytes 442376 | tf_op jit(solution)/shard_map/ppermute | solution.py:448
  113.1 13.6 %collective-permute-start.26 = (bf16[96,768]{1,0:T(8,128)(2,1)S(1)}, bf16[96,768]{1,0:T(8,128)(2,1)S(1)}, u32[]{:S(2)}, u32[]{:S(2)}) collective-permute-start(bf16[96,768]{1,0:T(8,128)(2,1)S(1)} %get-tuple-element.200), channel_id=1, source_target_pairs={{0,4},{2,6},{4,8},{6,10},{8,12},{10,14},{12,0},{14,2},{1,5},{3,7},... | collective-permute-start | bytes 442376 | tf_op jit(solution)/shard_map/ppermute | solution.py:448
  118.8 12.3 %collective-permute-start.35 = (bf16[6,192,128]{2,1,0:T(8,128)(2,1)S(1)}, bf16[6,192,128]{2,1,0:T(8,128)(2,1)S(1)}, u32[]{:S(2)}, u32[]{:S(2)}) collective-permute-start(bf16[6,192,128]{2,1,0:T(8,128)(2,1)S(1)} %copy-done.15), channel_id=1, source_target_pairs={{0,1},{1,0},{2,3},{3,2},{4,5},{5,4},{6,7},{7,6},{8,9},{9,8},{10,11... | collective-permute-start | bytes 884744 | tf_op jit(solution)/shard_map/ppermute | solution.py:441
  127.0 17.7 %copy-start.1 = (bf16[4,48,768]{2,1,0:T(8,128)(2,1)}, bf16[4,48,768]{2,1,0:T(8,128)(2,1)S(1)}, u32[]{:S(2)}) copy-start(bf16[4,48,768]{2,1,0:T(8,128)(2,1)S(1)} %pad_maximum_fusion.5) | copy-start | bytes 884740
  127.5 17.2 %collective-permute-start.30 = (bf16[384,768]{1,0:T(8,128)(2,1)S(1)}, bf16[384,768]{1,0:T(8,128)(2,1)S(1)}, u32[]{:S(2)}, u32[]{:S(2)}) collective-permute-start(bf16[384,768]{1,0:T(8,128)(2,1)S(1)} %pad_maximum_fusion.1), channel_id=1, source_target_pairs={{0,2},{2,0},{4,6},{6,4},{8,10},{10,8},{12,14},{14,12},{1,3},{3,1},... | collective-permute-start | bytes 1769480 | tf_op jit(solution)/shard_map/ppermute | solution.py:441
  127.5 17.1 %collective-permute-start.31 = (bf16[192,768]{1,0:T(8,128)(2,1)S(1)}, bf16[192,768]{1,0:T(8,128)(2,1)S(1)}, u32[]{:S(2)}, u32[]{:S(2)}) collective-permute-start(bf16[192,768]{1,0:T(8,128)(2,1)S(1)} %bitcast.149), channel_id=1, source_target_pairs={{0,16},{16,0},{1,17},{17,1},{2,18},{18,2},{3,19},{19,3},{4,20},{20... | collective-permute-start | bytes 884744 | tf_op jit(solution)/shard_map/ppermute | solution.py:441
  129.2 6.4 %collective-permute-start.34 = (bf16[96,768]{1,0:T(8,128)(2,1)S(1)}, bf16[96,768]{1,0:T(8,128)(2,1)S(1)}, u32[]{:S(2)}, u32[]{:S(2)}) collective-permute-start(bf16[96,768]{1,0:T(8,128)(2,1)S(1)} %get-tuple-element.195), channel_id=1, source_target_pairs={{0,12},{2,14},{4,0},{6,2},{8,4},{10,6},{12,8},{14,10},{1,13},{3,15... | collective-permute-start | bytes 442376 | tf_op jit(solution)/shard_map/ppermute | solution.py:448
  129.2 15.4 %collective-permute-start.33 = (bf16[96,768]{1,0:T(8,128)(2,1)S(1)}, bf16[96,768]{1,0:T(8,128)(2,1)S(1)}, u32[]{:S(2)}, u32[]{:S(2)}) collective-permute-start(bf16[96,768]{1,0:T(8,128)(2,1)S(1)} %get-tuple-element.196), channel_id=1, source_target_pairs={{0,8},{2,10},{4,12},{6,14},{8,0},{10,2},{12,4},{14,6},{1,9},{3,11}... | collective-permute-start | bytes 442376 | tf_op jit(solution)/shard_map/ppermute | solution.py:448
  131.0 18.6 %copy-start.21 = (bf16[6,192,128]{2,1,0:T(8,128)(2,1)}, bf16[6,192,128]{2,1,0:T(8,128)(2,1)S(1)}, u32[]{:S(2)}) copy-start(bf16[6,192,128]{2,1,0:T(8,128)(2,1)S(1)} %collective-permute-done.35.refs_2_) | copy-start | bytes 884740
  131.0 13.6 %collective-permute-start.32 = (bf16[96,768]{1,0:T(8,128)(2,1)S(1)}, bf16[96,768]{1,0:T(8,128)(2,1)S(1)}, u32[]{:S(2)}, u32[]{:S(2)}) collective-permute-start(bf16[96,768]{1,0:T(8,128)(2,1)S(1)} %get-tuple-element.197), channel_id=1, source_target_pairs={{0,4},{2,6},{4,8},{6,10},{8,12},{10,14},{12,0},{14,2},{1,5},{3,7},... | collective-permute-start | bytes 442376 | tf_op jit(solution)/shard_map/ppermute | solution.py:448
  135.6 14.0 %collective-permute-start.41 = (bf16[6,192,128]{2,1,0:T(8,128)(2,1)S(1)}, bf16[6,192,128]{2,1,0:T(8,128)(2,1)S(1)}, u32[]{:S(2)}, u32[]{:S(2)}) collective-permute-start(bf16[6,192,128]{2,1,0:T(8,128)(2,1)S(1)} %copy-done.14), channel_id=1, source_target_pairs={{0,1},{1,0},{2,3},{3,2},{4,5},{5,4},{6,7},{7,6},{8,9},{9,8},{10,11... | collective-permute-start | bytes 884744 | tf_op jit(solution)/shard_map/ppermute | solution.py:441
  144.8 7.8 %collective-permute-start.40 = (bf16[48,768]{1,0:T(8,128)(2,1)S(1)}, bf16[48,768]{1,0:T(8,128)(2,1)S(1)}, u32[]{:S(2)}, u32[]{:S(2)}) collective-permute-start(bf16[48,768]{1,0:T(8,128)(2,1)S(1)} %fusion.14), channel_id=1, source_target_pairs={{0,12},{2,14},{4,0},{6,2},{8,4},{10,6},{12,8},{14,10},{1,13},{3,15... | collective-permute-start | bytes 221192 | tf_op jit(solution)/shard_map/ppermute | solution.py:448
  144.9 8.4 %collective-permute-start.39 = (bf16[48,768]{1,0:T(8,128)(2,1)S(1)}, bf16[48,768]{1,0:T(8,128)(2,1)S(1)}, u32[]{:S(2)}, u32[]{:S(2)}) collective-permute-start(bf16[48,768]{1,0:T(8,128)(2,1)S(1)} %fusion.14), channel_id=1, source_target_pairs={{0,8},{2,10},{4,12},{6,14},{8,0},{10,2},{12,4},{14,6},{1,9},{3,11}... | collective-permute-start | bytes 221192 | tf_op jit(solution)/shard_map/ppermute | solution.py:448
  146.1 7.2 %collective-permute-start.38 = (bf16[48,768]{1,0:T(8,128)(2,1)S(1)}, bf16[48,768]{1,0:T(8,128)(2,1)S(1)}, u32[]{:S(2)}, u32[]{:S(2)}) collective-permute-start(bf16[48,768]{1,0:T(8,128)(2,1)S(1)} %fusion.14), channel_id=1, source_target_pairs={{0,4},{2,6},{4,8},{6,10},{8,12},{10,14},{12,0},{14,2},{1,5},{3,7},... | collective-permute-start | bytes 221192 | tf_op jit(solution)/shard_map/ppermute | solution.py:448
  148.1 8.2 %collective-permute-start.37 = (bf16[192,768]{1,0:T(8,128)(2,1)S(1)}, bf16[192,768]{1,0:T(8,128)(2,1)S(1)}, u32[]{:S(2)}, u32[]{:S(2)}) collective-permute-start(bf16[192,768]{1,0:T(8,128)(2,1)S(1)} %bitcast.151), channel_id=1, source_target_pairs={{0,16},{16,0},{1,17},{17,1},{2,18},{18,2},{3,19},{19,3},{4,20},{20... | collective-permute-start | bytes 884744 | tf_op jit(solution)/shard_map/ppermute | solution.py:441
  149.6 6.6 %collective-permute-start.36 = (bf16[384,768]{1,0:T(8,128)(2,1)S(1)}, bf16[384,768]{1,0:T(8,128)(2,1)S(1)}, u32[]{:S(2)}, u32[]{:S(2)}) collective-permute-start(bf16[384,768]{1,0:T(8,128)(2,1)S(1)} %pad_maximum_fusion.2), channel_id=1, source_target_pairs={{0,2},{2,0},{4,6},{6,4},{8,10},{10,8},{12,14},{14,12},{1,3},{3,1},... | collective-permute-start | bytes 1769480 | tf_op jit(solution)/shard_map/ppermute | solution.py:441
  156.3 7.6 %collective-permute-start.43 = (bf16[192,768]{1,0:T(8,128)(2,1)S(1)}, bf16[192,768]{1,0:T(8,128)(2,1)S(1)}, u32[]{:S(2)}, u32[]{:S(2)}) collective-permute-start(bf16[192,768]{1,0:T(8,128)(2,1)S(1)} %bitcast.154), channel_id=1, source_target_pairs={{0,16},{16,0},{1,17},{17,1},{2,18},{18,2},{3,19},{19,3},{4,20},{20... | collective-permute-start | bytes 884744 | tf_op jit(solution)/shard_map/ppermute | solution.py:441
  157.8 6.0 %collective-permute-start.42 = (bf16[384,768]{1,0:T(8,128)(2,1)S(1)}, bf16[384,768]{1,0:T(8,128)(2,1)S(1)}, u32[]{:S(2)}, u32[]{:S(2)}) collective-permute-start(bf16[384,768]{1,0:T(8,128)(2,1)S(1)} %pad_maximum_fusion.3), channel_id=1, source_target_pairs={{0,2},{2,0},{4,6},{6,4},{8,10},{10,8},{12,14},{14,12},{1,3},{3,1},... | collective-permute-start | bytes 1769480 | tf_op jit(solution)/shard_map/ppermute | solution.py:441
  163.9 4.2 %collective-permute-start.44 = (bf16[192,768]{1,0:T(8,128)(2,1)S(1)}, bf16[192,768]{1,0:T(8,128)(2,1)S(1)}, u32[]{:S(2)}, u32[]{:S(2)}) collective-permute-start(bf16[192,768]{1,0:T(8,128)(2,1)S(1)} %collective-permute-done.43.other), channel_id=1, source_target_pairs={{0,2},{2,0},{4,6},{6,4},{8,10},{10,8},{12,14},{14,12},{1,3},{3,1},... | collective-permute-start | bytes 884744 | tf_op jit(solution)/shard_map/ppermute | solution.py:441
  (33 other events, 235.7 us)

commit v2 on v1

--- a/solution.py
+++ b/solution.py
@@ -13,6 +13,7 @@
 SEG = 8
 TILE = 4
 SIZES = (2, 2, 2, 2)
+SENT = (4, 4)
 BF = jnp.bfloat16
 F32 = jnp.float32
 VMEM_LIMIT = 56 << 20
@@ -174,8 +175,8 @@
     )
 
 
-def slot_shapes(channels):
-    return [jax.ShapeDtypeStruct((CAP * size, channels, BLOCK), BF) for size in SIZES]
+def slot_shapes(channels, sizes):
+    return [jax.ShapeDtypeStruct((CAP * size, channels, BLOCK), BF) for size in sizes]
 
 
 def dense_part(images, halo, dw_kernel, ln_gain, w_expand, w_reduce, place, table, counts):
@@ -184,7 +185,7 @@
     hidden = w_expand.shape[1]
     args = [images, halo, dw_kernel, ln_gain[None], w_expand, w_reduce]
     args += dense_constants(width, channels)
-    slots = slot_shapes(channels)
+    slots = slot_shapes(channels, SENT)
     return pl.pallas_call(
         dense_kernel,
         grid=(rows // TILE,),
@@ -238,8 +239,8 @@
     copy_slots(place, table, blocks, slots)
 
 
-def route(blocks, labels, place):
-    slots = slot_shapes(blocks.shape[1])
+def route(blocks, labels, place, experts):
+    slots = slot_shapes(blocks.shape[1], (experts,))
     return pl.pallas_call(
         route_kernel,
         in_specs=[SM, SM, VM],
@@ -254,26 +255,23 @@
     )(labels, place, blocks)
 
 
-def expert_tokens(x, g, w_in_t, w_out_t, w_out):
-    pre = dot(w_in_t, x)
+def expert_tokens(x, g, w_in, w_out):
+    pre = dot(x.T, w_in)
     share = 0.5 + 0.5 * lax.erf(pre * 0.7071067811865476)
     hidden = (pre * share).astype(BF)
     slope = share + pre * (jnp.exp(pre * pre * -0.5) * 0.3989422804014327)
-    scaled = (dot(w_out_t, g) * slope).astype(BF)
-    out = dot(w_out, hidden).astype(BF)
-    return out, dot(x, scaled, ((1,), (1,))), dot(g, hidden, ((1,), (1,)))
-
-
-def expert_blocks(count, block, store, grads, w_in, w_out, w_in_t, w_out_t, carried):
-    w_in_t[...] = w_in[...].T
-    w_out_t[...] = w_out[...].T
-
+    scaled = (dot(g.T, w_out) * slope).astype(BF)
+    out = dot(w_out, hidden, ((1,), (1,))).astype(BF)
+    return out, dot(x, scaled), dot(g, hidden)
+
+
+def expert_blocks(count, block, store, grads, w_in, w_out, carried):
     def load(j):
         return [jnp.where(j < count, part, jnp.zeros_like(part)) for part in block(j)]
 
     both = [load(0), load(1)]
     x, g = [jnp.concatenate([a, b], axis=1) for a, b in zip(*both)]
-    out, grad_in, grad_out = expert_tokens(x, g, w_in_t[...], w_out_t[...], w_out[...])
+    out, grad_in, grad_out = expert_tokens(x, g, w_in[...], w_out[...])
     if carried is not None:
         grad_in, grad_out = grad_in + carried[0], grad_out + carried[1]
     grads[0][...] = grad_in
@@ -286,13 +284,13 @@
     @pl.when(count > 2)
     def _():
         x, g = block(2)
-        out, grad_in, grad_out = expert_tokens(x, g, w_in_t[...], w_out_t[...], w_out[...])
+        out, grad_in, grad_out = expert_tokens(x, g, w_in[...], w_out[...])
         grads[0][...] += grad_in
         grads[1][...] += grad_out
         store(2, x, out)
 
 
-def own_kernel(place, table, counts, dense_in, cots, w_in, w_out, dense, grad_in, grad_out, *scratch):
+def own_kernel(place, table, counts, dense_in, cots, w_in, w_out, dense, grad_in, grad_out):
     @pl.when(pl.program_id(0) == 0)
     def _():
         dense[...] = dense_in[...]
@@ -309,7 +307,7 @@
         dense[b // 2, :, here] = (x.astype(F32) + out.astype(F32)).astype(BF)
 
     grads = (grad_in.at[0], grad_out.at[0])
-    expert_blocks(counts[e], block, store, grads, w_in.at[0], w_out.at[0], *scratch, None)
+    expert_blocks(counts[e], block, store, grads, w_in.at[0], w_out.at[0], None)
 
 
 def own_part(place, table, counts, dense, cots, exp_in, exp_out):
@@ -322,7 +320,6 @@
         out_specs=[VM, one, one],
         out_shape=[jax.ShapeDtypeStruct(dense.shape, BF)]
         + [jax.ShapeDtypeStruct(exp_in.shape, F32)] * 2,
-        scratch_shapes=[pltpu.VMEM((hidden, channels), BF)] * 2,
         compiler_params=params(),
         cost_estimate=cost(64 << 30),
         name="own_blocks",
@@ -331,7 +328,7 @@
 
 def far_kernel(
     offset, place, theirs, xs, gs, w_in, w_out, own_in, own_out,
-    back, keep, send, w_in_t, w_out_t, grad_in, grad_out,
+    back, keep, send, grad_in, grad_out,
 ):
     k = pl.program_id(0)
 
@@ -343,7 +340,7 @@
 
     count = theirs[place[0] + offset + k]
     expert_blocks(
-        count, block, store, (grad_in, grad_out), w_in.at[0], w_out.at[0], w_in_t, w_out_t,
+        count, block, store, (grad_in, grad_out), w_in.at[0], w_out.at[0],
         (own_in[0], own_out[0]),
     )
     first = place[2] == 0
@@ -356,19 +353,25 @@
     channels, hidden = exp_in.shape[1:]
     one = pl.BlockSpec((1, channels, hidden), lambda i, place: (offset + i, 0, 0))
     half = size // 2
+
+    def slots(array):
+        sent = array.shape[0] // CAP
+        return pl.BlockSpec(
+            (CAP * size, channels, BLOCK), lambda i, place: (offset % sent // size, 0, 0)
+        )
+
     turned = pl.BlockSpec((1, channels, hidden), lambda i, place: ((i + place[3] * half) % size, 0, 0))
     return pl.pallas_call(
         functools.partial(far_kernel, offset),
         grid_spec=pltpu.PrefetchScalarGridSpec(
             num_scalar_prefetch=1,
             grid=(size,),
-            in_specs=[SM, VM, VM, one, one, one, one],
+            in_specs=[SM, slots(xs), slots(gs), one, one, one, one],
             out_specs=[VM, turned, turned],
-            scratch_shapes=[pltpu.VMEM((hidden, channels), BF)] * 2
-            + [pltpu.VMEM((channels, hidden), F32)] * 2,
+            scratch_shapes=[pltpu.VMEM((channels, hidden), F32)] * 2,
         ),
         out_shape=[
-            jax.ShapeDtypeStruct(xs.shape, BF),
+            jax.ShapeDtypeStruct((CAP * size, channels, BLOCK), BF),
             jax.ShapeDtypeStruct((size, channels, hidden), BF),
             jax.ShapeDtypeStruct((size, channels, hidden), BF),
         ],
@@ -582,43 +585,46 @@
     exp_out = jnp.swapaxes(exp_out, 1, 2)
     edge = lax.dynamic_slice_in_dim(picture, jnp.where(lat == 0, rows - 3, 0), 3, axis=0)
     halo = exchange(edge, "lat", 1)
-    table, counts, *cot_out = route(cots, labels.reshape(-1), place)
+    table, counts, cot_out = route(cots, labels.reshape(-1), place, experts)
     theirs = exchange(counts, "exp", 1)
-    cot_in = [exchange(c, "exp", 1) for c in cot_out]
+    cot_in = exchange(cot_out, "exp", 1)
 
     dense, *act_out = dense_part(
         picture, halo, dw_kernel, ln_gain, w_expand, w_reduce.T, place, table, counts
     )
-    ahead = min(2, parts)
-    act_out = [after(a, *cot_in) for a in act_out[:ahead]] + act_out[ahead:]
-    act_in = [exchange(a, "exp", 1) for a in act_out[:ahead]]
-
+    act_in = [exchange(after(act_out[0], cot_in), "exp", 1)]
     dense, *own = own_part(place, table, counts, dense, cots, exp_in, exp_out)
-    act_in += [exchange(after(a, *act_in[:ahead], dense), "exp", 1) for a in act_out[ahead:]]
-    backs, grads, rounds = [], None, Rounds()
+    for act in act_out[1:]:
+        act_in.append(exchange(after(act, act_in[-1], dense), "exp", 1))
     offsets = [sum(SIZES[:part]) for part in range(parts)]
+    source = [next(n for n in range(len(SENT)) if o < sum(SENT[: n + 1])) for o in offsets]
+    backs, grads, rounds, done = [], None, Rounds(), 0
     for part in range(parts):
         back, keep, send = far_part(
-            offsets[part], SIZES[part], place, theirs, act_in[part], cot_in[part], exp_in, exp_out, *own
+            offsets[part], SIZES[part], place, theirs, act_in[source[part]], cot_in,
+            exp_in, exp_out, *own
         )
-        if part + 1 < parts:
-            send, act_in[part + 1] = rounds.arrive(send, act_in[part + 1])
+        if part + 1 < parts and source[part + 1] != source[part]:
+            coming = source[part + 1]
+            send, act_in[coming] = rounds.arrive(send, act_in[coming])
         else:
             (send,) = rounds.arrive(send)
         rounds.start(reduce_chain(keep, send))
         rounds.depart()
-        backs.append(exchange(after(back, *act_in[ahead:], send), "exp", 1))
-    for part in range(parts):
-        (backs[part],) = rounds.arrive(backs[part])
+        backs.append(exchange(after(back, act_in[-1], send), "exp", 1))
+    output, turn = None, 0
+    while rounds.live:
+        needed = [backs[turn]] if turn < parts else [output] if turn == parts else []
+        arrived = rounds.arrive(*needed, *(grads or []))
+        if turn < parts:
+            backs[turn] = arrived[0]
+        elif turn == parts:
+            output = arrived[0]
+        grads = arrived[len(needed) :] or None
         rounds.depart()
-    output = combine(dense, backs, table, counts, place, experts)
-    done = 0
-    while rounds.live:
-        if done:
-            grads = list(rounds.arrive(*grads))
-        else:
-            (output,) = rounds.arrive(output)
-        rounds.depart()
+        if turn == parts - 1:
+            output = combine(dense, backs, table, counts, place, experts)
+        turn += 1
         while done < len(rounds.results):
             grads = widen_group(
                 offsets[done], SIZES[done], place, rounds.results[done], grads, experts, channels

time: 172 us -> 170 us (0.988)
  starting transfers between devices: 49.4 us -> 39.7 us
  waiting for transfers between devices: 36.7 us -> 41.2 us
  Pallas kernels: 75.2 us -> 77.7 us
    ppermute x30 -> x25, starting transfers between devices: 26 us -> 17.3 us  [exchange(): return lax.ppermute(value, axis, [(i, i ^ flip) for i in range(count)])]
    ppermute x30 -> x25, waiting for transfers between devices: 8.71 us -> 13.4 us  [exchange(): return lax.ppermute(value, axis, [(i, i ^ flip) for i in range(count)])]
  transfers between devices with their start and end apart: 45 -> 40, of which waited for: 10 -> 11; matrix products, arithmetic and copies ran while one was open for 3% -> 3% of each run, Pallas kernels for 42% -> 44%
where the time goes in v2:
time: 170 us
  Pallas kernels  77.7 us (46%)
  waiting for transfers between devices  41.2 us (24%)
  starting transfers between devices  39.7 us (23%)
  local copies, waits for them, and re-layouts  8.36 us (5%)
    ppermute x15, waiting for transfers between devices, shift(): return lax.ppermute(value, 'dp', perm)  27.8 us
    pallas_call x4, Pallas kernels, far_part(): pl.pallas_call(functools.partial(far_kernel, offset), grid_spec=pltpu.Pre...  23 us
    pallas_call x1, Pallas kernels, dense_part(): pl.pallas_call(dense_kernel, grid=(rows // TILE,), in_specs=[SM] * 3 + [V...  22.4 us
    ppermute x15, starting transfers between devices, shift(): return lax.ppermute(value, 'dp', perm)  22.4 us
    ppermute x25, starting transfers between devices, exchange(): return lax.ppermute(value, axis, [(i, i ^ flip) for i in range(count)])  17.3 us
    pallas_call x1, Pallas kernels, own_part(): pl.pallas_call(own_kernel, grid=(experts,), in_specs=[SM, SM, SM, VM, VM,...  14.6 us
    ppermute x25, waiting for transfers between devices, exchange(): return lax.ppermute(value, axis, [(i, i ^ flip) for i in range(count)])  13.4 us
    pallas_call x4, Pallas kernels, widen_group(): pl.pallas_call(functools.partial(widen_kernel, pieces), grid=(1,), in_spe...  11.3 us
  transfers between devices with their start and end apart: 40, of which 11 were waited for; matrix products, arithmetic and copies ran while one was open for 3% of the time, Pallas kernels for 44%

profile of v2, /device:TPU:0, one launch (start us, length us, event | category | flops | bytes accessed | tf_op | source)
XLA Modules:
  0.0 169.6 jit_solution(4058953113465622006)
XLA Ops:
  0.6 1.0 dynamic-slice_bitcast_fusion
  1.6 3.0 %collective-permute-start.1 = (bf16[3,192,256]{2,1,0:T(8,128)(2,1)S(1)}, bf16[3,192,256]{2,1,0:T(8,128)(2,1)S(1)}, u32[]{:S(2)}, u32[]{:S(2)}) collective-permute-start(bf16[3,192,256]{2,1,0:T(8,128)(2,1)S(1)} %dynamic-slice_bitcast_fusion), channel_id=1, source_target_pairs={{0,16},{16,0},{1,17},{17,1},{2,18},{18,2},{3,19},{19,3},{4,20},{20... | collective-permute-start | bytes 884744 | tf_op jit(solution)/shard_map/ppermute | solution.py:444
  4.6 0.8 copy.23
  6.6 3.3 %route_blocks.1 = (s32[48]{0:T(128)}, s32[16]{0:T(128)}, bf16[24,192,128]{2,1,0:T(8,128)(2,1)}) custom-call(s32[32]{0:T(128)} %reshape.104.labels, s32[5]{0:T(128)} %stack.83.place, bf16[16,192,256]{2,1,0:T(8,128)(2,1)} %bitcast.143), custom_call_target="tpu_custom_call" | custom-call | tf_op jit(solution)/shard_map/route_blocks/pallas_call | solution.py:244
  9.9 1.6 collective-permute-start
  12.0 0.7 copy-done.22
  12.7 22.4 %dense_block.1 = (bf16[16,192,256]{2,1,0:T(8,128)(2,1)}, bf16[12,192,128]{2,1,0:T(8,128)(2,1)}, bf16[12,192,128]{2,1,0:T(8,128)(2,1)}) custom-call(s32[5]{0:T(128)} %stack.83.place, s32[48]{0:T(128)} %get-tuple-element.85.table.tables, s32[16]{0:T(128)} %get-tuple-element.84.counts.tallies, bf16[16,192,256]{2,1,0:T(8,128)(2,1)} %bitcast.172, ...), custom_call_target="tpu_custom_call" | custom-call | flops 68719476736 | bytes 1048576 | tf_op jit(solution)/shard_map/dense_block/pallas_call | solution.py:189
  35.1 3.7 %collective-permute-done.2.gs = bf16[24,192,128]{2,1,0:T(8,128)(2,1)S(1)} collective-permute-done((bf16[24,192,128]{2,1,0:T(8,128)(2,1)}, bf16[24,192,128]{2,1,0:T(8,128)(2,1)S(1)}, u32[]{:S(2)}, u32[]{:S(2)}) %collective-permute-start.2) | collective-permute-done | bytes 1179680 | tf_op jit(solution)/shard_map/ppermute | solution.py:444
  39.3 14.6 %own_blocks.1 = (bf16[16,192,256]{2,1,0:T(8,128)(2,1)}, f32[8,192,768]{2,1,0:T(8,128)}, f32[8,192,768]{2,1,0:T(8,128)}) custom-call(s32[5]{0:T(128)} %stack.83.place, s32[48]{0:T(128)} %get-tuple-element.85.table.tables, s32[16]{0:T(128)} %get-tuple-element.84.counts.tallies, bf16[16,192,256]{2,1,0:T(8,128)(2,1)} %get-tuple-element.89.dense_in, ...), custom_call_target="tpu_custom_call" | custom-call | flops 68719476736 | bytes 1048576 | tf_op jit(solution)/shard_map/own_blocks/pallas_call | solution.py:316
  54.8 6.8 %far_blocks.4 = (bf16[6,192,128]{2,1,0:T(8,128)(2,1)}, bf16[2,192,768]{2,1,0:T(8,128)(2,1)}, bf16[2,192,768]{2,1,0:T(8,128)(2,1)}) custom-call(s32[5]{0:T(128)} %stack.83.place, s32[16]{0:T(128)} %copy-done.29, bf16[12,192,128]{2,1,0:T(8,128)(2,1)} %copy-done.16, bf16[24,192,128]{2,1,0:T(8,128)(2,1)} %copy-done.11, bf16[8,192,768]{2,1,0:T(8,128)(2,1)} %w_in.9, ...), custom_call_target="tpu_custom_call" | custom-call | flops 68719476736 | bytes 1048576 | tf_op jit(solution)/shard_map/far_blocks/pallas_call | solution.py:364
  61.7 5.4 %far_blocks.5 = (bf16[6,192,128]{2,1,0:T(8,128)(2,1)}, bf16[2,192,768]{2,1,0:T(8,128)(2,1)}, bf16[2,192,768]{2,1,0:T(8,128)(2,1)}) custom-call(s32[5]{0:T(128)} %stack.83.place, s32[16]{0:T(128)} %copy-done.29, bf16[12,192,128]{2,1,0:T(8,128)(2,1)} %copy-done.16, bf16[24,192,128]{2,1,0:T(8,128)(2,1)} %copy-done.11, bf16[8,192,768]{2,1,0:T(8,128)(2,1)} %w_in.9, ...), custom_call_target="tpu_custom_call" | custom-call | flops 68719476736 | bytes 1048576 | tf_op jit(solution)/shard_map/far_blocks/pallas_call | solution.py:364
  68.4 5.3 %far_blocks.6 = (bf16[6,192,128]{2,1,0:T(8,128)(2,1)}, bf16[2,192,768]{2,1,0:T(8,128)(2,1)}, bf16[2,192,768]{2,1,0:T(8,128)(2,1)}) custom-call(s32[5]{0:T(128)} %stack.83.place, s32[16]{0:T(128)} %copy-done.29, bf16[12,192,128]{2,1,0:T(8,128)(2,1)} %copy-done.13, bf16[24,192,128]{2,1,0:T(8,128)(2,1)} %copy-done.11, bf16[8,192,768]{2,1,0:T(8,128)(2,1)} %w_in.9, ...), custom_call_target="tpu_custom_call" | custom-call | flops 68719476736 | bytes 1048576 | tf_op jit(solution)/shard_map/far_blocks/pallas_call | solution.py:364
  73.7 2.8 %collective-permute-done.7 = bf16[192,768]{1,0:T(8,128)(2,1)S(1)} collective-permute-done((bf16[192,768]{1,0:T(8,128)(2,1)S(1)}, bf16[192,768]{1,0:T(8,128)(2,1)S(1)}, u32[]{:S(2)}, u32[]{:S(2)}) %collective-permute-start.7) | collective-permute-done | bytes 294944 | tf_op jit(solution)/shard_map/ppermute | solution.py:444
  76.7 3.7 %collective-permute-start.12 = (bf16[48,768]{1,0:T(8,128)(2,1)S(1)}, bf16[48,768]{1,0:T(8,128)(2,1)S(1)}, u32[]{:S(2)}, u32[]{:S(2)}) collective-permute-start(bf16[48,768]{1,0:T(8,128)(2,1)S(1)} %get-tuple-element.180), channel_id=1, source_target_pairs={{0,12},{2,14},{4,0},{6,2},{8,4},{10,6},{12,8},{14,10},{1,13},{3,15... | collective-permute-start | bytes 221192 | tf_op jit(solution)/shard_map/ppermute | solution.py:451
  80.4 1.0 collective-permute-start.10
  82.1 5.5 %far_blocks.7 = (bf16[6,192,128]{2,1,0:T(8,128)(2,1)}, bf16[2,192,768]{2,1,0:T(8,128)(2,1)}, bf16[2,192,768]{2,1,0:T(8,128)(2,1)}) custom-call(s32[5]{0:T(128)} %stack.83.place, s32[16]{0:T(128)} %copy-done.29, bf16[12,192,128]{2,1,0:T(8,128)(2,1)} %copy-done.13, bf16[24,192,128]{2,1,0:T(8,128)(2,1)} %copy-done.11, bf16[8,192,768]{2,1,0:T(8,128)(2,1)} %w_in.9, ...), custom_call_target="tpu_custom_call" | custom-call | flops 68719476736 | bytes 1048576 | tf_op jit(solution)/shard_map/far_blocks/pallas_call | solution.py:364
  88.0 0.7 collective-permute-done.9
  88.9 0.9 collective-permute-start.14
  89.9 2.9 %collective-permute-start.17 = (bf16[96,768]{1,0:T(8,128)(2,1)S(1)}, bf16[96,768]{1,0:T(8,128)(2,1)S(1)}, u32[]{:S(2)}, u32[]{:S(2)}) collective-permute-start(bf16[96,768]{1,0:T(8,128)(2,1)S(1)} %get-tuple-element.189), channel_id=1, source_target_pairs={{0,12},{2,14},{4,0},{6,2},{8,4},{10,6},{12,8},{14,10},{1,13},{3,15... | collective-permute-start | bytes 442376 | tf_op jit(solution)/shard_map/ppermute | solution.py:451
  92.8 1.1 collective-permute-start.16
  93.9 3.0 %collective-permute-done.18.refs_0_ = bf16[6,192,128]{2,1,0:T(8,128)(2,1)S(1)} collective-permute-done((bf16[6,192,128]{2,1,0:T(8,128)(2,1)S(1)}, bf16[6,192,128]{2,1,0:T(8,128)(2,1)S(1)}, u32[]{:S(2)}, u32[]{:S(2)}) %collective-permute-start.18) | collective-permute-done | bytes 294944 | tf_op jit(solution)/shard_map/ppermute | solution.py:444
  96.9 2.5 %collective-permute-start.15 = (bf16[96,768]{1,0:T(8,128)(2,1)S(1)}, bf16[96,768]{1,0:T(8,128)(2,1)S(1)}, u32[]{:S(2)}, u32[]{:S(2)}) collective-permute-start(bf16[96,768]{1,0:T(8,128)(2,1)S(1)} %get-tuple-element.191), channel_id=1, source_target_pairs={{0,4},{2,6},{4,8},{6,10},{8,12},{10,14},{12,0},{14,2},{1,5},{3,7},... | collective-permute-start | bytes 442376 | tf_op jit(solution)/shard_map/ppermute | solution.py:451
  99.7 7.9 %collective-permute-done.16 = bf16[96,768]{1,0:T(8,128)(2,1)S(1)} collective-permute-done((bf16[96,768]{1,0:T(8,128)(2,1)S(1)}, bf16[96,768]{1,0:T(8,128)(2,1)S(1)}, u32[]{:S(2)}, u32[]{:S(2)}) %collective-permute-start.16) | collective-permute-done | bytes 147488 | tf_op jit(solution)/shard_map/ppermute | solution.py:451
  108.0 1.3 collective-permute-start.20
  109.7 1.5 collective-permute-start.22
  111.2 2.5 %collective-permute-start.21 = (bf16[96,768]{1,0:T(8,128)(2,1)S(1)}, bf16[96,768]{1,0:T(8,128)(2,1)S(1)}, u32[]{:S(2)}, u32[]{:S(2)}) collective-permute-start(bf16[96,768]{1,0:T(8,128)(2,1)S(1)} %get-tuple-element.188), channel_id=1, source_target_pairs={{0,4},{2,6},{4,8},{6,10},{8,12},{10,14},{12,0},{14,2},{1,5},{3,7},... | collective-permute-start | bytes 442376 | tf_op jit(solution)/shard_map/ppermute | solution.py:451
  113.7 2.5 %collective-permute-done.23 = bf16[96,768]{1,0:T(8,128)(2,1)S(1)} collective-permute-done((bf16[96,768]{1,0:T(8,128)(2,1)S(1)}, bf16[96,768]{1,0:T(8,128)(2,1)S(1)}, u32[]{:S(2)}, u32[]{:S(2)}) %collective-permute-start.23) | collective-permute-done | bytes 147488 | tf_op jit(solution)/shard_map/ppermute | solution.py:451
  116.2 1.2 collective-permute-start.30
  117.5 7.3 %collective-permute-done.22 = bf16[96,768]{1,0:T(8,128)(2,1)S(1)} collective-permute-done((bf16[96,768]{1,0:T(8,128)(2,1)S(1)}, bf16[96,768]{1,0:T(8,128)(2,1)S(1)}, u32[]{:S(2)}, u32[]{:S(2)}) %collective-permute-start.22) | collective-permute-done | bytes 147488 | tf_op jit(solution)/shard_map/ppermute | solution.py:451
  126.2 1.8 %collective-permute-start.28 = (bf16[96,768]{1,0:T(8,128)(2,1)S(1)}, bf16[96,768]{1,0:T(8,128)(2,1)S(1)}, u32[]{:S(2)}, u32[]{:S(2)}) collective-permute-start(bf16[96,768]{1,0:T(8,128)(2,1)S(1)} %get-tuple-element.184), channel_id=1, source_target_pairs={{0,8},{2,10},{4,12},{6,14},{8,0},{10,2},{12,4},{14,6},{1,9},{3,11}... | collective-permute-start | bytes 442376 | tf_op jit(solution)/shard_map/ppermute | solution.py:451
  128.0 1.9 %collective-permute-start.27 = (bf16[96,768]{1,0:T(8,128)(2,1)S(1)}, bf16[96,768]{1,0:T(8,128)(2,1)S(1)}, u32[]{:S(2)}, u32[]{:S(2)}) collective-permute-start(bf16[96,768]{1,0:T(8,128)(2,1)S(1)} %get-tuple-element.185), channel_id=1, source_target_pairs={{0,4},{2,6},{4,8},{6,10},{8,12},{10,14},{12,0},{14,2},{1,5},{3,7},... | collective-permute-start | bytes 442376 | tf_op jit(solution)/shard_map/ppermute | solution.py:451
  130.0 2.6 %collective-permute-done.29 = bf16[96,768]{1,0:T(8,128)(2,1)S(1)} collective-permute-done((bf16[96,768]{1,0:T(8,128)(2,1)S(1)}, bf16[96,768]{1,0:T(8,128)(2,1)S(1)}, u32[]{:S(2)}, u32[]{:S(2)}) %collective-permute-start.29) | collective-permute-done | bytes 147488 | tf_op jit(solution)/shard_map/ppermute | solution.py:451
  132.6 1.6 collective-permute-start.36
  134.2 7.4 %collective-permute-done.28 = bf16[96,768]{1,0:T(8,128)(2,1)S(1)} collective-permute-done((bf16[96,768]{1,0:T(8,128)(2,1)S(1)}, bf16[96,768]{1,0:T(8,128)(2,1)S(1)}, u32[]{:S(2)}, u32[]{:S(2)}) %collective-permute-start.28) | collective-permute-done | bytes 147488 | tf_op jit(solution)/shard_map/ppermute | solution.py:451
  141.8 1.3 collective-permute-start.34
  143.1 1.9 %collective-permute-start.33 = (bf16[48,768]{1,0:T(8,128)(2,1)S(1)}, bf16[48,768]{1,0:T(8,128)(2,1)S(1)}, u32[]{:S(2)}, u32[]{:S(2)}) collective-permute-start(bf16[48,768]{1,0:T(8,128)(2,1)S(1)} %fusion.14), channel_id=1, source_target_pairs={{0,4},{2,6},{4,8},{6,10},{8,12},{10,14},{12,0},{14,2},{1,5},{3,7},... | collective-permute-start | bytes 221192 | tf_op jit(solution)/shard_map/ppermute | solution.py:451
  145.1 1.6 collective-permute-start.32
  146.8 0.9 fusion.26
  147.7 2.8 %widen_gradients.4 = (f32[8,192,768]{2,1,0:T(8,128)}, f32[8,192,768]{2,1,0:T(8,128)}) custom-call(s32[5]{0:T(128)} %stack.83.place, bf16[192,768]{1,0:T(8,128)(2,1)} %bitcast.147, bf16[192,768]{1,0:T(8,128)(2,1)} %copy-done.2, bf16[192,768]{1,0:T(8,128)(2,1)} %copy-done.23, bf16[192,768]{1,0:T(8,128)(2,1)} %get-tuple-element.170.other2), custom_call_target="tpu_custom_call" | custom-call | flops 68719476736 | bytes 1048576 | tf_op jit(solution)/shard_map/widen_gradients/pallas_call | solution.py:560
  150.6 2.7 %collective-permute-done.32.other = bf16[192,768]{1,0:T(8,128)(2,1)S(1)} collective-permute-done((bf16[192,768]{1,0:T(8,128)(2,1)S(1)}, bf16[192,768]{1,0:T(8,128)(2,1)S(1)}, u32[]{:S(2)}, u32[]{:S(2)}) %collective-permute-start.32) | collective-permute-done | bytes 294944 | tf_op jit(solution)/shard_map/ppermute | solution.py:444
  153.3 1.6 collective-permute-start.38
  155.0 0.8 fusion.25
  155.8 3.1 %combine_blocks.1 = bf16[16,192,256]{2,1,0:T(8,128)(2,1)} custom-call(s32[48]{0:T(128)} %get-tuple-element.85.table.tables, s32[16]{0:T(128)} %get-tuple-element.84.counts.tallies, s32[5]{0:T(128)} %stack.83.place, bf16[16,192,256]{2,1,0:T(8,128)(2,1)} %get-tuple-element.96.dense_in, ...), custom_call_target="tpu_custom_call", output_to_operand_aliasing={{}: (3, {})} | custom-call | flops 68719476736 | bytes 1048576 | tf_op jit(solution)/shard_map/combine_blocks/pallas_call | solution.py:425
  158.9 2.8 %widen_gradients.5 = (f32[8,192,768]{2,1,0:T(8,128)}, f32[8,192,768]{2,1,0:T(8,128)}) custom-call(s32[5]{0:T(128)} %stack.83.place, bf16[192,768]{1,0:T(8,128)(2,1)} %bitcast.150, bf16[192,768]{1,0:T(8,128)(2,1)} %copy-done.9, bf16[192,768]{1,0:T(8,128)(2,1)} %get-tuple-element.169.mine2, ...), custom_call_target="tpu_custom_call", output_to_operand_aliasing={{0}: (5, {}), {1}: (6, {})} | custom-call | flops 68719476736 | bytes 1048576 | tf_op jit(solution)/shard_map/widen_gradients/pallas_call | solution.py:560
  162.3 0.9 fusion.24
  163.2 2.8 %widen_gradients.6 = (f32[8,192,768]{2,1,0:T(8,128)}, f32[8,192,768]{2,1,0:T(8,128)}) custom-call(s32[5]{0:T(128)} %stack.83.place, bf16[192,768]{1,0:T(8,128)(2,1)} %bitcast.153, bf16[192,768]{1,0:T(8,128)(2,1)} %copy-done.10, bf16[192,768]{1,0:T(8,128)(2,1)} %get-tuple-element.167.mine2, ...), custom_call_target="tpu_custom_call", output_to_operand_aliasing={{0}: (5, {}), {1}: (6, {})} | custom-call | flops 68719476736 | bytes 1048576 | tf_op jit(solution)/shard_map/widen_gradients/pallas_call | solution.py:560
  166.0 0.7 copy-done.28
  166.7 2.8 %widen_gradients.7 = (f32[8,192,768]{2,1,0:T(8,128)}, f32[8,192,768]{2,1,0:T(8,128)}) custom-call(s32[5]{0:T(128)} %stack.83.place, bf16[192,768]{1,0:T(8,128)(2,1)} %bitcast.156, bf16[192,768]{1,0:T(8,128)(2,1)} %copy-done.27, bf16[192,768]{1,0:T(8,128)(2,1)} %get-tuple-element.166.mine2, ...), custom_call_target="tpu_custom_call", output_to_operand_aliasing={{0}: (5, {}), {1}: (6, {})} | custom-call | flops 68719476736 | bytes 1048576 | tf_op jit(solution)/shard_map/widen_gradients/pallas_call | solution.py:560
  (147 shorter events, 9.2 us)
Async XLA Ops:
  1.6 10.3 %collective-permute-start.1 = (bf16[3,192,256]{2,1,0:T(8,128)(2,1)S(1)}, bf16[3,192,256]{2,1,0:T(8,128)(2,1)S(1)}, u32[]{:S(2)}, u32[]{:S(2)}) collective-permute-start(bf16[3,192,256]{2,1,0:T(8,128)(2,1)S(1)} %dynamic-slice_bitcast_fusion), channel_id=1, source_target_pairs={{0,16},{16,0},{1,17},{17,1},{2,18},{18,2},{3,19},{19,3},{4,20},{20... | collective-permute-start | bytes 884744 | tf_op jit(solution)/shard_map/ppermute | solution.py:444
  9.9 44.4 %collective-permute-start = (s32[16]{0:T(128)}, s32[16]{0:T(128)S(1)}, u32[]{:S(2)}, u32[]{:S(2)}) collective-permute-start(s32[16]{0:T(128)} %get-tuple-element.84.counts.tallies), channel_id=1, source_target_pairs={{0,1},{1,0},{2,3},{3,2},{4,5},{5,4},{6,7},{7,6},{8,9},{9,8},{10,11... | collective-permute-start | bytes 200 | tf_op jit(solution)/shard_map/ppermute | solution.py:444
  11.4 27.4 %collective-permute-start.2 = (bf16[24,192,128]{2,1,0:T(8,128)(2,1)}, bf16[24,192,128]{2,1,0:T(8,128)(2,1)S(1)}, u32[]{:S(2)}, u32[]{:S(2)}) collective-permute-start(bf16[24,192,128]{2,1,0:T(8,128)(2,1)} %get-tuple-element.87), channel_id=1, source_target_pairs={{0,1},{1,0},{2,3},{3,2},{4,5},{5,4},{6,7},{7,6},{8,9},{9,8},{10,11... | collective-permute-start | bytes 3538952 | tf_op jit(solution)/shard_map/ppermute | solution.py:444
  38.8 15.2 %copy-start.11 = (bf16[24,192,128]{2,1,0:T(8,128)(2,1)}, bf16[24,192,128]{2,1,0:T(8,128)(2,1)S(1)}, u32[]{:S(2)}) copy-start(bf16[24,192,128]{2,1,0:T(8,128)(2,1)S(1)} %collective-permute-done.2.gs) | copy-start | bytes 3538948
  38.8 15.2 %collective-permute-start.3 = (bf16[12,192,128]{2,1,0:T(8,128)(2,1)}, bf16[12,192,128]{2,1,0:T(8,128)(2,1)S(1)}, u32[]{:S(2)}, u32[]{:S(2)}) collective-permute-start(bf16[12,192,128]{2,1,0:T(8,128)(2,1)} %get-tuple-element.88), channel_id=1, source_target_pairs={{0,1},{1,0},{2,3},{3,2},{4,5},{5,4},{6,7},{7,6},{8,9},{9,8},{10,11... | collective-permute-start | bytes 1769480 | tf_op jit(solution)/shard_map/ppermute | solution.py:444
  39.3 14.7 %copy-start.15 = (bf16[12,192,128]{2,1,0:T(8,128)(2,1)S(1)}, bf16[12,192,128]{2,1,0:T(8,128)(2,1)}, u32[]{:S(2)}) copy-start(bf16[12,192,128]{2,1,0:T(8,128)(2,1)} %get-tuple-element.97) | copy-start | bytes 1769476
  54.0 13.5 %collective-permute-start.5 = (bf16[12,192,128]{2,1,0:T(8,128)(2,1)S(1)}, bf16[12,192,128]{2,1,0:T(8,128)(2,1)S(1)}, u32[]{:S(2)}, u32[]{:S(2)}) collective-permute-start(bf16[12,192,128]{2,1,0:T(8,128)(2,1)S(1)} %copy-done.15), channel_id=1, source_target_pairs={{0,1},{1,0},{2,3},{3,2},{4,5},{5,4},{6,7},{7,6},{8,9},{9,8},{10,11... | collective-permute-start | bytes 1769480 | tf_op jit(solution)/shard_map/ppermute | solution.py:444
  61.6 5.9 %collective-permute-start.4 = (bf16[384,768]{1,0:T(8,128)(2,1)}, bf16[384,768]{1,0:T(8,128)(2,1)S(1)}, u32[]{:S(2)}, u32[]{:S(2)}) collective-permute-start(bf16[384,768]{1,0:T(8,128)(2,1)} %bitcast.181), channel_id=1, source_target_pairs={{0,2},{2,0},{4,6},{6,4},{8,10},{10,8},{12,14},{14,12},{1,3},{3,1},... | collective-permute-start | bytes 1769480 | tf_op jit(solution)/shard_map/ppermute | solution.py:444
  67.6 9.0 %collective-permute-start.7 = (bf16[192,768]{1,0:T(8,128)(2,1)S(1)}, bf16[192,768]{1,0:T(8,128)(2,1)S(1)}, u32[]{:S(2)}, u32[]{:S(2)}) collective-permute-start(bf16[192,768]{1,0:T(8,128)(2,1)S(1)} %fusion.8), channel_id=1, source_target_pairs={{0,16},{16,0},{1,17},{17,1},{2,18},{18,2},{3,19},{19,3},{4,20},{20... | collective-permute-start | bytes 884744 | tf_op jit(solution)/shard_map/ppermute | solution.py:444
  68.2 8.4 %collective-permute-start.6 = (bf16[384,768]{1,0:T(8,128)(2,1)}, bf16[384,768]{1,0:T(8,128)(2,1)S(1)}, u32[]{:S(2)}, u32[]{:S(2)}) collective-permute-start(bf16[384,768]{1,0:T(8,128)(2,1)} %bitcast.180), channel_id=1, source_target_pairs={{0,2},{2,0},{4,6},{6,4},{8,10},{10,8},{12,14},{14,12},{1,3},{3,1},... | collective-permute-start | bytes 1769480 | tf_op jit(solution)/shard_map/ppermute | solution.py:444
  76.7 10.8 %collective-permute-start.12 = (bf16[48,768]{1,0:T(8,128)(2,1)S(1)}, bf16[48,768]{1,0:T(8,128)(2,1)S(1)}, u32[]{:S(2)}, u32[]{:S(2)}) collective-permute-start(bf16[48,768]{1,0:T(8,128)(2,1)S(1)} %get-tuple-element.180), channel_id=1, source_target_pairs={{0,12},{2,14},{4,0},{6,2},{8,4},{10,6},{12,8},{14,10},{1,13},{3,15... | collective-permute-start | bytes 221192 | tf_op jit(solution)/shard_map/ppermute | solution.py:451
  80.4 7.6 %collective-permute-start.11 = (bf16[48,768]{1,0:T(8,128)(2,1)S(1)}, bf16[48,768]{1,0:T(8,128)(2,1)S(1)}, u32[]{:S(2)}, u32[]{:S(2)}) collective-permute-start(bf16[48,768]{1,0:T(8,128)(2,1)S(1)} %get-tuple-element.181), channel_id=1, source_target_pairs={{0,8},{2,10},{4,12},{6,14},{8,0},{10,2},{12,4},{14,6},{1,9},{3,11}... | collective-permute-start | bytes 221192 | tf_op jit(solution)/shard_map/ppermute | solution.py:451
  80.4 7.6 %collective-permute-start.10 = (bf16[48,768]{1,0:T(8,128)(2,1)S(1)}, bf16[48,768]{1,0:T(8,128)(2,1)S(1)}, u32[]{:S(2)}, u32[]{:S(2)}) collective-permute-start(bf16[48,768]{1,0:T(8,128)(2,1)S(1)} %get-tuple-element.182), channel_id=1, source_target_pairs={{0,4},{2,6},{4,8},{6,10},{8,12},{10,14},{12,0},{14,2},{1,5},{3,7},... | collective-permute-start | bytes 221192 | tf_op jit(solution)/shard_map/ppermute | solution.py:451
  81.5 7.3 %collective-permute-start.9 = (bf16[192,768]{1,0:T(8,128)(2,1)S(1)}, bf16[192,768]{1,0:T(8,128)(2,1)S(1)}, u32[]{:S(2)}, u32[]{:S(2)}) collective-permute-start(bf16[192,768]{1,0:T(8,128)(2,1)S(1)} %fusion.9), channel_id=1, source_target_pairs={{0,16},{16,0},{1,17},{17,1},{2,18},{18,2},{3,19},{19,3},{4,20},{20... | collective-permute-start | bytes 884744 | tf_op jit(solution)/shard_map/ppermute | solution.py:444
  82.0 6.7 %collective-permute-start.8 = (bf16[384,768]{1,0:T(8,128)(2,1)S(1)}, bf16[384,768]{1,0:T(8,128)(2,1)S(1)}, u32[]{:S(2)}, u32[]{:S(2)}) collective-permute-start(bf16[384,768]{1,0:T(8,128)(2,1)S(1)} %bitcast.179), channel_id=1, source_target_pairs={{0,2},{2,0},{4,6},{6,4},{8,10},{10,8},{12,14},{14,12},{1,3},{3,1},... | collective-permute-start | bytes 1769480 | tf_op jit(solution)/shard_map/ppermute | solution.py:444
  87.5 9.3 %collective-permute-start.18 = (bf16[6,192,128]{2,1,0:T(8,128)(2,1)S(1)}, bf16[6,192,128]{2,1,0:T(8,128)(2,1)S(1)}, u32[]{:S(2)}, u32[]{:S(2)}) collective-permute-start(bf16[6,192,128]{2,1,0:T(8,128)(2,1)S(1)} %copy-done.25), channel_id=1, source_target_pairs={{0,1},{1,0},{2,3},{3,2},{4,5},{5,4},{6,7},{7,6},{8,9},{9,8},{10,11... | collective-permute-start | bytes 884744 | tf_op jit(solution)/shard_map/ppermute | solution.py:444
  88.7 10.7 %copy-start.21 = (bf16[6,192,128]{2,1,0:T(8,128)(2,1)S(1)}, bf16[6,192,128]{2,1,0:T(8,128)(2,1)}, u32[]{:S(2)}) copy-start(bf16[6,192,128]{2,1,0:T(8,128)(2,1)} %get-tuple-element.123) | copy-start | bytes 884740
  88.9 18.9 %copy-start.5 = (bf16[2,192,768]{2,1,0:T(8,128)(2,1)S(1)}, bf16[2,192,768]{2,1,0:T(8,128)(2,1)}, u32[]{:S(2)}) copy-start(bf16[2,192,768]{2,1,0:T(8,128)(2,1)} %get-tuple-element.119) | copy-start | bytes 1769476
  88.9 18.7 %collective-permute-start.14 = (bf16[192,768]{1,0:T(8,128)(2,1)S(1)}, bf16[192,768]{1,0:T(8,128)(2,1)S(1)}, u32[]{:S(2)}, u32[]{:S(2)}) collective-permute-start(bf16[192,768]{1,0:T(8,128)(2,1)S(1)} %fusion.10), channel_id=1, source_target_pairs={{0,16},{16,0},{1,17},{17,1},{2,18},{18,2},{3,19},{19,3},{4,20},{20... | collective-permute-start | bytes 884744 | tf_op jit(solution)/shard_map/ppermute | solution.py:444
  89.8 17.8 %collective-permute-start.13 = (bf16[384,768]{1,0:T(8,128)(2,1)S(1)}, bf16[384,768]{1,0:T(8,128)(2,1)S(1)}, u32[]{:S(2)}, u32[]{:S(2)}) collective-permute-start(bf16[384,768]{1,0:T(8,128)(2,1)S(1)} %bitcast.178), channel_id=1, source_target_pairs={{0,2},{2,0},{4,6},{6,4},{8,10},{10,8},{12,14},{14,12},{1,3},{3,1},... | collective-permute-start | bytes 1769480 | tf_op jit(solution)/shard_map/ppermute | solution.py:444
  89.9 9.5 %collective-permute-start.17 = (bf16[96,768]{1,0:T(8,128)(2,1)S(1)}, bf16[96,768]{1,0:T(8,128)(2,1)S(1)}, u32[]{:S(2)}, u32[]{:S(2)}) collective-permute-start(bf16[96,768]{1,0:T(8,128)(2,1)S(1)} %get-tuple-element.189), channel_id=1, source_target_pairs={{0,12},{2,14},{4,0},{6,2},{8,4},{10,6},{12,8},{14,10},{1,13},{3,15... | collective-permute-start | bytes 442376 | tf_op jit(solution)/shard_map/ppermute | solution.py:451
  92.8 14.8 %collective-permute-start.16 = (bf16[96,768]{1,0:T(8,128)(2,1)S(1)}, bf16[96,768]{1,0:T(8,128)(2,1)S(1)}, u32[]{:S(2)}, u32[]{:S(2)}) collective-permute-start(bf16[96,768]{1,0:T(8,128)(2,1)S(1)} %get-tuple-element.190), channel_id=1, source_target_pairs={{0,8},{2,10},{4,12},{6,14},{8,0},{10,2},{12,4},{14,6},{1,9},{3,11}... | collective-permute-start | bytes 442376 | tf_op jit(solution)/shard_map/ppermute | solution.py:451
  96.9 11.1 %copy-start.17 = (bf16[6,192,128]{2,1,0:T(8,128)(2,1)}, bf16[6,192,128]{2,1,0:T(8,128)(2,1)S(1)}, u32[]{:S(2)}) copy-start(bf16[6,192,128]{2,1,0:T(8,128)(2,1)S(1)} %collective-permute-done.18.refs_0_) | copy-start | bytes 884740
  96.9 10.7 %collective-permute-start.15 = (bf16[96,768]{1,0:T(8,128)(2,1)S(1)}, bf16[96,768]{1,0:T(8,128)(2,1)S(1)}, u32[]{:S(2)}, u32[]{:S(2)}) collective-permute-start(bf16[96,768]{1,0:T(8,128)(2,1)S(1)} %get-tuple-element.191), channel_id=1, source_target_pairs={{0,4},{2,6},{4,8},{6,10},{8,12},{10,14},{12,0},{14,2},{1,5},{3,7},... | collective-permute-start | bytes 442376 | tf_op jit(solution)/shard_map/ppermute | solution.py:451
  99.4 11.8 %collective-permute-start.24 = (bf16[6,192,128]{2,1,0:T(8,128)(2,1)S(1)}, bf16[6,192,128]{2,1,0:T(8,128)(2,1)S(1)}, u32[]{:S(2)}, u32[]{:S(2)}) collective-permute-start(bf16[6,192,128]{2,1,0:T(8,128)(2,1)S(1)} %copy-done.21), channel_id=1, source_target_pairs={{0,1},{1,0},{2,3},{3,2},{4,5},{5,4},{6,7},{7,6},{8,9},{9,8},{10,11... | collective-permute-start | bytes 884744 | tf_op jit(solution)/shard_map/ppermute | solution.py:444
  107.8 17.0 %collective-permute-start.19 = (bf16[192,768]{1,0:T(8,128)(2,1)S(1)}, bf16[192,768]{1,0:T(8,128)(2,1)S(1)}, u32[]{:S(2)}, u32[]{:S(2)}) collective-permute-start(bf16[192,768]{1,0:T(8,128)(2,1)S(1)} %bitcast.145), channel_id=1, source_target_pairs={{0,2},{2,0},{4,6},{6,4},{8,10},{10,8},{12,14},{14,12},{1,3},{3,1},... | collective-permute-start | bytes 884744 | tf_op jit(solution)/shard_map/ppermute | solution.py:444
  108.0 16.8 %collective-permute-start.20 = (bf16[384,768]{1,0:T(8,128)(2,1)S(1)}, bf16[384,768]{1,0:T(8,128)(2,1)S(1)}, u32[]{:S(2)}, u32[]{:S(2)}) collective-permute-start(bf16[384,768]{1,0:T(8,128)(2,1)S(1)} %pad_maximum_fusion), channel_id=1, source_target_pairs={{0,16},{16,0},{1,17},{17,1},{2,18},{18,2},{3,19},{19,3},{4,20},{20... | collective-permute-start | bytes 1769480 | tf_op jit(solution)/shard_map/ppermute | solution.py:444
  109.5 6.7 %collective-permute-start.23 = (bf16[96,768]{1,0:T(8,128)(2,1)S(1)}, bf16[96,768]{1,0:T(8,128)(2,1)S(1)}, u32[]{:S(2)}, u32[]{:S(2)}) collective-permute-start(bf16[96,768]{1,0:T(8,128)(2,1)S(1)} %get-tuple-element.186), channel_id=1, source_target_pairs={{0,12},{2,14},{4,0},{6,2},{8,4},{10,6},{12,8},{14,10},{1,13},{3,15... | collective-permute-start | bytes 442376 | tf_op jit(solution)/shard_map/ppermute | solution.py:451
  109.7 15.1 %collective-permute-start.22 = (bf16[96,768]{1,0:T(8,128)(2,1)S(1)}, bf16[96,768]{1,0:T(8,128)(2,1)S(1)}, u32[]{:S(2)}, u32[]{:S(2)}) collective-permute-start(bf16[96,768]{1,0:T(8,128)(2,1)S(1)} %get-tuple-element.187), channel_id=1, source_target_pairs={{0,8},{2,10},{4,12},{6,14},{8,0},{10,2},{12,4},{14,6},{1,9},{3,11}... | collective-permute-start | bytes 442376 | tf_op jit(solution)/shard_map/ppermute | solution.py:451
  111.2 14.0 %copy-start.20 = (bf16[6,192,128]{2,1,0:T(8,128)(2,1)}, bf16[6,192,128]{2,1,0:T(8,128)(2,1)S(1)}, u32[]{:S(2)}) copy-start(bf16[6,192,128]{2,1,0:T(8,128)(2,1)S(1)} %collective-permute-done.24.refs_1_) | copy-start | bytes 884740
  111.2 13.6 %collective-permute-start.21 = (bf16[96,768]{1,0:T(8,128)(2,1)S(1)}, bf16[96,768]{1,0:T(8,128)(2,1)S(1)}, u32[]{:S(2)}, u32[]{:S(2)}) collective-permute-start(bf16[96,768]{1,0:T(8,128)(2,1)S(1)} %get-tuple-element.188), channel_id=1, source_target_pairs={{0,4},{2,6},{4,8},{6,10},{8,12},{10,14},{12,0},{14,2},{1,5},{3,7},... | collective-permute-start | bytes 442376 | tf_op jit(solution)/shard_map/ppermute | solution.py:451
  116.2 11.8 %collective-permute-start.30 = (bf16[6,192,128]{2,1,0:T(8,128)(2,1)S(1)}, bf16[6,192,128]{2,1,0:T(8,128)(2,1)S(1)}, u32[]{:S(2)}, u32[]{:S(2)}) collective-permute-start(bf16[6,192,128]{2,1,0:T(8,128)(2,1)S(1)} %copy-done.19), channel_id=1, source_target_pairs={{0,1},{1,0},{2,3},{3,2},{4,5},{5,4},{6,7},{7,6},{8,9},{9,8},{10,11... | collective-permute-start | bytes 884744 | tf_op jit(solution)/shard_map/ppermute | solution.py:444
  125.1 16.7 %copy-start.1 = (bf16[4,48,768]{2,1,0:T(8,128)(2,1)}, bf16[4,48,768]{2,1,0:T(8,128)(2,1)S(1)}, u32[]{:S(2)}) copy-start(bf16[4,48,768]{2,1,0:T(8,128)(2,1)S(1)} %pad_maximum_fusion.5) | copy-start | bytes 884740
  125.5 16.2 %collective-permute-start.25 = (bf16[384,768]{1,0:T(8,128)(2,1)S(1)}, bf16[384,768]{1,0:T(8,128)(2,1)S(1)}, u32[]{:S(2)}, u32[]{:S(2)}) collective-permute-start(bf16[384,768]{1,0:T(8,128)(2,1)S(1)} %pad_maximum_fusion.1), channel_id=1, source_target_pairs={{0,2},{2,0},{4,6},{6,4},{8,10},{10,8},{12,14},{14,12},{1,3},{3,1},... | collective-permute-start | bytes 1769480 | tf_op jit(solution)/shard_map/ppermute | solution.py:444
  125.5 16.1 %collective-permute-start.26 = (bf16[192,768]{1,0:T(8,128)(2,1)S(1)}, bf16[192,768]{1,0:T(8,128)(2,1)S(1)}, u32[]{:S(2)}, u32[]{:S(2)}) collective-permute-start(bf16[192,768]{1,0:T(8,128)(2,1)S(1)} %bitcast.149), channel_id=1, source_target_pairs={{0,16},{16,0},{1,17},{17,1},{2,18},{18,2},{3,19},{19,3},{4,20},{20... | collective-permute-start | bytes 884744 | tf_op jit(solution)/shard_map/ppermute | solution.py:444
  126.2 6.4 %collective-permute-start.29 = (bf16[96,768]{1,0:T(8,128)(2,1)S(1)}, bf16[96,768]{1,0:T(8,128)(2,1)S(1)}, u32[]{:S(2)}, u32[]{:S(2)}) collective-permute-start(bf16[96,768]{1,0:T(8,128)(2,1)S(1)} %get-tuple-element.183), channel_id=1, source_target_pairs={{0,12},{2,14},{4,0},{6,2},{8,4},{10,6},{12,8},{14,10},{1,13},{3,15... | collective-permute-start | bytes 442376 | tf_op jit(solution)/shard_map/ppermute | solution.py:451
  126.2 15.4 %collective-permute-start.28 = (bf16[96,768]{1,0:T(8,128)(2,1)S(1)}, bf16[96,768]{1,0:T(8,128)(2,1)S(1)}, u32[]{:S(2)}, u32[]{:S(2)}) collective-permute-start(bf16[96,768]{1,0:T(8,128)(2,1)S(1)} %get-tuple-element.184), channel_id=1, source_target_pairs={{0,8},{2,10},{4,12},{6,14},{8,0},{10,2},{12,4},{14,6},{1,9},{3,11}... | collective-permute-start | bytes 442376 | tf_op jit(solution)/shard_map/ppermute | solution.py:451
  128.0 19.6 %copy-start.24 = (bf16[6,192,128]{2,1,0:T(8,128)(2,1)}, bf16[6,192,128]{2,1,0:T(8,128)(2,1)S(1)}, u32[]{:S(2)}) copy-start(bf16[6,192,128]{2,1,0:T(8,128)(2,1)S(1)} %collective-permute-done.30.refs_2_) | copy-start | bytes 884740
  128.0 13.6 %collective-permute-start.27 = (bf16[96,768]{1,0:T(8,128)(2,1)S(1)}, bf16[96,768]{1,0:T(8,128)(2,1)S(1)}, u32[]{:S(2)}, u32[]{:S(2)}) collective-permute-start(bf16[96,768]{1,0:T(8,128)(2,1)S(1)} %get-tuple-element.185), channel_id=1, source_target_pairs={{0,4},{2,6},{4,8},{6,10},{8,12},{10,14},{12,0},{14,2},{1,5},{3,7},... | collective-permute-start | bytes 442376 | tf_op jit(solution)/shard_map/ppermute | solution.py:451
  132.6 15.0 %collective-permute-start.36 = (bf16[6,192,128]{2,1,0:T(8,128)(2,1)S(1)}, bf16[6,192,128]{2,1,0:T(8,128)(2,1)S(1)}, u32[]{:S(2)}, u32[]{:S(2)}) collective-permute-start(bf16[6,192,128]{2,1,0:T(8,128)(2,1)S(1)} %copy-done.18), channel_id=1, source_target_pairs={{0,1},{1,0},{2,3},{3,2},{4,5},{5,4},{6,7},{7,6},{8,9},{9,8},{10,11... | collective-permute-start | bytes 884744 | tf_op jit(solution)/shard_map/ppermute | solution.py:444
  141.8 8.8 %collective-permute-start.35 = (bf16[48,768]{1,0:T(8,128)(2,1)S(1)}, bf16[48,768]{1,0:T(8,128)(2,1)S(1)}, u32[]{:S(2)}, u32[]{:S(2)}) collective-permute-start(bf16[48,768]{1,0:T(8,128)(2,1)S(1)} %fusion.14), channel_id=1, source_target_pairs={{0,12},{2,14},{4,0},{6,2},{8,4},{10,6},{12,8},{14,10},{1,13},{3,15... | collective-permute-start | bytes 221192 | tf_op jit(solution)/shard_map/ppermute | solution.py:451
  141.8 8.7 %collective-permute-start.34 = (bf16[48,768]{1,0:T(8,128)(2,1)S(1)}, bf16[48,768]{1,0:T(8,128)(2,1)S(1)}, u32[]{:S(2)}, u32[]{:S(2)}) collective-permute-start(bf16[48,768]{1,0:T(8,128)(2,1)S(1)} %fusion.14), channel_id=1, source_target_pairs={{0,8},{2,10},{4,12},{6,14},{8,0},{10,2},{12,4},{14,6},{1,9},{3,11}... | collective-permute-start | bytes 221192 | tf_op jit(solution)/shard_map/ppermute | solution.py:451
  143.1 7.5 %collective-permute-start.33 = (bf16[48,768]{1,0:T(8,128)(2,1)S(1)}, bf16[48,768]{1,0:T(8,128)(2,1)S(1)}, u32[]{:S(2)}, u32[]{:S(2)}) collective-permute-start(bf16[48,768]{1,0:T(8,128)(2,1)S(1)} %fusion.14), channel_id=1, source_target_pairs={{0,4},{2,6},{4,8},{6,10},{8,12},{10,14},{12,0},{14,2},{1,5},{3,7},... | collective-permute-start | bytes 221192 | tf_op jit(solution)/shard_map/ppermute | solution.py:451
  145.1 8.2 %collective-permute-start.32 = (bf16[192,768]{1,0:T(8,128)(2,1)S(1)}, bf16[192,768]{1,0:T(8,128)(2,1)S(1)}, u32[]{:S(2)}, u32[]{:S(2)}) collective-permute-start(bf16[192,768]{1,0:T(8,128)(2,1)S(1)} %bitcast.151), channel_id=1, source_target_pairs={{0,16},{16,0},{1,17},{17,1},{2,18},{18,2},{3,19},{19,3},{4,20},{20... | collective-permute-start | bytes 884744 | tf_op jit(solution)/shard_map/ppermute | solution.py:444
  147.7 5.6 %collective-permute-start.31 = (bf16[384,768]{1,0:T(8,128)(2,1)S(1)}, bf16[384,768]{1,0:T(8,128)(2,1)S(1)}, u32[]{:S(2)}, u32[]{:S(2)}) collective-permute-start(bf16[384,768]{1,0:T(8,128)(2,1)S(1)} %pad_maximum_fusion.2), channel_id=1, source_target_pairs={{0,2},{2,0},{4,6},{6,4},{8,10},{10,8},{12,14},{14,12},{1,3},{3,1},... | collective-permute-start | bytes 1769480 | tf_op jit(solution)/shard_map/ppermute | solution.py:444
  153.3 8.4 %collective-permute-start.38 = (bf16[192,768]{1,0:T(8,128)(2,1)S(1)}, bf16[192,768]{1,0:T(8,128)(2,1)S(1)}, u32[]{:S(2)}, u32[]{:S(2)}) collective-permute-start(bf16[192,768]{1,0:T(8,128)(2,1)S(1)} %bitcast.154), channel_id=1, source_target_pairs={{0,16},{16,0},{1,17},{17,1},{2,18},{18,2},{3,19},{19,3},{4,20},{20... | collective-permute-start | bytes 884744 | tf_op jit(solution)/shard_map/ppermute | solution.py:444
  155.8 6.0 %collective-permute-start.37 = (bf16[384,768]{1,0:T(8,128)(2,1)S(1)}, bf16[384,768]{1,0:T(8,128)(2,1)S(1)}, u32[]{:S(2)}, u32[]{:S(2)}) collective-permute-start(bf16[384,768]{1,0:T(8,128)(2,1)S(1)} %pad_maximum_fusion.3), channel_id=1, source_target_pairs={{0,2},{2,0},{4,6},{6,4},{8,10},{10,8},{12,14},{14,12},{1,3},{3,1},... | collective-permute-start | bytes 1769480 | tf_op jit(solution)/shard_map/ppermute | solution.py:444
  161.8 4.3 %collective-permute-start.39 = (bf16[192,768]{1,0:T(8,128)(2,1)S(1)}, bf16[192,768]{1,0:T(8,128)(2,1)S(1)}, u32[]{:S(2)}, u32[]{:S(2)}) collective-permute-start(bf16[192,768]{1,0:T(8,128)(2,1)S(1)} %collective-permute-done.38.other), channel_id=1, source_target_pairs={{0,2},{2,0},{4,6},{6,4},{8,10},{10,8},{12,14},{14,12},{1,3},{3,1},... | collective-permute-start | bytes 884744 | tf_op jit(solution)/shard_map/ppermute | solution.py:444
  (22 other events, 89.6 us)

commit v3 on v2

--- a/solution.py
+++ b/solution.py
@@ -85,7 +85,7 @@
         joined = jnp.concatenate([tall[q + 2][:, :128], tall[q + 3][:, :128]], axis=1)
         wide[TILE + 4 + q] = joined.astype(BF).reshape(steps + 6, SEG, 256)
 
-    part = 16
+    part = 32
     parts = steps // part
 
     def conv(n, carry):
@@ -507,7 +507,7 @@
         for _, values in self.live:
             for kind, value in values:
                 ways.setdefault(kind, []).append(value.reshape(-1, value.shape[-1]))
-        self.sent = {kind: transfer(kind, jnp.concatenate(flat)) for kind, flat in ways.items()}
+        self.sent = {kind: transfer(kind, jnp.concatenate(flat)) for kind, flat in sorted(ways.items(), reverse=True)}
 
     def arrive(self, *others):
         sent, others = lax.optimization_barrier((self.sent, others))

time: 170 us -> 170 us (level)
  waiting for transfers between devices: 41.2 us -> 43.2 us
  transfers between devices with their start and end apart: 40 -> 40, of which waited for: 11 -> 10; matrix products, arithmetic and copies ran while one was open for 3% -> 3% of each run, Pallas kernels for 44% -> 43%
where the time goes in v3:
time: 170 us
  Pallas kernels  76.2 us (45%)
  waiting for transfers between devices  43.2 us (25%)
  starting transfers between devices  39.7 us (23%)
  local copies, waits for them, and re-layouts  8.19 us (5%)
    ppermute x15, waiting for transfers between devices, shift(): return lax.ppermute(value, 'dp', perm)  29.5 us
    pallas_call x4, Pallas kernels, far_part(): pl.pallas_call(functools.partial(far_kernel, offset), grid_spec=pltpu.Pre...  22.3 us
    pallas_call x1, Pallas kernels, dense_part(): pl.pallas_call(dense_kernel, grid=(rows // TILE,), in_specs=[SM] * 3 + [V...  22.2 us
    ppermute x15, starting transfers between devices, shift(): return lax.ppermute(value, 'dp', perm)  21.9 us
    ppermute x25, starting transfers between devices, exchange(): return lax.ppermute(value, axis, [(i, i ^ flip) for i in range(count)])  17.8 us
    pallas_call x1, Pallas kernels, own_part(): pl.pallas_call(own_kernel, grid=(experts,), in_specs=[SM, SM, SM, VM, VM,...  14 us
    ppermute x25, waiting for transfers between devices, exchange(): return lax.ppermute(value, axis, [(i, i ^ flip) for i in range(count)])  13.7 us
    pallas_call x4, Pallas kernels, widen_group(): pl.pallas_call(functools.partial(widen_kernel, pieces), grid=(1,), in_spe...  11.3 us
  transfers between devices with their start and end apart: 40, of which 10 were waited for; matrix products, arithmetic and copies ran while one was open for 3% of the time, Pallas kernels for 43%

profile of v3, /device:TPU:0, one launch (start us, length us, event | category | flops | bytes accessed | tf_op | source)
XLA Modules:
  0.0 169.9 jit_solution(12150824619786485422)
XLA Ops:
  0.6 1.0 dynamic-slice_bitcast_fusion
  1.6 3.0 %collective-permute-start.1 = (bf16[3,192,256]{2,1,0:T(8,128)(2,1)S(1)}, bf16[3,192,256]{2,1,0:T(8,128)(2,1)S(1)}, u32[]{:S(2)}, u32[]{:S(2)}) collective-permute-start(bf16[3,192,256]{2,1,0:T(8,128)(2,1)S(1)} %dynamic-slice_bitcast_fusion), channel_id=1, source_target_pairs={{0,16},{16,0},{1,17},{17,1},{2,18},{18,2},{3,19},{19,3},{4,20},{20... | collective-permute-start | bytes 884744 | tf_op jit(solution)/shard_map/ppermute | solution.py:444
  4.6 0.8 copy.23
  6.6 3.3 %route_blocks.1 = (s32[48]{0:T(128)}, s32[16]{0:T(128)}, bf16[24,192,128]{2,1,0:T(8,128)(2,1)}) custom-call(s32[32]{0:T(128)} %reshape.104.labels, s32[5]{0:T(128)} %stack.83.place, bf16[16,192,256]{2,1,0:T(8,128)(2,1)} %bitcast.143), custom_call_target="tpu_custom_call" | custom-call | tf_op jit(solution)/shard_map/route_blocks/pallas_call | solution.py:244
  9.9 1.6 collective-permute-start
  12.0 0.7 copy-done.22
  12.7 22.2 %dense_block.1 = (bf16[16,192,256]{2,1,0:T(8,128)(2,1)}, bf16[12,192,128]{2,1,0:T(8,128)(2,1)}, bf16[12,192,128]{2,1,0:T(8,128)(2,1)}) custom-call(s32[5]{0:T(128)} %stack.83.place, s32[48]{0:T(128)} %get-tuple-element.85.table.tables, s32[16]{0:T(128)} %get-tuple-element.84.counts.tallies, bf16[16,192,256]{2,1,0:T(8,128)(2,1)} %bitcast.172, ...), custom_call_target="tpu_custom_call" | custom-call | flops 68719476736 | bytes 1048576 | tf_op jit(solution)/shard_map/dense_block/pallas_call | solution.py:189
  34.9 3.9 %collective-permute-done.2.gs = bf16[24,192,128]{2,1,0:T(8,128)(2,1)S(1)} collective-permute-done((bf16[24,192,128]{2,1,0:T(8,128)(2,1)}, bf16[24,192,128]{2,1,0:T(8,128)(2,1)S(1)}, u32[]{:S(2)}, u32[]{:S(2)}) %collective-permute-start.2) | collective-permute-done | bytes 1179680 | tf_op jit(solution)/shard_map/ppermute | solution.py:444
  39.3 14.0 %own_blocks.1 = (bf16[16,192,256]{2,1,0:T(8,128)(2,1)}, f32[8,192,768]{2,1,0:T(8,128)}, f32[8,192,768]{2,1,0:T(8,128)}) custom-call(s32[5]{0:T(128)} %stack.83.place, s32[48]{0:T(128)} %get-tuple-element.85.table.tables, s32[16]{0:T(128)} %get-tuple-element.84.counts.tallies, bf16[16,192,256]{2,1,0:T(8,128)(2,1)} %get-tuple-element.89.dense_in, ...), custom_call_target="tpu_custom_call" | custom-call | flops 68719476736 | bytes 1048576 | tf_op jit(solution)/shard_map/own_blocks/pallas_call | solution.py:316
  53.3 1.6 collective-permute-start.5
  55.4 5.3 %far_blocks.4 = (bf16[6,192,128]{2,1,0:T(8,128)(2,1)}, bf16[2,192,768]{2,1,0:T(8,128)(2,1)}, bf16[2,192,768]{2,1,0:T(8,128)(2,1)}) custom-call(s32[5]{0:T(128)} %stack.83.place, s32[16]{0:T(128)} %copy-done.29, bf16[12,192,128]{2,1,0:T(8,128)(2,1)} %copy-done.16, bf16[24,192,128]{2,1,0:T(8,128)(2,1)} %copy-done.11, bf16[8,192,768]{2,1,0:T(8,128)(2,1)} %w_in.9, ...), custom_call_target="tpu_custom_call" | custom-call | flops 68719476736 | bytes 1048576 | tf_op jit(solution)/shard_map/far_blocks/pallas_call | solution.py:364
  60.8 6.2 %far_blocks.5 = (bf16[6,192,128]{2,1,0:T(8,128)(2,1)}, bf16[2,192,768]{2,1,0:T(8,128)(2,1)}, bf16[2,192,768]{2,1,0:T(8,128)(2,1)}) custom-call(s32[5]{0:T(128)} %stack.83.place, s32[16]{0:T(128)} %copy-done.29, bf16[12,192,128]{2,1,0:T(8,128)(2,1)} %copy-done.16, bf16[24,192,128]{2,1,0:T(8,128)(2,1)} %copy-done.11, bf16[8,192,768]{2,1,0:T(8,128)(2,1)} %w_in.9, ...), custom_call_target="tpu_custom_call" | custom-call | flops 68719476736 | bytes 1048576 | tf_op jit(solution)/shard_map/far_blocks/pallas_call | solution.py:364
  67.8 5.3 %far_blocks.6 = (bf16[6,192,128]{2,1,0:T(8,128)(2,1)}, bf16[2,192,768]{2,1,0:T(8,128)(2,1)}, bf16[2,192,768]{2,1,0:T(8,128)(2,1)}) custom-call(s32[5]{0:T(128)} %stack.83.place, s32[16]{0:T(128)} %copy-done.29, bf16[12,192,128]{2,1,0:T(8,128)(2,1)} %copy-done.13, bf16[24,192,128]{2,1,0:T(8,128)(2,1)} %copy-done.11, bf16[8,192,768]{2,1,0:T(8,128)(2,1)} %w_in.9, ...), custom_call_target="tpu_custom_call" | custom-call | flops 68719476736 | bytes 1048576 | tf_op jit(solution)/shard_map/far_blocks/pallas_call | solution.py:364
  73.2 3.2 %collective-permute-done.7 = bf16[192,768]{1,0:T(8,128)(2,1)S(1)} collective-permute-done((bf16[192,768]{1,0:T(8,128)(2,1)S(1)}, bf16[192,768]{1,0:T(8,128)(2,1)S(1)}, u32[]{:S(2)}, u32[]{:S(2)}) %collective-permute-start.7) | collective-permute-done | bytes 294944 | tf_op jit(solution)/shard_map/ppermute | solution.py:444
  76.6 3.7 %collective-permute-start.12 = (bf16[48,768]{1,0:T(8,128)(2,1)S(1)}, bf16[48,768]{1,0:T(8,128)(2,1)S(1)}, u32[]{:S(2)}, u32[]{:S(2)}) collective-permute-start(bf16[48,768]{1,0:T(8,128)(2,1)S(1)} %get-tuple-element.180), channel_id=1, source_target_pairs={{0,12},{2,14},{4,0},{6,2},{8,4},{10,6},{12,8},{14,10},{1,13},{3,15... | collective-permute-start | bytes 221192 | tf_op jit(solution)/shard_map/ppermute | solution.py:451
  80.2 1.0 collective-permute-start.10
  81.9 5.5 %far_blocks.7 = (bf16[6,192,128]{2,1,0:T(8,128)(2,1)}, bf16[2,192,768]{2,1,0:T(8,128)(2,1)}, bf16[2,192,768]{2,1,0:T(8,128)(2,1)}) custom-call(s32[5]{0:T(128)} %stack.83.place, s32[16]{0:T(128)} %copy-done.29, bf16[12,192,128]{2,1,0:T(8,128)(2,1)} %copy-done.13, bf16[24,192,128]{2,1,0:T(8,128)(2,1)} %copy-done.11, bf16[8,192,768]{2,1,0:T(8,128)(2,1)} %w_in.9, ...), custom_call_target="tpu_custom_call" | custom-call | flops 68719476736 | bytes 1048576 | tf_op jit(solution)/shard_map/far_blocks/pallas_call | solution.py:364
  88.0 1.0 collective-permute-done.9
  90.0 3.1 %collective-permute-start.17 = (bf16[96,768]{1,0:T(8,128)(2,1)S(1)}, bf16[96,768]{1,0:T(8,128)(2,1)S(1)}, u32[]{:S(2)}, u32[]{:S(2)}) collective-permute-start(bf16[96,768]{1,0:T(8,128)(2,1)S(1)} %get-tuple-element.189), channel_id=1, source_target_pairs={{0,12},{2,14},{4,0},{6,2},{8,4},{10,6},{12,8},{14,10},{1,13},{3,15... | collective-permute-start | bytes 442376 | tf_op jit(solution)/shard_map/ppermute | solution.py:451
  93.1 0.9 collective-permute-start.16
  93.9 2.8 %collective-permute-done.18.refs_0_ = bf16[6,192,128]{2,1,0:T(8,128)(2,1)S(1)} collective-permute-done((bf16[6,192,128]{2,1,0:T(8,128)(2,1)S(1)}, bf16[6,192,128]{2,1,0:T(8,128)(2,1)S(1)}, u32[]{:S(2)}, u32[]{:S(2)}) %collective-permute-start.18) | collective-permute-done | bytes 294944 | tf_op jit(solution)/shard_map/ppermute | solution.py:444
  96.7 2.5 %collective-permute-start.15 = (bf16[96,768]{1,0:T(8,128)(2,1)S(1)}, bf16[96,768]{1,0:T(8,128)(2,1)S(1)}, u32[]{:S(2)}, u32[]{:S(2)}) collective-permute-start(bf16[96,768]{1,0:T(8,128)(2,1)S(1)} %get-tuple-element.191), channel_id=1, source_target_pairs={{0,4},{2,6},{4,8},{6,10},{8,12},{10,14},{12,0},{14,2},{1,5},{3,7},... | collective-permute-start | bytes 442376 | tf_op jit(solution)/shard_map/ppermute | solution.py:451
  99.7 7.9 %collective-permute-done.16 = bf16[96,768]{1,0:T(8,128)(2,1)S(1)} collective-permute-done((bf16[96,768]{1,0:T(8,128)(2,1)S(1)}, bf16[96,768]{1,0:T(8,128)(2,1)S(1)}, u32[]{:S(2)}, u32[]{:S(2)}) %collective-permute-start.16) | collective-permute-done | bytes 147488 | tf_op jit(solution)/shard_map/ppermute | solution.py:451
  108.0 1.5 collective-permute-start.20
  109.9 1.6 collective-permute-start.22
  111.4 2.0 %collective-permute-start.21 = (bf16[96,768]{1,0:T(8,128)(2,1)S(1)}, bf16[96,768]{1,0:T(8,128)(2,1)S(1)}, u32[]{:S(2)}, u32[]{:S(2)}) collective-permute-start(bf16[96,768]{1,0:T(8,128)(2,1)S(1)} %get-tuple-element.188), channel_id=1, source_target_pairs={{0,4},{2,6},{4,8},{6,10},{8,12},{10,14},{12,0},{14,2},{1,5},{3,7},... | collective-permute-start | bytes 442376 | tf_op jit(solution)/shard_map/ppermute | solution.py:451
  113.5 3.0 %collective-permute-done.23 = bf16[96,768]{1,0:T(8,128)(2,1)S(1)} collective-permute-done((bf16[96,768]{1,0:T(8,128)(2,1)S(1)}, bf16[96,768]{1,0:T(8,128)(2,1)S(1)}, u32[]{:S(2)}, u32[]{:S(2)}) %collective-permute-start.23) | collective-permute-done | bytes 147488 | tf_op jit(solution)/shard_map/ppermute | solution.py:451
  116.5 0.8 collective-permute-start.30
  117.3 7.7 %collective-permute-done.22 = bf16[96,768]{1,0:T(8,128)(2,1)S(1)} collective-permute-done((bf16[96,768]{1,0:T(8,128)(2,1)S(1)}, bf16[96,768]{1,0:T(8,128)(2,1)S(1)}, u32[]{:S(2)}, u32[]{:S(2)}) %collective-permute-start.22) | collective-permute-done | bytes 147488 | tf_op jit(solution)/shard_map/ppermute | solution.py:451
  126.5 1.5 collective-permute-start.28
  128.1 1.9 %collective-permute-start.27 = (bf16[96,768]{1,0:T(8,128)(2,1)S(1)}, bf16[96,768]{1,0:T(8,128)(2,1)S(1)}, u32[]{:S(2)}, u32[]{:S(2)}) collective-permute-start(bf16[96,768]{1,0:T(8,128)(2,1)S(1)} %get-tuple-element.185), channel_id=1, source_target_pairs={{0,4},{2,6},{4,8},{6,10},{8,12},{10,14},{12,0},{14,2},{1,5},{3,7},... | collective-permute-start | bytes 442376 | tf_op jit(solution)/shard_map/ppermute | solution.py:451
  130.0 3.3 %collective-permute-done.29 = bf16[96,768]{1,0:T(8,128)(2,1)S(1)} collective-permute-done((bf16[96,768]{1,0:T(8,128)(2,1)S(1)}, bf16[96,768]{1,0:T(8,128)(2,1)S(1)}, u32[]{:S(2)}, u32[]{:S(2)}) %collective-permute-start.29) | collective-permute-done | bytes 147488 | tf_op jit(solution)/shard_map/ppermute | solution.py:451
  133.3 0.8 collective-permute-start.36
  134.1 7.6 %collective-permute-done.28 = bf16[96,768]{1,0:T(8,128)(2,1)S(1)} collective-permute-done((bf16[96,768]{1,0:T(8,128)(2,1)S(1)}, bf16[96,768]{1,0:T(8,128)(2,1)S(1)}, u32[]{:S(2)}, u32[]{:S(2)}) %collective-permute-start.28) | collective-permute-done | bytes 147488 | tf_op jit(solution)/shard_map/ppermute | solution.py:451
  141.9 1.5 collective-permute-start.34
  143.4 1.9 %collective-permute-start.33 = (bf16[48,768]{1,0:T(8,128)(2,1)S(1)}, bf16[48,768]{1,0:T(8,128)(2,1)S(1)}, u32[]{:S(2)}, u32[]{:S(2)}) collective-permute-start(bf16[48,768]{1,0:T(8,128)(2,1)S(1)} %fusion.14), channel_id=1, source_target_pairs={{0,4},{2,6},{4,8},{6,10},{8,12},{10,14},{12,0},{14,2},{1,5},{3,7},... | collective-permute-start | bytes 221192 | tf_op jit(solution)/shard_map/ppermute | solution.py:451
  145.4 1.6 collective-permute-start.32
  147.0 0.9 fusion.26
  148.0 2.8 %widen_gradients.4 = (f32[8,192,768]{2,1,0:T(8,128)}, f32[8,192,768]{2,1,0:T(8,128)}) custom-call(s32[5]{0:T(128)} %stack.83.place, bf16[192,768]{1,0:T(8,128)(2,1)} %bitcast.147, bf16[192,768]{1,0:T(8,128)(2,1)} %copy-done.2, bf16[192,768]{1,0:T(8,128)(2,1)} %copy-done.23, bf16[192,768]{1,0:T(8,128)(2,1)} %get-tuple-element.170.other2), custom_call_target="tpu_custom_call" | custom-call | flops 68719476736 | bytes 1048576 | tf_op jit(solution)/shard_map/widen_gradients/pallas_call | solution.py:560
  150.9 2.7 %collective-permute-done.32.other = bf16[192,768]{1,0:T(8,128)(2,1)S(1)} collective-permute-done((bf16[192,768]{1,0:T(8,128)(2,1)S(1)}, bf16[192,768]{1,0:T(8,128)(2,1)S(1)}, u32[]{:S(2)}, u32[]{:S(2)}) %collective-permute-start.32) | collective-permute-done | bytes 294944 | tf_op jit(solution)/shard_map/ppermute | solution.py:444
  153.6 1.6 collective-permute-start.38
  155.2 0.8 fusion.25
  156.1 3.2 %combine_blocks.1 = bf16[16,192,256]{2,1,0:T(8,128)(2,1)} custom-call(s32[48]{0:T(128)} %get-tuple-element.85.table.tables, s32[16]{0:T(128)} %get-tuple-element.84.counts.tallies, s32[5]{0:T(128)} %stack.83.place, bf16[16,192,256]{2,1,0:T(8,128)(2,1)} %get-tuple-element.96.dense_in, ...), custom_call_target="tpu_custom_call", output_to_operand_aliasing={{}: (3, {})} | custom-call | flops 68719476736 | bytes 1048576 | tf_op jit(solution)/shard_map/combine_blocks/pallas_call | solution.py:425
  159.3 2.8 %widen_gradients.5 = (f32[8,192,768]{2,1,0:T(8,128)}, f32[8,192,768]{2,1,0:T(8,128)}) custom-call(s32[5]{0:T(128)} %stack.83.place, bf16[192,768]{1,0:T(8,128)(2,1)} %bitcast.150, bf16[192,768]{1,0:T(8,128)(2,1)} %copy-done.9, bf16[192,768]{1,0:T(8,128)(2,1)} %get-tuple-element.169.mine2, ...), custom_call_target="tpu_custom_call", output_to_operand_aliasing={{0}: (5, {}), {1}: (6, {})} | custom-call | flops 68719476736 | bytes 1048576 | tf_op jit(solution)/shard_map/widen_gradients/pallas_call | solution.py:560
  162.7 0.9 fusion.24
  163.6 2.8 %widen_gradients.6 = (f32[8,192,768]{2,1,0:T(8,128)}, f32[8,192,768]{2,1,0:T(8,128)}) custom-call(s32[5]{0:T(128)} %stack.83.place, bf16[192,768]{1,0:T(8,128)(2,1)} %bitcast.153, bf16[192,768]{1,0:T(8,128)(2,1)} %copy-done.10, bf16[192,768]{1,0:T(8,128)(2,1)} %get-tuple-element.167.mine2, ...), custom_call_target="tpu_custom_call", output_to_operand_aliasing={{0}: (5, {}), {1}: (6, {})} | custom-call | flops 68719476736 | bytes 1048576 | tf_op jit(solution)/shard_map/widen_gradients/pallas_call | solution.py:560
  166.4 0.7 copy-done.28
  167.1 2.8 %widen_gradients.7 = (f32[8,192,768]{2,1,0:T(8,128)}, f32[8,192,768]{2,1,0:T(8,128)}) custom-call(s32[5]{0:T(128)} %stack.83.place, bf16[192,768]{1,0:T(8,128)(2,1)} %bitcast.156, bf16[192,768]{1,0:T(8,128)(2,1)} %copy-done.27, bf16[192,768]{1,0:T(8,128)(2,1)} %get-tuple-element.166.mine2, ...), custom_call_target="tpu_custom_call", output_to_operand_aliasing={{0}: (5, {}), {1}: (6, {})} | custom-call | flops 68719476736 | bytes 1048576 | tf_op jit(solution)/shard_map/widen_gradients/pallas_call | solution.py:560
  (147 shorter events, 9.4 us)
Async XLA Ops:
  1.6 10.3 %collective-permute-start.1 = (bf16[3,192,256]{2,1,0:T(8,128)(2,1)S(1)}, bf16[3,192,256]{2,1,0:T(8,128)(2,1)S(1)}, u32[]{:S(2)}, u32[]{:S(2)}) collective-permute-start(bf16[3,192,256]{2,1,0:T(8,128)(2,1)S(1)} %dynamic-slice_bitcast_fusion), channel_id=1, source_target_pairs={{0,16},{16,0},{1,17},{17,1},{2,18},{18,2},{3,19},{19,3},{4,20},{20... | collective-permute-start | bytes 884744 | tf_op jit(solution)/shard_map/ppermute | solution.py:444
  9.9 45.0 %collective-permute-start = (s32[16]{0:T(128)}, s32[16]{0:T(128)S(1)}, u32[]{:S(2)}, u32[]{:S(2)}) collective-permute-start(s32[16]{0:T(128)} %get-tuple-element.84.counts.tallies), channel_id=1, source_target_pairs={{0,1},{1,0},{2,3},{3,2},{4,5},{5,4},{6,7},{7,6},{8,9},{9,8},{10,11... | collective-permute-start | bytes 200 | tf_op jit(solution)/shard_map/ppermute | solution.py:444
  11.4 27.4 %collective-permute-start.2 = (bf16[24,192,128]{2,1,0:T(8,128)(2,1)}, bf16[24,192,128]{2,1,0:T(8,128)(2,1)S(1)}, u32[]{:S(2)}, u32[]{:S(2)}) collective-permute-start(bf16[24,192,128]{2,1,0:T(8,128)(2,1)} %get-tuple-element.87), channel_id=1, source_target_pairs={{0,1},{1,0},{2,3},{3,2},{4,5},{5,4},{6,7},{7,6},{8,9},{9,8},{10,11... | collective-permute-start | bytes 3538952 | tf_op jit(solution)/shard_map/ppermute | solution.py:444
  38.8 14.5 %copy-start.11 = (bf16[24,192,128]{2,1,0:T(8,128)(2,1)}, bf16[24,192,128]{2,1,0:T(8,128)(2,1)S(1)}, u32[]{:S(2)}) copy-start(bf16[24,192,128]{2,1,0:T(8,128)(2,1)S(1)} %collective-permute-done.2.gs) | copy-start | bytes 3538948
  38.8 14.5 %collective-permute-start.3 = (bf16[12,192,128]{2,1,0:T(8,128)(2,1)}, bf16[12,192,128]{2,1,0:T(8,128)(2,1)S(1)}, u32[]{:S(2)}, u32[]{:S(2)}) collective-permute-start(bf16[12,192,128]{2,1,0:T(8,128)(2,1)} %get-tuple-element.88), channel_id=1, source_target_pairs={{0,1},{1,0},{2,3},{3,2},{4,5},{5,4},{6,7},{7,6},{8,9},{9,8},{10,11... | collective-permute-start | bytes 1769480 | tf_op jit(solution)/shard_map/ppermute | solution.py:444
  39.3 14.0 %copy-start.15 = (bf16[12,192,128]{2,1,0:T(8,128)(2,1)S(1)}, bf16[12,192,128]{2,1,0:T(8,128)(2,1)}, u32[]{:S(2)}) copy-start(bf16[12,192,128]{2,1,0:T(8,128)(2,1)} %get-tuple-element.97) | copy-start | bytes 1769476
  53.3 13.6 %collective-permute-start.5 = (bf16[12,192,128]{2,1,0:T(8,128)(2,1)S(1)}, bf16[12,192,128]{2,1,0:T(8,128)(2,1)S(1)}, u32[]{:S(2)}, u32[]{:S(2)}) collective-permute-start(bf16[12,192,128]{2,1,0:T(8,128)(2,1)S(1)} %copy-done.15), channel_id=1, source_target_pairs={{0,1},{1,0},{2,3},{3,2},{4,5},{5,4},{6,7},{7,6},{8,9},{9,8},{10,11... | collective-permute-start | bytes 1769480 | tf_op jit(solution)/shard_map/ppermute | solution.py:444
  60.7 6.3 %collective-permute-start.4 = (bf16[384,768]{1,0:T(8,128)(2,1)}, bf16[384,768]{1,0:T(8,128)(2,1)S(1)}, u32[]{:S(2)}, u32[]{:S(2)}) collective-permute-start(bf16[384,768]{1,0:T(8,128)(2,1)} %bitcast.181), channel_id=1, source_target_pairs={{0,2},{2,0},{4,6},{6,4},{8,10},{10,8},{12,14},{14,12},{1,3},{3,1},... | collective-permute-start | bytes 1769480 | tf_op jit(solution)/shard_map/ppermute | solution.py:444
  67.1 9.3 %collective-permute-start.7 = (bf16[192,768]{1,0:T(8,128)(2,1)S(1)}, bf16[192,768]{1,0:T(8,128)(2,1)S(1)}, u32[]{:S(2)}, u32[]{:S(2)}) collective-permute-start(bf16[192,768]{1,0:T(8,128)(2,1)S(1)} %fusion.8), channel_id=1, source_target_pairs={{0,16},{16,0},{1,17},{17,1},{2,18},{18,2},{3,19},{19,3},{4,20},{20... | collective-permute-start | bytes 884744 | tf_op jit(solution)/shard_map/ppermute | solution.py:444
  67.6 8.8 %collective-permute-start.6 = (bf16[384,768]{1,0:T(8,128)(2,1)}, bf16[384,768]{1,0:T(8,128)(2,1)S(1)}, u32[]{:S(2)}, u32[]{:S(2)}) collective-permute-start(bf16[384,768]{1,0:T(8,128)(2,1)} %bitcast.180), channel_id=1, source_target_pairs={{0,2},{2,0},{4,6},{6,4},{8,10},{10,8},{12,14},{14,12},{1,3},{3,1},... | collective-permute-start | bytes 1769480 | tf_op jit(solution)/shard_map/ppermute | solution.py:444
  76.6 10.8 %collective-permute-start.12 = (bf16[48,768]{1,0:T(8,128)(2,1)S(1)}, bf16[48,768]{1,0:T(8,128)(2,1)S(1)}, u32[]{:S(2)}, u32[]{:S(2)}) collective-permute-start(bf16[48,768]{1,0:T(8,128)(2,1)S(1)} %get-tuple-element.180), channel_id=1, source_target_pairs={{0,12},{2,14},{4,0},{6,2},{8,4},{10,6},{12,8},{14,10},{1,13},{3,15... | collective-permute-start | bytes 221192 | tf_op jit(solution)/shard_map/ppermute | solution.py:451
  80.2 7.8 %collective-permute-start.11 = (bf16[48,768]{1,0:T(8,128)(2,1)S(1)}, bf16[48,768]{1,0:T(8,128)(2,1)S(1)}, u32[]{:S(2)}, u32[]{:S(2)}) collective-permute-start(bf16[48,768]{1,0:T(8,128)(2,1)S(1)} %get-tuple-element.181), channel_id=1, source_target_pairs={{0,8},{2,10},{4,12},{6,14},{8,0},{10,2},{12,4},{14,6},{1,9},{3,11}... | collective-permute-start | bytes 221192 | tf_op jit(solution)/shard_map/ppermute | solution.py:451
  80.2 7.8 %collective-permute-start.10 = (bf16[48,768]{1,0:T(8,128)(2,1)S(1)}, bf16[48,768]{1,0:T(8,128)(2,1)S(1)}, u32[]{:S(2)}, u32[]{:S(2)}) collective-permute-start(bf16[48,768]{1,0:T(8,128)(2,1)S(1)} %get-tuple-element.182), channel_id=1, source_target_pairs={{0,4},{2,6},{4,8},{6,10},{8,12},{10,14},{12,0},{14,2},{1,5},{3,7},... | collective-permute-start | bytes 221192 | tf_op jit(solution)/shard_map/ppermute | solution.py:451
  81.3 7.7 %collective-permute-start.9 = (bf16[192,768]{1,0:T(8,128)(2,1)S(1)}, bf16[192,768]{1,0:T(8,128)(2,1)S(1)}, u32[]{:S(2)}, u32[]{:S(2)}) collective-permute-start(bf16[192,768]{1,0:T(8,128)(2,1)S(1)} %fusion.9), channel_id=1, source_target_pairs={{0,16},{16,0},{1,17},{17,1},{2,18},{18,2},{3,19},{19,3},{4,20},{20... | collective-permute-start | bytes 884744 | tf_op jit(solution)/shard_map/ppermute | solution.py:444
  81.9 7.1 %collective-permute-start.8 = (bf16[384,768]{1,0:T(8,128)(2,1)S(1)}, bf16[384,768]{1,0:T(8,128)(2,1)S(1)}, u32[]{:S(2)}, u32[]{:S(2)}) collective-permute-start(bf16[384,768]{1,0:T(8,128)(2,1)S(1)} %bitcast.179), channel_id=1, source_target_pairs={{0,2},{2,0},{4,6},{6,4},{8,10},{10,8},{12,14},{14,12},{1,3},{3,1},... | collective-permute-start | bytes 1769480 | tf_op jit(solution)/shard_map/ppermute | solution.py:444
  87.4 9.3 %collective-permute-start.18 = (bf16[6,192,128]{2,1,0:T(8,128)(2,1)S(1)}, bf16[6,192,128]{2,1,0:T(8,128)(2,1)S(1)}, u32[]{:S(2)}, u32[]{:S(2)}) collective-permute-start(bf16[6,192,128]{2,1,0:T(8,128)(2,1)S(1)} %copy-done.25), channel_id=1, source_target_pairs={{0,1},{1,0},{2,3},{3,2},{4,5},{5,4},{6,7},{7,6},{8,9},{9,8},{10,11... | collective-permute-start | bytes 884744 | tf_op jit(solution)/shard_map/ppermute | solution.py:444
  89.0 10.2 %copy-start.21 = (bf16[6,192,128]{2,1,0:T(8,128)(2,1)S(1)}, bf16[6,192,128]{2,1,0:T(8,128)(2,1)}, u32[]{:S(2)}) copy-start(bf16[6,192,128]{2,1,0:T(8,128)(2,1)} %get-tuple-element.123) | copy-start | bytes 884740
  89.2 18.7 %copy-start.5 = (bf16[2,192,768]{2,1,0:T(8,128)(2,1)S(1)}, bf16[2,192,768]{2,1,0:T(8,128)(2,1)}, u32[]{:S(2)}) copy-start(bf16[2,192,768]{2,1,0:T(8,128)(2,1)} %get-tuple-element.119) | copy-start | bytes 1769476
  89.2 18.5 %collective-permute-start.14 = (bf16[192,768]{1,0:T(8,128)(2,1)S(1)}, bf16[192,768]{1,0:T(8,128)(2,1)S(1)}, u32[]{:S(2)}, u32[]{:S(2)}) collective-permute-start(bf16[192,768]{1,0:T(8,128)(2,1)S(1)} %fusion.10), channel_id=1, source_target_pairs={{0,16},{16,0},{1,17},{17,1},{2,18},{18,2},{3,19},{19,3},{4,20},{20... | collective-permute-start | bytes 884744 | tf_op jit(solution)/shard_map/ppermute | solution.py:444
  89.8 17.8 %collective-permute-start.13 = (bf16[384,768]{1,0:T(8,128)(2,1)S(1)}, bf16[384,768]{1,0:T(8,128)(2,1)S(1)}, u32[]{:S(2)}, u32[]{:S(2)}) collective-permute-start(bf16[384,768]{1,0:T(8,128)(2,1)S(1)} %bitcast.178), channel_id=1, source_target_pairs={{0,2},{2,0},{4,6},{6,4},{8,10},{10,8},{12,14},{14,12},{1,3},{3,1},... | collective-permute-start | bytes 1769480 | tf_op jit(solution)/shard_map/ppermute | solution.py:444
  90.0 9.3 %collective-permute-start.17 = (bf16[96,768]{1,0:T(8,128)(2,1)S(1)}, bf16[96,768]{1,0:T(8,128)(2,1)S(1)}, u32[]{:S(2)}, u32[]{:S(2)}) collective-permute-start(bf16[96,768]{1,0:T(8,128)(2,1)S(1)} %get-tuple-element.189), channel_id=1, source_target_pairs={{0,12},{2,14},{4,0},{6,2},{8,4},{10,6},{12,8},{14,10},{1,13},{3,15... | collective-permute-start | bytes 442376 | tf_op jit(solution)/shard_map/ppermute | solution.py:451
  93.1 14.6 %collective-permute-start.16 = (bf16[96,768]{1,0:T(8,128)(2,1)S(1)}, bf16[96,768]{1,0:T(8,128)(2,1)S(1)}, u32[]{:S(2)}, u32[]{:S(2)}) collective-permute-start(bf16[96,768]{1,0:T(8,128)(2,1)S(1)} %get-tuple-element.190), channel_id=1, source_target_pairs={{0,8},{2,10},{4,12},{6,14},{8,0},{10,2},{12,4},{14,6},{1,9},{3,11}... | collective-permute-start | bytes 442376 | tf_op jit(solution)/shard_map/ppermute | solution.py:451
  96.7 11.3 %copy-start.17 = (bf16[6,192,128]{2,1,0:T(8,128)(2,1)}, bf16[6,192,128]{2,1,0:T(8,128)(2,1)S(1)}, u32[]{:S(2)}) copy-start(bf16[6,192,128]{2,1,0:T(8,128)(2,1)S(1)} %collective-permute-done.18.refs_0_) | copy-start | bytes 884740
  96.7 10.9 %collective-permute-start.15 = (bf16[96,768]{1,0:T(8,128)(2,1)S(1)}, bf16[96,768]{1,0:T(8,128)(2,1)S(1)}, u32[]{:S(2)}, u32[]{:S(2)}) collective-permute-start(bf16[96,768]{1,0:T(8,128)(2,1)S(1)} %get-tuple-element.191), channel_id=1, source_target_pairs={{0,4},{2,6},{4,8},{6,10},{8,12},{10,14},{12,0},{14,2},{1,5},{3,7},... | collective-permute-start | bytes 442376 | tf_op jit(solution)/shard_map/ppermute | solution.py:451
  99.2 12.2 %collective-permute-start.24 = (bf16[6,192,128]{2,1,0:T(8,128)(2,1)S(1)}, bf16[6,192,128]{2,1,0:T(8,128)(2,1)S(1)}, u32[]{:S(2)}, u32[]{:S(2)}) collective-permute-start(bf16[6,192,128]{2,1,0:T(8,128)(2,1)S(1)} %copy-done.21), channel_id=1, source_target_pairs={{0,1},{1,0},{2,3},{3,2},{4,5},{5,4},{6,7},{7,6},{8,9},{9,8},{10,11... | collective-permute-start | bytes 884744 | tf_op jit(solution)/shard_map/ppermute | solution.py:444
  107.8 17.2 %collective-permute-start.19 = (bf16[192,768]{1,0:T(8,128)(2,1)S(1)}, bf16[192,768]{1,0:T(8,128)(2,1)S(1)}, u32[]{:S(2)}, u32[]{:S(2)}) collective-permute-start(bf16[192,768]{1,0:T(8,128)(2,1)S(1)} %bitcast.145), channel_id=1, source_target_pairs={{0,2},{2,0},{4,6},{6,4},{8,10},{10,8},{12,14},{14,12},{1,3},{3,1},... | collective-permute-start | bytes 884744 | tf_op jit(solution)/shard_map/ppermute | solution.py:444
  108.0 17.0 %collective-permute-start.20 = (bf16[384,768]{1,0:T(8,128)(2,1)S(1)}, bf16[384,768]{1,0:T(8,128)(2,1)S(1)}, u32[]{:S(2)}, u32[]{:S(2)}) collective-permute-start(bf16[384,768]{1,0:T(8,128)(2,1)S(1)} %pad_maximum_fusion), channel_id=1, source_target_pairs={{0,16},{16,0},{1,17},{17,1},{2,18},{18,2},{3,19},{19,3},{4,20},{20... | collective-permute-start | bytes 1769480 | tf_op jit(solution)/shard_map/ppermute | solution.py:444
  109.8 6.7 %collective-permute-start.23 = (bf16[96,768]{1,0:T(8,128)(2,1)S(1)}, bf16[96,768]{1,0:T(8,128)(2,1)S(1)}, u32[]{:S(2)}, u32[]{:S(2)}) collective-permute-start(bf16[96,768]{1,0:T(8,128)(2,1)S(1)} %get-tuple-element.186), channel_id=1, source_target_pairs={{0,12},{2,14},{4,0},{6,2},{8,4},{10,6},{12,8},{14,10},{1,13},{3,15... | collective-permute-start | bytes 442376 | tf_op jit(solution)/shard_map/ppermute | solution.py:451
  109.9 15.2 %collective-permute-start.22 = (bf16[96,768]{1,0:T(8,128)(2,1)S(1)}, bf16[96,768]{1,0:T(8,128)(2,1)S(1)}, u32[]{:S(2)}, u32[]{:S(2)}) collective-permute-start(bf16[96,768]{1,0:T(8,128)(2,1)S(1)} %get-tuple-element.187), channel_id=1, source_target_pairs={{0,8},{2,10},{4,12},{6,14},{8,0},{10,2},{12,4},{14,6},{1,9},{3,11}... | collective-permute-start | bytes 442376 | tf_op jit(solution)/shard_map/ppermute | solution.py:451
  111.4 14.0 %copy-start.20 = (bf16[6,192,128]{2,1,0:T(8,128)(2,1)}, bf16[6,192,128]{2,1,0:T(8,128)(2,1)S(1)}, u32[]{:S(2)}) copy-start(bf16[6,192,128]{2,1,0:T(8,128)(2,1)S(1)} %collective-permute-done.24.refs_1_) | copy-start | bytes 884740
  111.4 13.6 %collective-permute-start.21 = (bf16[96,768]{1,0:T(8,128)(2,1)S(1)}, bf16[96,768]{1,0:T(8,128)(2,1)S(1)}, u32[]{:S(2)}, u32[]{:S(2)}) collective-permute-start(bf16[96,768]{1,0:T(8,128)(2,1)S(1)} %get-tuple-element.188), channel_id=1, source_target_pairs={{0,4},{2,6},{4,8},{6,10},{8,12},{10,14},{12,0},{14,2},{1,5},{3,7},... | collective-permute-start | bytes 442376 | tf_op jit(solution)/shard_map/ppermute | solution.py:451
  116.5 11.6 %collective-permute-start.30 = (bf16[6,192,128]{2,1,0:T(8,128)(2,1)S(1)}, bf16[6,192,128]{2,1,0:T(8,128)(2,1)S(1)}, u32[]{:S(2)}, u32[]{:S(2)}) collective-permute-start(bf16[6,192,128]{2,1,0:T(8,128)(2,1)S(1)} %copy-done.19), channel_id=1, source_target_pairs={{0,1},{1,0},{2,3},{3,2},{4,5},{5,4},{6,7},{7,6},{8,9},{9,8},{10,11... | collective-permute-start | bytes 884744 | tf_op jit(solution)/shard_map/ppermute | solution.py:444
  125.3 16.5 %copy-start.1 = (bf16[4,48,768]{2,1,0:T(8,128)(2,1)}, bf16[4,48,768]{2,1,0:T(8,128)(2,1)S(1)}, u32[]{:S(2)}) copy-start(bf16[4,48,768]{2,1,0:T(8,128)(2,1)S(1)} %pad_maximum_fusion.5) | copy-start | bytes 884740
  125.7 15.9 %collective-permute-start.25 = (bf16[384,768]{1,0:T(8,128)(2,1)S(1)}, bf16[384,768]{1,0:T(8,128)(2,1)S(1)}, u32[]{:S(2)}, u32[]{:S(2)}) collective-permute-start(bf16[384,768]{1,0:T(8,128)(2,1)S(1)} %pad_maximum_fusion.1), channel_id=1, source_target_pairs={{0,2},{2,0},{4,6},{6,4},{8,10},{10,8},{12,14},{14,12},{1,3},{3,1},... | collective-permute-start | bytes 1769480 | tf_op jit(solution)/shard_map/ppermute | solution.py:444
  125.8 15.9 %collective-permute-start.26 = (bf16[192,768]{1,0:T(8,128)(2,1)S(1)}, bf16[192,768]{1,0:T(8,128)(2,1)S(1)}, u32[]{:S(2)}, u32[]{:S(2)}) collective-permute-start(bf16[192,768]{1,0:T(8,128)(2,1)S(1)} %bitcast.149), channel_id=1, source_target_pairs={{0,16},{16,0},{1,17},{17,1},{2,18},{18,2},{3,19},{19,3},{4,20},{20... | collective-permute-start | bytes 884744 | tf_op jit(solution)/shard_map/ppermute | solution.py:444
  126.5 6.8 %collective-permute-start.29 = (bf16[96,768]{1,0:T(8,128)(2,1)S(1)}, bf16[96,768]{1,0:T(8,128)(2,1)S(1)}, u32[]{:S(2)}, u32[]{:S(2)}) collective-permute-start(bf16[96,768]{1,0:T(8,128)(2,1)S(1)} %get-tuple-element.183), channel_id=1, source_target_pairs={{0,12},{2,14},{4,0},{6,2},{8,4},{10,6},{12,8},{14,10},{1,13},{3,15... | collective-permute-start | bytes 442376 | tf_op jit(solution)/shard_map/ppermute | solution.py:451
  126.5 15.1 %collective-permute-start.28 = (bf16[96,768]{1,0:T(8,128)(2,1)S(1)}, bf16[96,768]{1,0:T(8,128)(2,1)S(1)}, u32[]{:S(2)}, u32[]{:S(2)}) collective-permute-start(bf16[96,768]{1,0:T(8,128)(2,1)S(1)} %get-tuple-element.184), channel_id=1, source_target_pairs={{0,8},{2,10},{4,12},{6,14},{8,0},{10,2},{12,4},{14,6},{1,9},{3,11}... | collective-permute-start | bytes 442376 | tf_op jit(solution)/shard_map/ppermute | solution.py:451
  128.1 19.9 %copy-start.24 = (bf16[6,192,128]{2,1,0:T(8,128)(2,1)}, bf16[6,192,128]{2,1,0:T(8,128)(2,1)S(1)}, u32[]{:S(2)}) copy-start(bf16[6,192,128]{2,1,0:T(8,128)(2,1)S(1)} %collective-permute-done.30.refs_2_) | copy-start | bytes 884740
  128.1 13.6 %collective-permute-start.27 = (bf16[96,768]{1,0:T(8,128)(2,1)S(1)}, bf16[96,768]{1,0:T(8,128)(2,1)S(1)}, u32[]{:S(2)}, u32[]{:S(2)}) collective-permute-start(bf16[96,768]{1,0:T(8,128)(2,1)S(1)} %get-tuple-element.185), channel_id=1, source_target_pairs={{0,4},{2,6},{4,8},{6,10},{8,12},{10,14},{12,0},{14,2},{1,5},{3,7},... | collective-permute-start | bytes 442376 | tf_op jit(solution)/shard_map/ppermute | solution.py:451
  133.3 14.7 %collective-permute-start.36 = (bf16[6,192,128]{2,1,0:T(8,128)(2,1)S(1)}, bf16[6,192,128]{2,1,0:T(8,128)(2,1)S(1)}, u32[]{:S(2)}, u32[]{:S(2)}) collective-permute-start(bf16[6,192,128]{2,1,0:T(8,128)(2,1)S(1)} %copy-done.18), channel_id=1, source_target_pairs={{0,1},{1,0},{2,3},{3,2},{4,5},{5,4},{6,7},{7,6},{8,9},{9,8},{10,11... | collective-permute-start | bytes 884744 | tf_op jit(solution)/shard_map/ppermute | solution.py:444
  141.8 9.0 %collective-permute-start.35 = (bf16[48,768]{1,0:T(8,128)(2,1)S(1)}, bf16[48,768]{1,0:T(8,128)(2,1)S(1)}, u32[]{:S(2)}, u32[]{:S(2)}) collective-permute-start(bf16[48,768]{1,0:T(8,128)(2,1)S(1)} %fusion.14), channel_id=1, source_target_pairs={{0,12},{2,14},{4,0},{6,2},{8,4},{10,6},{12,8},{14,10},{1,13},{3,15... | collective-permute-start | bytes 221192 | tf_op jit(solution)/shard_map/ppermute | solution.py:451
  141.9 9.0 %collective-permute-start.34 = (bf16[48,768]{1,0:T(8,128)(2,1)S(1)}, bf16[48,768]{1,0:T(8,128)(2,1)S(1)}, u32[]{:S(2)}, u32[]{:S(2)}) collective-permute-start(bf16[48,768]{1,0:T(8,128)(2,1)S(1)} %fusion.14), channel_id=1, source_target_pairs={{0,8},{2,10},{4,12},{6,14},{8,0},{10,2},{12,4},{14,6},{1,9},{3,11}... | collective-permute-start | bytes 221192 | tf_op jit(solution)/shard_map/ppermute | solution.py:451
  143.4 7.5 %collective-permute-start.33 = (bf16[48,768]{1,0:T(8,128)(2,1)S(1)}, bf16[48,768]{1,0:T(8,128)(2,1)S(1)}, u32[]{:S(2)}, u32[]{:S(2)}) collective-permute-start(bf16[48,768]{1,0:T(8,128)(2,1)S(1)} %fusion.14), channel_id=1, source_target_pairs={{0,4},{2,6},{4,8},{6,10},{8,12},{10,14},{12,0},{14,2},{1,5},{3,7},... | collective-permute-start | bytes 221192 | tf_op jit(solution)/shard_map/ppermute | solution.py:451
  145.4 8.2 %collective-permute-start.32 = (bf16[192,768]{1,0:T(8,128)(2,1)S(1)}, bf16[192,768]{1,0:T(8,128)(2,1)S(1)}, u32[]{:S(2)}, u32[]{:S(2)}) collective-permute-start(bf16[192,768]{1,0:T(8,128)(2,1)S(1)} %bitcast.151), channel_id=1, source_target_pairs={{0,16},{16,0},{1,17},{17,1},{2,18},{18,2},{3,19},{19,3},{4,20},{20... | collective-permute-start | bytes 884744 | tf_op jit(solution)/shard_map/ppermute | solution.py:444
  147.9 5.6 %collective-permute-start.31 = (bf16[384,768]{1,0:T(8,128)(2,1)S(1)}, bf16[384,768]{1,0:T(8,128)(2,1)S(1)}, u32[]{:S(2)}, u32[]{:S(2)}) collective-permute-start(bf16[384,768]{1,0:T(8,128)(2,1)S(1)} %pad_maximum_fusion.2), channel_id=1, source_target_pairs={{0,2},{2,0},{4,6},{6,4},{8,10},{10,8},{12,14},{14,12},{1,3},{3,1},... | collective-permute-start | bytes 1769480 | tf_op jit(solution)/shard_map/ppermute | solution.py:444
  153.6 8.5 %collective-permute-start.38 = (bf16[192,768]{1,0:T(8,128)(2,1)S(1)}, bf16[192,768]{1,0:T(8,128)(2,1)S(1)}, u32[]{:S(2)}, u32[]{:S(2)}) collective-permute-start(bf16[192,768]{1,0:T(8,128)(2,1)S(1)} %bitcast.154), channel_id=1, source_target_pairs={{0,16},{16,0},{1,17},{17,1},{2,18},{18,2},{3,19},{19,3},{4,20},{20... | collective-permute-start | bytes 884744 | tf_op jit(solution)/shard_map/ppermute | solution.py:444
  156.1 6.0 %collective-permute-start.37 = (bf16[384,768]{1,0:T(8,128)(2,1)S(1)}, bf16[384,768]{1,0:T(8,128)(2,1)S(1)}, u32[]{:S(2)}, u32[]{:S(2)}) collective-permute-start(bf16[384,768]{1,0:T(8,128)(2,1)S(1)} %pad_maximum_fusion.3), channel_id=1, source_target_pairs={{0,2},{2,0},{4,6},{6,4},{8,10},{10,8},{12,14},{14,12},{1,3},{3,1},... | collective-permute-start | bytes 1769480 | tf_op jit(solution)/shard_map/ppermute | solution.py:444
  162.1 4.3 %collective-permute-start.39 = (bf16[192,768]{1,0:T(8,128)(2,1)S(1)}, bf16[192,768]{1,0:T(8,128)(2,1)S(1)}, u32[]{:S(2)}, u32[]{:S(2)}) collective-permute-start(bf16[192,768]{1,0:T(8,128)(2,1)S(1)} %collective-permute-done.38.other), channel_id=1, source_target_pairs={{0,2},{2,0},{4,6},{6,4},{8,10},{10,8},{12,14},{14,12},{1,3},{3,1},... | collective-permute-start | bytes 884744 | tf_op jit(solution)/shard_map/ppermute | solution.py:444
  (22 other events, 93.2 us)
